TPU v7x, 32 devices: a whole 2x2x4 slice. The times are simulated.
32 devices in a mesh: row: 8 (over y, x, core), col: 4 (over z).
Axes of the slice: x: 2, y: 2, z: 4, core: 2. Of those that a mesh axis runs over, the one named last changes fastest.
Arguments:
- tokens: bfloat16 [128, 12288], P('col', 'row'), may hold values from -6 to 6
- cotangent: bfloat16 [128, 12288], P('col', 'row'), may hold values from -1.5 to 1.5
- w_in: bfloat16 [12288, 24576], P('row', 'col'), may hold values from -0.0546875 to 0.0546875
- w_out: bfloat16 [24576, 12288], P('col', 'row'), may hold values from -0.0390625 to 0.0390625
Outputs:
- layer_out: bfloat16 [128, 12288], P('col', 'row')
- grad_tokens: bfloat16 [128, 12288], P('col', 'row')
- grad_w_in: bfloat16 [12288, 24576], P('row', 'col')
- grad_w_out: bfloat16 [24576, 12288], P('col', 'row')
All inputs are finite; a program needn't handle non-finite values.
Results may differ from a plain program's by a relative error of at most 0.034.
Values may be sent and summed in bfloat16 or wider, within the bound.
No kernel may reach another device: no remote copies, remote signals or barrier semaphores. Data moves between devices by JAX's collectives and lax.ppermute only.
A program may use at most 128 MiB of HBM per device.

v0:
```python
import functools

import jax
import jax.numpy as jnp
from jax import lax
from jax.experimental import pallas as pl
from jax.experimental.pallas import tpu as pltpu
from jax.sharding import PartitionSpec as P

BF16 = jnp.bfloat16
F32 = jnp.float32
VMEM_LIMIT = 10 * 1024 * 1024
WRITES = 6
READ_CUTS, WRITE_CUTS = 4, 3
WEIGHTY = 6 * 10**9


def gelu_fn(value):
    return jax.nn.gelu(value, approximate=True)


def gelu_back(hidden, grad_act):
    unused, pullback = jax.vjp(gelu_fn, hidden)
    return pullback(grad_act)[0].astype(BF16)


def swap(value, axis, flip, count):
    return lax.ppermute(value, axis, [(i, i ^ flip) for i in range(count)])


def reverse(p, bits):
    return sum(((p >> j) & 1) << (bits - 1 - j) for j in range(bits))


def across(value, step, rows):
    bits = rows.bit_length() - 2
    flips = [2 << (bits - 1 - step if i & 1 else step) for i in range(rows)]
    return lax.ppermute(value, "row", [(i, i ^ flips[i]) for i in range(rows)])


def dot(left, right, left_dim, right_dim):
    return lax.dot_general(
        left, right, (((left_dim,), (right_dim,)), ((), ())), preferred_element_type=F32
    )


LAST = []


def call(kernel, arrays, outs, flops, moved, after=(), scratch=(), in_place=False):
    unread, count = [*LAST, *after], len(arrays)

    def body(*refs):
        kernel(*refs[:count], *refs[count + len(unread) :])

    specs = {
        "smem": pl.BlockSpec(memory_space=pltpu.SMEM),
        "vmem": pl.BlockSpec(memory_space=pltpu.VMEM),
        "hbm": pl.BlockSpec(memory_space=pl.ANY),
        "window": pl.BlockSpec(),
    }
    operands = []
    for space, value in arrays:
        if space != "smem":
            value = pltpu.with_memory_space_constraint(
                value, pltpu.HBM if space == "hbm" else pltpu.VMEM
            )
        operands.append(value)
    results = pl.pallas_call(
        body,
        in_specs=[specs[space] for space, value in arrays]
        + [pl.BlockSpec(memory_space=pl.ANY)] * len(unread),
        out_specs=[specs[space] for space, value in outs],
        scratch_shapes=list(scratch),
        input_output_aliases={count - 1: 0} if in_place else {},
        out_shape=[
            pltpu.VMEM(shape, dtype) if space == "vmem" else jax.ShapeDtypeStruct(shape, dtype)
            for space, (shape, dtype) in outs
        ],
        compiler_params=pltpu.CompilerParams(vmem_limit_bytes=VMEM_LIMIT),
        cost_estimate=pl.CostEstimate(flops=flops, bytes_accessed=moved, transcendentals=0),
    )(*operands, *unread)
    last = results[-1]
    if outs[-1][0] != "vmem":
        last = pltpu.with_memory_space_constraint(last, pltpu.HBM)
    LAST[:] = [last]
    return results


def in_vmem(values):
    return [("vmem", value) for value in values]


def join(pieces, out):
    at = 0
    for piece in pieces:
        out[at : at + piece.shape[0], :] = piece[...]
        at += piece.shape[0]


def place(pieces, order, out):
    size, order = pieces[0].shape[0], list(order)
    for piece in pieces:
        for at in range(0, piece.shape[0], size):
            to = order.pop(0) * size
            out[to : to + size, :] = piece[at : at + size, :]


def joined(pieces, after=()):
    rows = sum(piece.shape[0] for piece in pieces)

    def kernel(*refs):
        join(refs[: len(pieces)], refs[-1])

    return call(
        kernel, in_vmem(pieces), [("vmem", ((rows, pieces[0].shape[1]), BF16))], 0, 0, after
    )[0]


class Weight:
    def __init__(self, me, value, rows, by_rows):
        self.me, self.value, self.by_rows = me, value, by_rows
        self.bits = rows.bit_length() - 2
        self.block = value.shape[0 if by_rows else 1] // rows
        self.width = value.shape[1 if by_rows else 0]
        self.shape = (self.block, self.width) if by_rows else (self.width, self.block)
        self.held = {}

    def part(self, ref, me, key):
        p, odd = key
        chip = p + (me & 1) * (reverse(p, self.bits) - p)
        at = (me ^ (2 * chip + odd)) * self.block
        at = pl.ds(pl.multiple_of(at, 128), self.block)
        return ref.at[at, :] if self.by_rows else ref.at[:, at]


def cut(ref, i, cuts):
    size = ref.shape[0] // cuts
    return ref.at[i * size : (i + 1) * size, :]


class Coming:
    def __init__(self, blocks):
        self.blocks = blocks
        self.weights = list(dict.fromkeys(weight for weight, key in blocks))
        self.count = len(blocks) * READ_CUTS
        self.inputs = [("hbm", weight.value) for weight in self.weights]
        self.outs = [("vmem", (weight.shape, BF16)) for weight, key in blocks]
        self.scratch = [pltpu.SemaphoreType.DMA((self.count,))] if blocks else []

    def copies(self, sources, helds, arrived, me):
        return [
            pltpu.make_async_copy(
                cut(weight.part(sources[self.weights.index(weight)], me, key), i, READ_CUTS),
                cut(held, i, READ_CUTS),
                arrived.at[n * READ_CUTS + i],
            )
            for n, ((weight, key), held) in enumerate(zip(self.blocks, helds))
            for i in range(READ_CUTS)
        ]

    def arrive(self, helds):
        for (weight, key), held in zip(self.blocks, helds):
            weight.held[key] = held


def load(blocks, after=()):
    coming = Coming(blocks)
    n = len(coming.inputs)

    def kernel(me_ref, *refs):
        copies = coming.copies(refs[:n], refs[n:-1], refs[-1], me_ref[0])
        for copy in copies:
            copy.start()
        for copy in copies:
            copy.wait()

    me = blocks[0][0].me
    coming.arrive(
        call(kernel, [("smem", me), *coming.inputs], coming.outs, 0, 0, after, coming.scratch)
    )


def project(weight, shards, positions, blocks, after=()):
    pieces, order = shards
    coming = Coming(blocks)
    tokens, n = sum(piece.shape[0] for piece in pieces), len(positions)
    block, by_rows = weight.block, weight.by_rows
    keys = [(reverse(p, weight.bits), 1) for p in positions] + [(p, 0) for p in positions]

    def kernel(me_ref, *refs):
        piece_refs, refs = refs[: len(pieces)], refs[len(pieces) :]
        parts, refs = refs[: 2 * n], refs[2 * n :]
        sources, refs = refs[: len(coming.inputs)], refs[len(coming.inputs) :]
        keep, send, refs = refs[0], refs[1], refs[2:]
        left, copies = refs[len(blocks)], []
        if blocks:
            copies = coming.copies(sources, refs[: len(blocks)], refs[-1], me_ref[0])
        for copy in copies:
            copy.start()
        place(piece_refs, order, left)
        for i, part in enumerate(parts):
            out = dot(left[...], part[...], 1, 1 if by_rows else 0).astype(BF16)
            (send if i < n else keep)[i % n] = out
        for copy in copies:
            copy.wait()

    keep, send, *helds = call(
        kernel,
        [("smem", weight.me)]
        + in_vmem(pieces)
        + in_vmem([weight.held[key] for key in keys])
        + coming.inputs,
        [("vmem", ((n, tokens, block), BF16))] * 2 + coming.outs,
        0,
        0,
        after,
        [pltpu.VMEM((tokens, weight.width), BF16)] + coming.scratch,
    )
    coming.arrive(helds)
    return keep, send


def block_sum(weight, stacks, odds, cols, groups, after=()):
    width, by_rows, block = weight.width, weight.by_rows, weight.block
    chips = len(weight.held) // 2
    tokens = stacks[0].shape[0] // chips
    n, size = len(stacks), tokens // cols
    parts = [
        weight.held[(reverse(p, weight.bits) if odd else p, odd)]
        for odd in odds
        for p in range(chips)
    ]

    def kernel(*refs):
        stack_refs, part_refs, refs = refs[:n], refs[n : n + len(parts)], refs[n + len(parts) :]
        outs, total = refs[:-1], refs[-1]
        for i, part in enumerate(part_refs):
            p = i % chips
            value = stack_refs[i // chips][p * tokens : (p + 1) * tokens, :]
            term = dot(value, part[...], 1, 0 if by_rows else 1)
            total[...] = term if i == 0 else total[...] + term
        for group, out in zip(groups, outs):
            for i, q in enumerate(group):
                out[i * size : (i + 1) * size, :] = total[q * size : (q + 1) * size, :].astype(BF16)

    return call(
        kernel,
        in_vmem(stacks) + in_vmem(parts),
        [("vmem", ((len(group) * size, width), BF16)) for group in groups],
        2 * tokens * width * block * chips * n,
        2 * width * block * chips * n,
        after,
        [pltpu.VMEM((tokens, width), F32)],
    )


def weight_grad(weight, stacks, odds, shards, into=None):
    pieces, order = shards
    width, by_rows, block = weight.width, weight.by_rows, weight.block
    chips = len(weight.held) // 2
    tokens = stacks[0].shape[0] // chips
    halves = 2
    size = (block if by_rows else width) // halves
    keys = [
        (i, p, (reverse(p, weight.bits) if odd else p, odd))
        for p in range(chips)
        for i, odd in enumerate(odds)
    ]

    def kernel(me_ref, *refs):
        stack_refs, refs = refs[: len(stacks)], refs[len(stacks) :]
        piece_refs, refs = refs[: len(pieces)], refs[len(pieces) :]
        grad, other, turned, ready, sent = refs[-5:]
        place(piece_refs, order, other)
        if not by_rows:
            turned[...] = other[...].T
        me = me_ref[0]

        def writes(step):
            to = weight.part(grad, me, keys[step // halves][2])
            at = step % halves * size
            to = to.at[at : at + size, :]
            slot = step % WRITES
            return [
                pltpu.make_async_copy(
                    cut(ready.at[slot], i, WRITE_CUTS), cut(to, i, WRITE_CUTS), sent.at[slot, i]
                )
                for i in range(WRITE_CUTS)
            ]

        steps = len(keys) * halves
        for step in range(steps):
            if step >= WRITES:
                for write in writes(step - WRITES):
                    write.wait()
            i, p, key = keys[step // halves]
            stack, of = stack_refs[i], slice(p * tokens, (p + 1) * tokens)
            at = slice(step % halves * size, (step % halves + 1) * size)
            if by_rows:
                out = dot(stack[of, at], other[...], 0, 0)
            else:
                out = dot(turned[at, :], stack[of, :], 1, 0)
            ready[step % WRITES] = out.astype(BF16)
            for write in writes(step):
                write.start()
        for step in range(max(0, steps - WRITES), steps):
            for write in writes(step):
                write.wait()

    return call(
        kernel,
        [("smem", weight.me)]
        + in_vmem(stacks)
        + in_vmem(pieces)
        + ([("hbm", into)] if into is not None else []),
        [("hbm", (weight.value.shape, BF16))],
        2 * tokens * width * block * len(keys),
        2 * width * block * len(keys),
        (),
        [
            pltpu.VMEM((tokens, width), BF16),
            pltpu.VMEM((width, tokens), BF16),
            pltpu.VMEM((WRITES, size, width if by_rows else block), BF16),
            pltpu.SemaphoreType.DMA((WRITES, WRITE_CUTS)),
        ],
        into is not None,
    )[0]


def summed_half(keep, got, count, after=()):
    size = keep.shape[0] // count

    def kernel(keep_ref, got_ref, *outs):
        for i, out in enumerate(outs):
            at = slice(i * size, (i + 1) * size)
            total = keep_ref[at, :].astype(F32) + got_ref[at, :].astype(F32)
            out[...] = total.astype(out.dtype)

    shape = (size, keep.shape[1])
    outs = [("vmem", (shape, F32))] + [("vmem", (shape, BF16))] * (count - 1)
    return call(kernel, in_vmem([keep, got]), outs, 0, 0, after)


def added(terms, space="vmem"):
    def kernel(*refs):
        refs[-1][...] = sum(ref[...].astype(F32) for ref in refs[: len(terms)]).astype(BF16)

    return call(kernel, in_vmem(terms), [(space, (terms[0].shape, BF16))], 0, 0)[0]


def block_of(terms):
    def total(refs):
        return sum(ref[block].astype(F32) for ref, (array, block) in zip(refs, terms))

    return total


def sent_sum(terms):
    def kernel(*refs):
        refs[-1][0] = block_of(terms)(refs).astype(BF16)

    shape = (1, *terms[0][0].shape[1:])
    return call(kernel, in_vmem([array for array, block in terms]), [("vmem", (shape, BF16))], 0, 0)[0]


def activate(terms):
    def kernel(*refs):
        total = block_of(terms)(refs)
        refs[-2][...] = total
        refs[-1][...] = gelu_fn(total).astype(BF16)

    shape = terms[0][0].shape[1:]
    outs = [("vmem", (shape, F32)), ("vmem", (shape, BF16))]
    return call(kernel, in_vmem([array for array, block in terms]), outs, WEIGHTY, 0)


def activate_back(hidden, terms):
    def kernel(hidden_ref, *refs):
        refs[-1][...] = gelu_back(hidden_ref[...], block_of(terms)(refs))

    arrays = [hidden] + [array for array, block in terms]
    return call(kernel, in_vmem(arrays), [("vmem", (hidden.shape, BF16))], WEIGHTY, 0)[0]


def exchange_col(parts, cols):
    return [parts[0]] + [swap(parts[q], "col", q, cols) for q in range(cols - 1, 0, -1)]


def summed(parts):
    return sum(part.astype(F32) for part in parts).astype(BF16)


def blocked(rows, cols, tokens, cotangent, w_in, w_out):
    LAST.clear()
    me = lax.axis_index("row").astype(jnp.int32).reshape(1)
    w_in, w_out = Weight(me, w_in, rows, False), Weight(me, w_out, rows, True)
    first, second, own = [1, 3], [2], [0]

    def keys(positions):
        return [(reverse(p, 2), 1) for p in positions] + [(p, 0) for p in positions]

    def other_core(value):
        return swap(value, "row", 1, rows)

    def doubled(stack, step):
        return joined([stack, across(stack, step, rows)])

    wanted = [(w, key) for w in (w_in, w_out) for part in (first, second, own) for key in keys(part)]

    flips = [1 << bit for bit in range(cols.bit_length() - 1)][::-1]
    token_pieces, cot_pieces, order = [tokens], [cotangent], [0]
    for hop, flip in enumerate(flips):
        sent = joined(token_pieces) if hop else tokens
        token_pieces.append(swap(sent, "col", flip, cols))
        if hop:
            sent = joined(cot_pieces, (token_pieces[hop],))
            cot_pieces.append(swap(sent, "col", flips[hop - 1], cols))
        if hop < 2:
            load(wanted[5 * hop : 5 * hop + 5])
        order += [q ^ flip for q in order]
    sent = joined(cot_pieces, (token_pieces[-1],))
    cot_pieces.append(swap(sent, "col", flips[-1], cols))
    token_shards, cot_shards = (token_pieces, order), (cot_pieces, order)

    keep, sent = project(w_in, token_shards, first, [])
    got = other_core(sent)
    here, sent = project(w_in, token_shards, second + own, [])
    got_here, came = other_core(sent), across(added([keep, got]), 0, rows)
    load(wanted[5 * min(2, len(flips)) : 12])
    keep, sent = project(w_out, cot_shards, first, [])
    got = other_core(sent)
    sent = sent_sum([(here, 0), (got_here, 0), (came, 1)])
    terms = [(here, 1), (got_here, 1), (came, 0), (across(sent, 1, rows), 0)]

    came = across(added([keep, got]), 0, rows)
    load(wanted[12:14])
    keep, sent = project(w_out, cot_shards, second, [])
    got = other_core(sent)
    hidden, act = activate(terms)
    sent = sent_sum([(keep, 0), (got, 0), (came, 1)])
    last = across(sent, 1, rows)
    load(wanted[14:])
    stack = doubled(act, 0)
    keep, sent = project(w_out, cot_shards, own, [])
    got = other_core(sent)
    grad_hidden = activate_back(hidden, [(keep, 0), (came, 0), (last, 0), (got, 0)])
    stack = doubled(stack, 1)
    act = stack, other_core(stack)
    grad_w_out = weight_grad(w_out, act[:1], (0,), cot_shards)
    back_stack = doubled(grad_hidden, 0)

    even, odd = range(0, cols, 2), range(1, cols, 2)
    keep, send = block_sum(w_out, act, (0, 1), cols, (even, odd))
    got = swap(send, "col", 1, cols)
    grad_w_out = weight_grad(w_out, act[1:], (1,), cot_shards, grad_w_out)
    layer_out, *sums = summed_half(keep, got, len(even))
    layer_parts = [swap(part, "col", q, cols) for part, q in zip(sums, even[1:])]
    back_stack = doubled(back_stack, 1)
    grad_hidden = back_stack, other_core(back_stack)

    token_parts = block_sum(w_in, grad_hidden, (0, 1), cols, [[q] for q in range(cols)])
    layer_out = added([layer_out, *layer_parts], "window")
    grad_w_in = weight_grad(w_in, grad_hidden, (0, 1), token_shards)
    token_parts = exchange_col(token_parts, cols)
    return (layer_out, summed(token_parts), grad_w_in, grad_w_out)


def collective(tokens, cotangent, w_in, w_out):
    token_full = lax.all_gather(tokens, "col", axis=0, tiled=True)
    cot_full = lax.all_gather(cotangent, "col", axis=0, tiled=True)

    def over(value, axis):
        return lax.psum_scatter(value.astype(BF16), axis, scatter_dimension=0, tiled=True)

    hidden = over(dot(token_full, w_in, 1, 0), "row").astype(F32)
    grad_act = over(dot(cot_full, w_out, 1, 1), "row").astype(F32)
    act = lax.all_gather(gelu_fn(hidden).astype(BF16), "row", axis=0, tiled=True)
    grad_hidden = lax.all_gather(gelu_back(hidden, grad_act), "row", axis=0, tiled=True)
    layer_out = over(dot(act, w_out, 1, 0), "col")
    grad_tokens = over(dot(grad_hidden, w_in, 1, 1), "col")
    grad_w_in = dot(token_full, grad_hidden, 0, 0).astype(BF16)
    grad_w_out = dot(act, cot_full, 0, 0).astype(BF16)
    return (layer_out, grad_tokens, grad_w_in, grad_w_out)


def solution(mesh):
    rows, cols = mesh.shape["row"], mesh.shape["col"]

    def shards(tokens, cotangent, w_in, w_out):
        powers = rows & (rows - 1) == 0 and cols & (cols - 1) == 0
        if powers and rows == 8 and cols > 1 and w_in.shape[1] % (rows * 128) == 0:
            return blocked(rows, cols, tokens, cotangent, w_in, w_out)
        return collective(tokens, cotangent, w_in, w_out)

    return jax.shard_map(
        shards,
        mesh=mesh,
        in_specs=(P("col", "row"), P("col", "row"), P("row", "col"), P("col", "row")),
        out_specs=(P("col", "row"), P("col", "row"), P("row", "col"), P("col", "row")),
        check_vma=False,
    )
```

profile of v0, /device:TPU:0, one launch (start us, length us, event | category | flops | bytes accessed | tf_op | source)
XLA Modules:
  0.0 97.4 jit_solution(9390401102566404635)
XLA Ops:
  0.6 4.1 %collective-permute-start = (bf16[32,1536]{1,0:T(8,128)(2,1)}, bf16[32,1536]{1,0:T(8,128)(2,1)S(1)}, u32[]{:S(2)}, u32[]{:S(2)}) collective-permute-start(bf16[32,1536]{1,0:T(8,128)(2,1)} %refs_3_.1), channel_id=1, source_target_pairs={{0,2},{1,3},{2,0},{3,1},{4,6},{5,7},{6,4},{7,5},{8,10},{9,11},{10,... | collective-permute-start | bytes 294920 | tf_op jit(solution)/shard_map/ppermute | solution.py:28
  4.7 4.6 %shard_map.75 = (bf16[1536,768]{1,0:T(8,128)(2,1)S(1)}, bf16[1536,768]{1,0:T(8,128)(2,1)S(1)}, bf16[1536,768]{1,0:T(8,128)(2,1)S(1)}, bf16[1536,768]{1,0:T(8,128)(2,1)S(1)}, bf16[1536,768]{1,0:T(8,128)(2,1)S(1)}) custom-call(s32[1]{0:T(128)} %bitcast.refs_0_, bf16[1536,6144]{1,0:T(8,128)(2,1)} %refs_1_.11), custom_call_target="tpu_custom_call" | custom-call | tf_op jit(solution)/shard_map/pallas_call | solution.py:69
  11.1 3.0 %collective-permute-start.2 = (bf16[32,1536]{1,0:T(8,128)(2,1)S(1)}, bf16[32,1536]{1,0:T(8,128)(2,1)S(1)}, u32[]{:S(2)}, u32[]{:S(2)}) collective-permute-start(bf16[32,1536]{1,0:T(8,128)(2,1)S(1)} %shard_map.77.refs_3_), channel_id=1, source_target_pairs={{0,2},{1,3},{2,0},{3,1},{4,6},{5,7},{6,4},{7,5},{8,10},{9,11},{10,... | collective-permute-start | bytes 294920 | tf_op jit(solution)/shard_map/ppermute | solution.py:28
  14.1 4.6 %shard_map.78 = (bf16[1536,768]{1,0:T(8,128)(2,1)S(1)}, bf16[1536,768]{1,0:T(8,128)(2,1)S(1)}, bf16[1536,768]{1,0:T(8,128)(2,1)S(1)}, bf16[768,1536]{1,0:T(8,128)(2,1)S(1)}, bf16[768,1536]{1,0:T(8,128)(2,1)S(1)}) custom-call(s32[1]{0:T(128)} %bitcast.refs_0_, bf16[1536,6144]{1,0:T(8,128)(2,1)} %refs_1_.11, bf16[6144,1536]{1,0:T(8,128)(2,1)} %refs_1_.18, ...), custom_call_target="tpu_custom_call" | custom-call | tf_op jit(solution)/shard_map/pallas_call | solution.py:69
  20.3 2.5 %collective-permute-start.6 = (bf16[64,1536]{1,0:T(8,128)(2,1)S(1)}, bf16[64,1536]{1,0:T(8,128)(2,1)S(1)}, u32[]{:S(2)}, u32[]{:S(2)}) collective-permute-start(bf16[64,1536]{1,0:T(8,128)(2,1)S(1)} %shard_map.79.refs_8_), channel_id=1, source_target_pairs={{0,1},{1,0},{2,3},{3,2},{4,5},{5,4},{6,7},{7,6},{8,9},{9,8},{10,11... | collective-permute-start | bytes 589832 | tf_op jit(solution)/shard_map/ppermute | solution.py:28
  26.1 2.4 %shard_map.83 = (bf16[768,1536]{1,0:T(8,128)(2,1)S(1)}, bf16[768,1536]{1,0:T(8,128)(2,1)S(1)}) custom-call(s32[1]{0:T(128)} %bitcast.refs_0_, bf16[6144,1536]{1,0:T(8,128)(2,1)} %refs_1_.18, bf16[2,128,768]{2,1,0:T(8,128)(2,1)S(1)} %shard_map.82.refs_2_), custom_call_target="tpu_custom_call" | custom-call | tf_op jit(solution)/shard_map/pallas_call | solution.py:69
  28.5 3.1 %shard_map.84 = (bf16[2,128,768]{2,1,0:T(8,128)(2,1)S(1)}, bf16[2,128,768]{2,1,0:T(8,128)(2,1)S(1)}) custom-call(s32[1]{0:T(128)} %bitcast.refs_0_, bf16[32,1536]{1,0:T(8,128)(2,1)S(1)} %copy-done, bf16[32,1536]{1,0:T(8,128)(2,1)S(1)} %collective-permute-done.2.refs_1_.refs_2_.refs_3_, bf16[64,1536]{1,0:T(8,128)(2,1)S(1)} %collective-permute-done.6.refs_3_.refs_4_, ...), custom_call_target="tpu_custom_call" | custom-call | tf_op jit(solution)/shard_map/pallas_call | solution.py:69
  35.7 2.4 %shard_map.87 = (bf16[768,1536]{1,0:T(8,128)(2,1)S(1)}, bf16[768,1536]{1,0:T(8,128)(2,1)S(1)}) custom-call(s32[1]{0:T(128)} %bitcast.refs_0_, bf16[6144,1536]{1,0:T(8,128)(2,1)} %refs_1_.18, bf16[2,128,768]{2,1,0:T(8,128)(2,1)S(1)} %shard_map.86.refs_2_), custom_call_target="tpu_custom_call" | custom-call | tf_op jit(solution)/shard_map/pallas_call | solution.py:69
  38.1 1.6 %shard_map.88 = (bf16[1,128,768]{2,1,0:T(8,128)(2,1)S(1)}, bf16[1,128,768]{2,1,0:T(8,128)(2,1)S(1)}) custom-call(s32[1]{0:T(128)} %bitcast.refs_0_, bf16[32,1536]{1,0:T(8,128)(2,1)S(1)} %copy-done, bf16[32,1536]{1,0:T(8,128)(2,1)S(1)} %collective-permute-done.2.refs_1_.refs_2_.refs_3_, bf16[64,1536]{1,0:T(8,128)(2,1)S(1)} %collective-permute-done.6.refs_3_.refs_4_, ...), custom_call_target="tpu_custom_call" | custom-call | tf_op jit(solution)/shard_map/pallas_call | solution.py:69
  42.1 1.6 %collective-permute-start.13 = (bf16[1,128,768]{2,1,0:T(8,128)(2,1)S(1)}, bf16[1,128,768]{2,1,0:T(8,128)(2,1)S(1)}, u32[]{:S(2)}, u32[]{:S(2)}) collective-permute-start(bf16[1,128,768]{2,1,0:T(8,128)(2,1)S(1)} %shard_map.90.refs_2_), channel_id=1, source_target_pairs={{0,16},{4,12},{8,24},{12,4},{16,0},{20,28},{24,8},{28,20},{1,17},{... | collective-permute-start | bytes 589832 | tf_op jit(solution)/shard_map/ppermute | solution.py:38
  43.7 2.4 %shard_map.91 = (bf16[768,1536]{1,0:T(8,128)(2,1)S(1)}, bf16[768,1536]{1,0:T(8,128)(2,1)S(1)}) custom-call(s32[1]{0:T(128)} %bitcast.refs_0_, bf16[6144,1536]{1,0:T(8,128)(2,1)} %refs_1_.18, bf16[1,128,768]{2,1,0:T(8,128)(2,1)S(1)} %shard_map.90.refs_2_), custom_call_target="tpu_custom_call" | custom-call | tf_op jit(solution)/shard_map/pallas_call | solution.py:69
  47.1 1.6 %shard_map.93 = (bf16[1,128,768]{2,1,0:T(8,128)(2,1)S(1)}, bf16[1,128,768]{2,1,0:T(8,128)(2,1)S(1)}) custom-call(s32[1]{0:T(128)} %bitcast.refs_0_, bf16[32,1536]{1,0:T(8,128)(2,1)S(1)} %copy-done, bf16[32,1536]{1,0:T(8,128)(2,1)S(1)} %collective-permute-done.2.refs_1_.refs_2_.refs_3_, bf16[64,1536]{1,0:T(8,128)(2,1)S(1)} %collective-permute-done.6.refs_3_.refs_4_, ...), custom_call_target="tpu_custom_call" | custom-call | tf_op jit(solution)/shard_map/pallas_call | solution.py:69
  50.8 5.9 %collective-permute-done.12.refs_1_ = bf16[256,768]{1,0:T(8,128)(2,1)S(1)} collective-permute-done((bf16[256,768]{1,0:T(8,128)(2,1)S(1)}, bf16[256,768]{1,0:T(8,128)(2,1)S(1)}, u32[]{:S(2)}, u32[]{:S(2)}) %collective-permute-start.12) | collective-permute-done | bytes 393248 | tf_op jit(solution)/shard_map/ppermute | solution.py:38
  56.8 1.6 %collective-permute-start.16 = (bf16[128,768]{1,0:T(8,128)(2,1)S(1)}, bf16[128,768]{1,0:T(8,128)(2,1)S(1)}, u32[]{:S(2)}, u32[]{:S(2)}) collective-permute-start(bf16[128,768]{1,0:T(8,128)(2,1)S(1)} %shard_map.94.refs_2_.refs_0_), channel_id=1, source_target_pairs={{0,8},{4,20},{8,0},{12,28},{16,24},{20,4},{24,16},{28,12},{1,9},{5... | collective-permute-start | bytes 589832 | tf_op jit(solution)/shard_map/ppermute | solution.py:38
  58.4 4.2 %shard_map.96.refs_2_.refs_5_ = bf16[6144,1536]{1,0:T(8,128)(2,1)} custom-call(s32[1]{0:T(128)} %bitcast.refs_0_, bf16[512,768]{1,0:T(8,128)(2,1)S(1)} %shard_map.95.refs_1_.refs_5_.refs_0_, bf16[32,1536]{1,0:T(8,128)(2,1)S(1)} %copy-done, bf16[32,1536]{1,0:T(8,128)(2,1)S(1)} %collective-permute-done.2.refs_1_.refs_2_.refs_3_, ...), custom_call_target="tpu_custom_call" | custom-call | flops 1207959552 | bytes 9437184 | tf_op jit(solution)/shard_map/pallas_call | solution.py:69
  62.7 1.9 %collective-permute-start.19 = (bf16[256,768]{1,0:T(8,128)(2,1)S(1)}, bf16[256,768]{1,0:T(8,128)(2,1)S(1)}, u32[]{:S(2)}, u32[]{:S(2)}) collective-permute-start(bf16[256,768]{1,0:T(8,128)(2,1)S(1)} %shard_map.97.refs_10_.refs_0_), channel_id=1, source_target_pairs={{0,16},{4,12},{8,24},{12,4},{16,0},{20,28},{24,8},{28,20},{1,17},{... | collective-permute-start | bytes 1179656 | tf_op jit(solution)/shard_map/ppermute | solution.py:38
  64.6 2.8 %shard_map.98 = (bf16[64,1536]{1,0:T(8,128)(2,1)S(1)}, bf16[64,1536]{1,0:T(8,128)(2,1)S(1)}) custom-call(bf16[512,768]{1,0:T(8,128)(2,1)S(1)} %shard_map.95.refs_1_.refs_5_.refs_0_, bf16[512,768]{1,0:T(8,128)(2,1)S(1)} %collective-permute-done.15.refs_1_, bf16[768,1536]{1,0:T(8,128)(2,1)S(1)} %get-tuple-element.63.refs_2_.refs_5_, ...), custom_call_target="tpu_custom_call" | custom-call | flops 2415919104 | bytes 18874368 | tf_op jit(solution)/shard_map/pallas_call | solution.py:69
  67.5 4.2 %shard_map.99.refs_2_ = bf16[6144,1536]{1,0:T(8,128)(2,1)} custom-call(s32[1]{0:T(128)} %bitcast.refs_0_, bf16[512,768]{1,0:T(8,128)(2,1)S(1)} %collective-permute-done.15.refs_1_, bf16[32,1536]{1,0:T(8,128)(2,1)S(1)} %copy-done, bf16[32,1536]{1,0:T(8,128)(2,1)S(1)} %collective-permute-done.2.refs_1_.refs_2_.refs_3_, ...), custom_call_target="tpu_custom_call", output_to_operand_aliasing={{}: (5, {})} | custom-call | flops 1207959552 | bytes 9437184 | tf_op jit(solution)/shard_map/pallas_call | solution.py:69
  71.8 2.4 %collective-permute-done.17.refs_1_ = bf16[64,1536]{1,0:T(8,128)(2,1)S(1)} collective-permute-done((bf16[64,1536]{1,0:T(8,128)(2,1)S(1)}, bf16[64,1536]{1,0:T(8,128)(2,1)S(1)}, u32[]{:S(2)}, u32[]{:S(2)}) %collective-permute-start.17) | collective-permute-done | bytes 196640 | tf_op jit(solution)/shard_map/ppermute | solution.py:28
  74.4 1.8 %collective-permute-start.18 = (bf16[32,1536]{1,0:T(8,128)(2,1)S(1)}, bf16[32,1536]{1,0:T(8,128)(2,1)S(1)}, u32[]{:S(2)}, u32[]{:S(2)}) collective-permute-start(bf16[32,1536]{1,0:T(8,128)(2,1)S(1)} %get-tuple-element.71.refs_2_), channel_id=1, source_target_pairs={{0,2},{1,3},{2,0},{3,1},{4,6},{5,7},{6,4},{7,5},{8,10},{9,11},{10,... | collective-permute-start | bytes 294920 | tf_op jit(solution)/shard_map/ppermute | solution.py:28
  76.6 6.0 %shard_map.102 = (bf16[32,1536]{1,0:T(8,128)(2,1)S(1)}, bf16[32,1536]{1,0:T(8,128)(2,1)S(1)}, bf16[32,1536]{1,0:T(8,128)(2,1)S(1)}, bf16[32,1536]{1,0:T(8,128)(2,1)S(1)}) custom-call(bf16[512,768]{1,0:T(8,128)(2,1)S(1)} %shard_map.101.refs_0_.refs_10_.refs_1_, bf16[512,768]{1,0:T(8,128)(2,1)S(1)} %collective-permute-done.20.refs_1_.refs_2_, ...), custom_call_target="tpu_custom_call" | custom-call | flops 2415919104 | bytes 18874368 | tf_op jit(solution)/shard_map/pallas_call | solution.py:69
  82.7 1.8 %collective-permute-start.22 = (bf16[32,1536]{1,0:T(8,128)(2,1)S(1)}, bf16[32,1536]{1,0:T(8,128)(2,1)S(1)}, u32[]{:S(2)}, u32[]{:S(2)}) collective-permute-start(bf16[32,1536]{1,0:T(8,128)(2,1)S(1)} %get-tuple-element.74), channel_id=1, source_target_pairs={{0,2},{1,3},{2,0},{3,1},{4,6},{5,7},{6,4},{7,5},{8,10},{9,11},{10,... | collective-permute-start | bytes 294920 | tf_op jit(solution)/shard_map/ppermute | solution.py:28
  84.8 2.3 %collective-permute-start.21 = (bf16[32,1536]{1,0:T(8,128)(2,1)S(1)}, bf16[32,1536]{1,0:T(8,128)(2,1)S(1)}, u32[]{:S(2)}, u32[]{:S(2)}) collective-permute-start(bf16[32,1536]{1,0:T(8,128)(2,1)S(1)} %get-tuple-element.72.refs_2_), channel_id=1, source_target_pairs={{0,3},{1,2},{2,1},{3,0},{4,7},{5,6},{6,5},{7,4},{8,11},{9,10},{10,... | collective-permute-start | bytes 294920 | tf_op jit(solution)/shard_map/ppermute | solution.py:28
  87.8 8.8 %shard_map.104 = bf16[1536,6144]{1,0:T(8,128)(2,1)} custom-call(s32[1]{0:T(128)} %bitcast.refs_0_, bf16[512,768]{1,0:T(8,128)(2,1)S(1)} %shard_map.101.refs_0_.refs_10_.refs_1_, bf16[512,768]{1,0:T(8,128)(2,1)S(1)} %collective-permute-done.20.refs_1_.refs_2_, bf16[32,1536]{1,0:T(8,128)(2,1)S(1)} %copy-done.1, ...), custom_call_target="tpu_custom_call" | custom-call | flops 2415919104 | bytes 18874368 | tf_op jit(solution)/shard_map/pallas_call | solution.py:69
  (59 shorter events, 18.3 us)
Async XLA Ops:
  0.6 9.2 %collective-permute-start = (bf16[32,1536]{1,0:T(8,128)(2,1)}, bf16[32,1536]{1,0:T(8,128)(2,1)S(1)}, u32[]{:S(2)}, u32[]{:S(2)}) collective-permute-start(bf16[32,1536]{1,0:T(8,128)(2,1)} %refs_3_.1), channel_id=1, source_target_pairs={{0,2},{1,3},{2,0},{3,1},{4,6},{5,7},{6,4},{7,5},{8,10},{9,11},{10,... | collective-permute-start | bytes 294920 | tf_op jit(solution)/shard_map/ppermute | solution.py:28
  9.9 8.9 %collective-permute-start.1 = (bf16[64,1536]{1,0:T(8,128)(2,1)S(1)}, bf16[64,1536]{1,0:T(8,128)(2,1)S(1)}, u32[]{:S(2)}, u32[]{:S(2)}) collective-permute-start(bf16[64,1536]{1,0:T(8,128)(2,1)S(1)} %shard_map.76.refs_1_), channel_id=1, source_target_pairs={{0,1},{1,0},{2,3},{3,2},{4,5},{5,4},{6,7},{7,6},{8,9},{9,8},{10,11... | collective-permute-start | bytes 589832 | tf_op jit(solution)/shard_map/ppermute | solution.py:28
  11.1 7.7 %collective-permute-start.2 = (bf16[32,1536]{1,0:T(8,128)(2,1)S(1)}, bf16[32,1536]{1,0:T(8,128)(2,1)S(1)}, u32[]{:S(2)}, u32[]{:S(2)}) collective-permute-start(bf16[32,1536]{1,0:T(8,128)(2,1)S(1)} %shard_map.77.refs_3_), channel_id=1, source_target_pairs={{0,2},{1,3},{2,0},{3,1},{4,6},{5,7},{6,4},{7,5},{8,10},{9,11},{10,... | collective-permute-start | bytes 294920 | tf_op jit(solution)/shard_map/ppermute | solution.py:28
  20.2 4.2 %collective-permute-start.4 = (bf16[2,128,768]{2,1,0:T(8,128)(2,1)S(1)}, bf16[2,128,768]{2,1,0:T(8,128)(2,1)S(1)}, u32[]{:S(2)}, u32[]{:S(2)}) collective-permute-start(bf16[2,128,768]{2,1,0:T(8,128)(2,1)S(1)} %get-tuple-element.49.refs_8_), channel_id=1, source_target_pairs={{0,4},{4,0},{8,12},{12,8},{16,20},{20,16},{24,28},{28,24},{1,5},{5... | collective-permute-start | bytes 1179656 | tf_op jit(solution)/shard_map/ppermute | solution.py:28
  20.3 8.2 %collective-permute-start.6 = (bf16[64,1536]{1,0:T(8,128)(2,1)S(1)}, bf16[64,1536]{1,0:T(8,128)(2,1)S(1)}, u32[]{:S(2)}, u32[]{:S(2)}) collective-permute-start(bf16[64,1536]{1,0:T(8,128)(2,1)S(1)} %shard_map.79.refs_8_), channel_id=1, source_target_pairs={{0,1},{1,0},{2,3},{3,2},{4,5},{5,4},{6,7},{7,6},{8,9},{9,8},{10,11... | collective-permute-start | bytes 589832 | tf_op jit(solution)/shard_map/ppermute | solution.py:28
  24.2 7.6 %collective-permute-start.3 = (bf16[2,128,768]{2,1,0:T(8,128)(2,1)S(1)}, bf16[2,128,768]{2,1,0:T(8,128)(2,1)S(1)}, u32[]{:S(2)}, u32[]{:S(2)}) collective-permute-start(bf16[2,128,768]{2,1,0:T(8,128)(2,1)S(1)} %get-tuple-element.51.refs_2_), channel_id=1, source_target_pairs={{0,4},{4,0},{8,12},{12,8},{16,20},{20,16},{24,28},{28,24},{1,5},{5... | collective-permute-start | bytes 1179656 | tf_op jit(solution)/shard_map/ppermute | solution.py:28
  24.5 7.8 %collective-permute-start.5 = (bf16[2,128,768]{2,1,0:T(8,128)(2,1)S(1)}, bf16[2,128,768]{2,1,0:T(8,128)(2,1)S(1)}, u32[]{:S(2)}, u32[]{:S(2)}) collective-permute-start(bf16[2,128,768]{2,1,0:T(8,128)(2,1)S(1)} %shard_map.82.refs_2_), channel_id=1, source_target_pairs={{0,8},{4,20},{8,0},{12,28},{16,24},{20,4},{24,16},{28,12},{1,9},{5... | collective-permute-start | bytes 1179656 | tf_op jit(solution)/shard_map/ppermute | solution.py:38
  31.6 2.4 %collective-permute-start.8 = (bf16[2,128,768]{2,1,0:T(8,128)(2,1)S(1)}, bf16[2,128,768]{2,1,0:T(8,128)(2,1)S(1)}, u32[]{:S(2)}, u32[]{:S(2)}) collective-permute-start(bf16[2,128,768]{2,1,0:T(8,128)(2,1)S(1)} %get-tuple-element.56.refs_3_), channel_id=1, source_target_pairs={{0,4},{4,0},{8,12},{12,8},{16,20},{20,16},{24,28},{28,24},{1,5},{5... | collective-permute-start | bytes 1179656 | tf_op jit(solution)/shard_map/ppermute | solution.py:28
  32.4 7.6 %collective-permute-start.7 = (bf16[1,128,768]{2,1,0:T(8,128)(2,1)S(1)}, bf16[1,128,768]{2,1,0:T(8,128)(2,1)S(1)}, u32[]{:S(2)}, u32[]{:S(2)}) collective-permute-start(bf16[1,128,768]{2,1,0:T(8,128)(2,1)S(1)} %shard_map.85.refs_2_), channel_id=1, source_target_pairs={{0,16},{4,12},{8,24},{12,4},{16,0},{20,28},{24,8},{28,20},{1,17},{... | collective-permute-start | bytes 589832 | tf_op jit(solution)/shard_map/ppermute | solution.py:38
  34.1 7.8 %collective-permute-start.11 = (bf16[2,128,768]{2,1,0:T(8,128)(2,1)S(1)}, bf16[2,128,768]{2,1,0:T(8,128)(2,1)S(1)}, u32[]{:S(2)}, u32[]{:S(2)}) collective-permute-start(bf16[2,128,768]{2,1,0:T(8,128)(2,1)S(1)} %shard_map.86.refs_2_), channel_id=1, source_target_pairs={{0,8},{4,20},{8,0},{12,28},{16,24},{20,4},{24,16},{28,12},{1,9},{5... | collective-permute-start | bytes 1179656 | tf_op jit(solution)/shard_map/ppermute | solution.py:38
  39.7 2.1 %collective-permute-start.10 = (bf16[1,128,768]{2,1,0:T(8,128)(2,1)S(1)}, bf16[1,128,768]{2,1,0:T(8,128)(2,1)S(1)}, u32[]{:S(2)}, u32[]{:S(2)}) collective-permute-start(bf16[1,128,768]{2,1,0:T(8,128)(2,1)S(1)} %get-tuple-element.60.refs_4_), channel_id=1, source_target_pairs={{0,4},{4,0},{8,12},{12,8},{16,20},{20,16},{24,28},{28,24},{1,5},{5... | collective-permute-start | bytes 589832 | tf_op jit(solution)/shard_map/ppermute | solution.py:28
  40.3 6.8 %collective-permute-start.9 = (bf16[128,768]{1,0:T(8,128)(2,1)S(1)}, bf16[128,768]{1,0:T(8,128)(2,1)S(1)}, u32[]{:S(2)}, u32[]{:S(2)}) collective-permute-start(bf16[128,768]{1,0:T(8,128)(2,1)S(1)} %get-tuple-element.61.refs_3_.refs_0_), channel_id=1, source_target_pairs={{0,8},{4,20},{8,0},{12,28},{16,24},{20,4},{24,16},{28,12},{1,9},{5... | collective-permute-start | bytes 589832 | tf_op jit(solution)/shard_map/ppermute | solution.py:38
  42.1 8.4 %collective-permute-start.13 = (bf16[1,128,768]{2,1,0:T(8,128)(2,1)S(1)}, bf16[1,128,768]{2,1,0:T(8,128)(2,1)S(1)}, u32[]{:S(2)}, u32[]{:S(2)}) collective-permute-start(bf16[1,128,768]{2,1,0:T(8,128)(2,1)S(1)} %shard_map.90.refs_2_), channel_id=1, source_target_pairs={{0,16},{4,12},{8,24},{12,4},{16,0},{20,28},{24,8},{28,20},{1,17},{... | collective-permute-start | bytes 589832 | tf_op jit(solution)/shard_map/ppermute | solution.py:38
  48.8 1.6 %collective-permute-start.14 = (bf16[1,128,768]{2,1,0:T(8,128)(2,1)S(1)}, bf16[1,128,768]{2,1,0:T(8,128)(2,1)S(1)}, u32[]{:S(2)}, u32[]{:S(2)}) collective-permute-start(bf16[1,128,768]{2,1,0:T(8,128)(2,1)S(1)} %get-tuple-element.67.refs_5_), channel_id=1, source_target_pairs={{0,4},{4,0},{8,12},{12,8},{16,20},{20,16},{24,28},{28,24},{1,5},{5... | collective-permute-start | bytes 589832 | tf_op jit(solution)/shard_map/ppermute | solution.py:28
  48.9 7.8 %collective-permute-start.12 = (bf16[256,768]{1,0:T(8,128)(2,1)S(1)}, bf16[256,768]{1,0:T(8,128)(2,1)S(1)}, u32[]{:S(2)}, u32[]{:S(2)}) collective-permute-start(bf16[256,768]{1,0:T(8,128)(2,1)S(1)} %shard_map.92.refs_6_.refs_0_), channel_id=1, source_target_pairs={{0,16},{4,12},{8,24},{12,4},{16,0},{20,28},{24,8},{28,20},{1,17},{... | collective-permute-start | bytes 1179656 | tf_op jit(solution)/shard_map/ppermute | solution.py:38
  56.8 7.9 %collective-permute-start.15 = (bf16[512,768]{1,0:T(8,128)(2,1)S(1)}, bf16[512,768]{1,0:T(8,128)(2,1)S(1)}, u32[]{:S(2)}, u32[]{:S(2)}) collective-permute-start(bf16[512,768]{1,0:T(8,128)(2,1)S(1)} %shard_map.95.refs_1_.refs_5_.refs_0_), channel_id=1, source_target_pairs={{0,4},{4,0},{8,12},{12,8},{16,20},{20,16},{24,28},{28,24},{1,5},{5... | collective-permute-start | bytes 2359304 | tf_op jit(solution)/shard_map/ppermute | solution.py:28
  56.8 5.9 %collective-permute-start.16 = (bf16[128,768]{1,0:T(8,128)(2,1)S(1)}, bf16[128,768]{1,0:T(8,128)(2,1)S(1)}, u32[]{:S(2)}, u32[]{:S(2)}) collective-permute-start(bf16[128,768]{1,0:T(8,128)(2,1)S(1)} %shard_map.94.refs_2_.refs_0_), channel_id=1, source_target_pairs={{0,8},{4,20},{8,0},{12,28},{16,24},{20,4},{24,16},{28,12},{1,9},{5... | collective-permute-start | bytes 589832 | tf_op jit(solution)/shard_map/ppermute | solution.py:38
  62.7 11.5 %collective-permute-start.19 = (bf16[256,768]{1,0:T(8,128)(2,1)S(1)}, bf16[256,768]{1,0:T(8,128)(2,1)S(1)}, u32[]{:S(2)}, u32[]{:S(2)}) collective-permute-start(bf16[256,768]{1,0:T(8,128)(2,1)S(1)} %shard_map.97.refs_10_.refs_0_), channel_id=1, source_target_pairs={{0,16},{4,12},{8,24},{12,4},{16,0},{20,28},{24,8},{28,20},{1,17},{... | collective-permute-start | bytes 1179656 | tf_op jit(solution)/shard_map/ppermute | solution.py:38
  67.4 6.7 %collective-permute-start.17 = (bf16[64,1536]{1,0:T(8,128)(2,1)S(1)}, bf16[64,1536]{1,0:T(8,128)(2,1)S(1)}, u32[]{:S(2)}, u32[]{:S(2)}) collective-permute-start(bf16[64,1536]{1,0:T(8,128)(2,1)S(1)} %get-tuple-element.69.refs_6_), channel_id=1, source_target_pairs={{0,1},{1,0},{2,3},{3,2},{4,5},{5,4},{6,7},{7,6},{8,9},{9,8},{10,11... | collective-permute-start | bytes 589832 | tf_op jit(solution)/shard_map/ppermute | solution.py:28
  74.3 2.4 %collective-permute-start.20 = (bf16[512,768]{1,0:T(8,128)(2,1)S(1)}, bf16[512,768]{1,0:T(8,128)(2,1)S(1)}, u32[]{:S(2)}, u32[]{:S(2)}) collective-permute-start(bf16[512,768]{1,0:T(8,128)(2,1)S(1)} %shard_map.101.refs_0_.refs_10_.refs_1_), channel_id=1, source_target_pairs={{0,4},{4,0},{8,12},{12,8},{16,20},{20,16},{24,28},{28,24},{1,5},{5... | collective-permute-start | bytes 2359304 | tf_op jit(solution)/shard_map/ppermute | solution.py:28
  74.4 12.8 %collective-permute-start.18 = (bf16[32,1536]{1,0:T(8,128)(2,1)S(1)}, bf16[32,1536]{1,0:T(8,128)(2,1)S(1)}, u32[]{:S(2)}, u32[]{:S(2)}) collective-permute-start(bf16[32,1536]{1,0:T(8,128)(2,1)S(1)} %get-tuple-element.71.refs_2_), channel_id=1, source_target_pairs={{0,2},{1,3},{2,0},{3,1},{4,6},{5,7},{6,4},{7,5},{8,10},{9,11},{10,... | collective-permute-start | bytes 294920 | tf_op jit(solution)/shard_map/ppermute | solution.py:28
  82.7 14.0 %collective-permute-start.22 = (bf16[32,1536]{1,0:T(8,128)(2,1)S(1)}, bf16[32,1536]{1,0:T(8,128)(2,1)S(1)}, u32[]{:S(2)}, u32[]{:S(2)}) collective-permute-start(bf16[32,1536]{1,0:T(8,128)(2,1)S(1)} %get-tuple-element.74), channel_id=1, source_target_pairs={{0,2},{1,3},{2,0},{3,1},{4,6},{5,7},{6,4},{7,5},{8,10},{9,11},{10,... | collective-permute-start | bytes 294920 | tf_op jit(solution)/shard_map/ppermute | solution.py:28
  84.5 12.1 %collective-permute-start.23 = (bf16[32,1536]{1,0:T(8,128)(2,1)S(1)}, bf16[32,1536]{1,0:T(8,128)(2,1)S(1)}, u32[]{:S(2)}, u32[]{:S(2)}) collective-permute-start(bf16[32,1536]{1,0:T(8,128)(2,1)S(1)} %get-tuple-element.75), channel_id=1, source_target_pairs={{0,1},{1,0},{2,3},{3,2},{4,5},{5,4},{6,7},{7,6},{8,9},{9,8},{10,11... | collective-permute-start | bytes 294920 | tf_op jit(solution)/shard_map/ppermute | solution.py:28
  84.8 11.9 %collective-permute-start.21 = (bf16[32,1536]{1,0:T(8,128)(2,1)S(1)}, bf16[32,1536]{1,0:T(8,128)(2,1)S(1)}, u32[]{:S(2)}, u32[]{:S(2)}) collective-permute-start(bf16[32,1536]{1,0:T(8,128)(2,1)S(1)} %get-tuple-element.72.refs_2_), channel_id=1, source_target_pairs={{0,3},{1,2},{2,1},{3,0},{4,7},{5,6},{6,5},{7,4},{8,11},{9,10},{10,... | collective-permute-start | bytes 294920 | tf_op jit(solution)/shard_map/ppermute | solution.py:28
  (2 other events, 6.8 us)
where the time goes:
time: 97.5 us; the launch traced here: 97.4 us
  Pallas kernels  53.6 us (55%)
  starting transfers between devices  30.9 us (32%)
  waiting for transfers between devices  11.2 us (11%)
    pallas_call x30, Pallas kernels, call(): pl.pallas_call(body, in_specs=[specs[space] for space, value in arrays] +...  53.6 us
    ppermute x16, starting transfers between devices, swap(): return lax.ppermute(value, axis, [(i, i ^ flip) for i in range(count)])  18 us
    ppermute x8, starting transfers between devices, across(): return lax.ppermute(value, 'row', [(i, i ^ flips[i]) for i in range(rows)])  13 us
    ppermute x8, waiting for transfers between devices, across(): return lax.ppermute(value, 'row', [(i, i ^ flips[i]) for i in range(rows)])  7.84 us
    ppermute x16, waiting for transfers between devices, swap(): return lax.ppermute(value, axis, [(i, i ^ flip) for i in range(count)])  3.38 us
  transfers between devices with their start and end apart: 24, of which 8 were waited for; matrix products, arithmetic and copies ran while one was open for 0% of the time, Pallas kernels for 53%

commit v1 on v0

--- a/solution.py
+++ b/solution.py
@@ -12,7 +12,7 @@
 VMEM_LIMIT = 10 * 1024 * 1024
 WRITES = 6
 READ_CUTS, WRITE_CUTS = 4, 3
-WEIGHTY = 6 * 10**9
+PART_COST = 10**9
 
 
 def gelu_fn(value):
@@ -356,12 +356,13 @@
     return total
 
 
-def sent_sum(terms):
+def one_block(terms, dtype=BF16, flops=0):
     def kernel(*refs):
-        refs[-1][0] = block_of(terms)(refs).astype(BF16)
+        refs[-1][0] = block_of(terms)(refs).astype(dtype)
 
     shape = (1, *terms[0][0].shape[1:])
-    return call(kernel, in_vmem([array for array, block in terms]), [("vmem", (shape, BF16))], 0, 0)[0]
+    arrays = in_vmem([array for array, block in terms])
+    return call(kernel, arrays, [("vmem", (shape, dtype))], flops, 0)[0]
 
 
 def activate(terms):
@@ -372,7 +373,7 @@
 
     shape = terms[0][0].shape[1:]
     outs = [("vmem", (shape, F32)), ("vmem", (shape, BF16))]
-    return call(kernel, in_vmem([array for array, block in terms]), outs, WEIGHTY, 0)
+    return call(kernel, in_vmem([array for array, block in terms]), outs, 0, 0)
 
 
 def activate_back(hidden, terms):
@@ -380,7 +381,7 @@
         refs[-1][...] = gelu_back(hidden_ref[...], block_of(terms)(refs))
 
     arrays = [hidden] + [array for array, block in terms]
-    return call(kernel, in_vmem(arrays), [("vmem", (hidden.shape, BF16))], WEIGHTY, 0)[0]
+    return call(kernel, in_vmem(arrays), [("vmem", (hidden.shape, BF16))], 0, 0)[0]
 
 
 def exchange_col(parts, cols):
@@ -430,21 +431,22 @@
     load(wanted[5 * min(2, len(flips)) : 12])
     keep, sent = project(w_out, cot_shards, first, [])
     got = other_core(sent)
-    sent = sent_sum([(here, 0), (got_here, 0), (came, 1)])
+    sent = one_block([(here, 0), (got_here, 0), (came, 1)])
     terms = [(here, 1), (got_here, 1), (came, 0), (across(sent, 1, rows), 0)]
 
     came = across(added([keep, got]), 0, rows)
     load(wanted[12:14])
+    hidden, act = activate(terms)
     keep, sent = project(w_out, cot_shards, second, [])
     got = other_core(sent)
-    hidden, act = activate(terms)
-    sent = sent_sum([(keep, 0), (got, 0), (came, 1)])
+    stack = doubled(act, 0)
+    sent = one_block([(keep, 0), (got, 0), (came, 1)])
     last = across(sent, 1, rows)
     load(wanted[14:])
-    stack = doubled(act, 0)
     keep, sent = project(w_out, cot_shards, own, [])
     got = other_core(sent)
-    grad_hidden = activate_back(hidden, [(keep, 0), (came, 0), (last, 0), (got, 0)])
+    part = one_block([(came, 0), (last, 0)], F32, PART_COST)
+    grad_hidden = activate_back(hidden, [(keep, 0), (part, 0), (got, 0)])
     stack = doubled(stack, 1)
     act = stack, other_core(stack)
     grad_w_out = weight_grad(w_out, act[:1], (0,), cot_shards)

time: 97.5 us -> 97 us (level)
  starting transfers between devices: 30.9 us -> 29.9 us
    ppermute x8, starting transfers between devices: 13 us -> 11.8 us  [across(): return lax.ppermute(value, 'row', [(i, i ^ flips[i]) for i in range(rows)])]
    pallas_call x30 -> x31, Pallas kernels: 53.6 us -> 53.5 us  [call(): pl.pallas_call(body, in_specs=[specs[space] for space, value in arrays] +...]
  transfers between devices with their start and end apart: 24 -> 24, of which waited for: 8 -> 7; matrix products, arithmetic and copies ran while one was open for 0% -> 0% of each run, Pallas kernels for 53% -> 54%
where the time goes in v1:
time: 97 us; the launch traced here: 96.9 us
  Pallas kernels  53.5 us (55%)
  starting transfers between devices  29.9 us (31%)
  waiting for transfers between devices  11.8 us (12%)
  between operations  0.97 us (1%)
    pallas_call x31, Pallas kernels, call(): pl.pallas_call(body, in_specs=[specs[space] for space, value in arrays] +...  53.5 us
    ppermute x16, starting transfers between devices, swap(): return lax.ppermute(value, axis, [(i, i ^ flip) for i in range(count)])  18.1 us
    ppermute x8, starting transfers between devices, across(): return lax.ppermute(value, 'row', [(i, i ^ flips[i]) for i in range(rows)])  11.8 us
    ppermute x8, waiting for transfers between devices, across(): return lax.ppermute(value, 'row', [(i, i ^ flips[i]) for i in range(rows)])  8.54 us
    ppermute x16, waiting for transfers between devices, swap(): return lax.ppermute(value, axis, [(i, i ^ flip) for i in range(count)])  3.27 us
  transfers between devices with their start and end apart: 24, of which 7 were waited for; matrix products, arithmetic and copies ran while one was open for 0% of the time, Pallas kernels for 54%

profile of v1, /device:TPU:0, one launch (start us, length us, event | category | flops | bytes accessed | tf_op | source)
XLA Modules:
  0.0 96.9 jit_solution(2138736857900977390)
XLA Ops:
  0.6 4.1 %collective-permute-start = (bf16[32,1536]{1,0:T(8,128)(2,1)}, bf16[32,1536]{1,0:T(8,128)(2,1)S(1)}, u32[]{:S(2)}, u32[]{:S(2)}) collective-permute-start(bf16[32,1536]{1,0:T(8,128)(2,1)} %refs_3_.1), channel_id=1, source_target_pairs={{0,2},{1,3},{2,0},{3,1},{4,6},{5,7},{6,4},{7,5},{8,10},{9,11},{10,... | collective-permute-start | bytes 294920 | tf_op jit(solution)/shard_map/ppermute | solution.py:28
  4.7 4.6 %shard_map.75 = (bf16[1536,768]{1,0:T(8,128)(2,1)S(1)}, bf16[1536,768]{1,0:T(8,128)(2,1)S(1)}, bf16[1536,768]{1,0:T(8,128)(2,1)S(1)}, bf16[1536,768]{1,0:T(8,128)(2,1)S(1)}, bf16[1536,768]{1,0:T(8,128)(2,1)S(1)}) custom-call(s32[1]{0:T(128)} %bitcast.refs_0_, bf16[1536,6144]{1,0:T(8,128)(2,1)} %refs_1_.11), custom_call_target="tpu_custom_call" | custom-call | tf_op jit(solution)/shard_map/pallas_call | solution.py:69
  11.1 3.0 %collective-permute-start.2 = (bf16[32,1536]{1,0:T(8,128)(2,1)S(1)}, bf16[32,1536]{1,0:T(8,128)(2,1)S(1)}, u32[]{:S(2)}, u32[]{:S(2)}) collective-permute-start(bf16[32,1536]{1,0:T(8,128)(2,1)S(1)} %shard_map.77.refs_3_), channel_id=1, source_target_pairs={{0,2},{1,3},{2,0},{3,1},{4,6},{5,7},{6,4},{7,5},{8,10},{9,11},{10,... | collective-permute-start | bytes 294920 | tf_op jit(solution)/shard_map/ppermute | solution.py:28
  14.1 4.6 %shard_map.78 = (bf16[1536,768]{1,0:T(8,128)(2,1)S(1)}, bf16[1536,768]{1,0:T(8,128)(2,1)S(1)}, bf16[1536,768]{1,0:T(8,128)(2,1)S(1)}, bf16[768,1536]{1,0:T(8,128)(2,1)S(1)}, bf16[768,1536]{1,0:T(8,128)(2,1)S(1)}) custom-call(s32[1]{0:T(128)} %bitcast.refs_0_, bf16[1536,6144]{1,0:T(8,128)(2,1)} %refs_1_.11, bf16[6144,1536]{1,0:T(8,128)(2,1)} %refs_1_.18, ...), custom_call_target="tpu_custom_call" | custom-call | tf_op jit(solution)/shard_map/pallas_call | solution.py:69
  20.3 2.5 %collective-permute-start.6 = (bf16[64,1536]{1,0:T(8,128)(2,1)S(1)}, bf16[64,1536]{1,0:T(8,128)(2,1)S(1)}, u32[]{:S(2)}, u32[]{:S(2)}) collective-permute-start(bf16[64,1536]{1,0:T(8,128)(2,1)S(1)} %shard_map.79.refs_8_), channel_id=1, source_target_pairs={{0,1},{1,0},{2,3},{3,2},{4,5},{5,4},{6,7},{7,6},{8,9},{9,8},{10,11... | collective-permute-start | bytes 589832 | tf_op jit(solution)/shard_map/ppermute | solution.py:28
  26.1 2.4 %shard_map.83 = (bf16[768,1536]{1,0:T(8,128)(2,1)S(1)}, bf16[768,1536]{1,0:T(8,128)(2,1)S(1)}) custom-call(s32[1]{0:T(128)} %bitcast.refs_0_, bf16[6144,1536]{1,0:T(8,128)(2,1)} %refs_1_.18, bf16[2,128,768]{2,1,0:T(8,128)(2,1)S(1)} %shard_map.82.refs_2_), custom_call_target="tpu_custom_call" | custom-call | tf_op jit(solution)/shard_map/pallas_call | solution.py:69
  28.5 3.2 %shard_map.84 = (bf16[2,128,768]{2,1,0:T(8,128)(2,1)S(1)}, bf16[2,128,768]{2,1,0:T(8,128)(2,1)S(1)}) custom-call(s32[1]{0:T(128)} %bitcast.refs_0_, bf16[32,1536]{1,0:T(8,128)(2,1)S(1)} %copy-done, bf16[32,1536]{1,0:T(8,128)(2,1)S(1)} %collective-permute-done.2.refs_1_.refs_2_.refs_3_, bf16[64,1536]{1,0:T(8,128)(2,1)S(1)} %collective-permute-done.6.refs_3_.refs_4_, ...), custom_call_target="tpu_custom_call" | custom-call | tf_op jit(solution)/shard_map/pallas_call | solution.py:69
  35.7 2.4 %shard_map.87 = (bf16[768,1536]{1,0:T(8,128)(2,1)S(1)}, bf16[768,1536]{1,0:T(8,128)(2,1)S(1)}) custom-call(s32[1]{0:T(128)} %bitcast.refs_0_, bf16[6144,1536]{1,0:T(8,128)(2,1)} %refs_1_.18, bf16[2,128,768]{2,1,0:T(8,128)(2,1)S(1)} %shard_map.86.refs_2_), custom_call_target="tpu_custom_call" | custom-call | tf_op jit(solution)/shard_map/pallas_call | solution.py:69
  38.1 2.0 %collective-permute-done.7.refs_3_ = bf16[1,128,768]{2,1,0:T(8,128)(2,1)S(1)} collective-permute-done((bf16[1,128,768]{2,1,0:T(8,128)(2,1)S(1)}, bf16[1,128,768]{2,1,0:T(8,128)(2,1)S(1)}, u32[]{:S(2)}, u32[]{:S(2)}) %collective-permute-start.7) | collective-permute-done | bytes 196640 | tf_op jit(solution)/shard_map/ppermute | solution.py:38
  41.9 1.6 %shard_map.89 = (bf16[1,128,768]{2,1,0:T(8,128)(2,1)S(1)}, bf16[1,128,768]{2,1,0:T(8,128)(2,1)S(1)}) custom-call(s32[1]{0:T(128)} %bitcast.refs_0_, bf16[32,1536]{1,0:T(8,128)(2,1)S(1)} %copy-done, bf16[32,1536]{1,0:T(8,128)(2,1)S(1)} %collective-permute-done.2.refs_1_.refs_2_.refs_3_, bf16[64,1536]{1,0:T(8,128)(2,1)S(1)} %collective-permute-done.6.refs_3_.refs_4_, ...), custom_call_target="tpu_custom_call" | custom-call | tf_op jit(solution)/shard_map/pallas_call | solution.py:69
  43.6 2.4 %collective-permute-done.9.refs_1_ = bf16[128,768]{1,0:T(8,128)(2,1)S(1)} collective-permute-done((bf16[128,768]{1,0:T(8,128)(2,1)S(1)}, bf16[128,768]{1,0:T(8,128)(2,1)S(1)}, u32[]{:S(2)}, u32[]{:S(2)}) %collective-permute-start.9) | collective-permute-done | bytes 196640 | tf_op jit(solution)/shard_map/ppermute | solution.py:38
  48.3 2.4 %shard_map.92 = (bf16[768,1536]{1,0:T(8,128)(2,1)S(1)}, bf16[768,1536]{1,0:T(8,128)(2,1)S(1)}) custom-call(s32[1]{0:T(128)} %bitcast.refs_0_, bf16[6144,1536]{1,0:T(8,128)(2,1)} %refs_1_.18, bf16[1,128,768]{2,1,0:T(8,128)(2,1)S(1)} %shard_map.91.refs_2_), custom_call_target="tpu_custom_call" | custom-call | tf_op jit(solution)/shard_map/pallas_call | solution.py:69
  50.7 1.6 %shard_map.93 = (bf16[1,128,768]{2,1,0:T(8,128)(2,1)S(1)}, bf16[1,128,768]{2,1,0:T(8,128)(2,1)S(1)}) custom-call(s32[1]{0:T(128)} %bitcast.refs_0_, bf16[32,1536]{1,0:T(8,128)(2,1)S(1)} %copy-done, bf16[32,1536]{1,0:T(8,128)(2,1)S(1)} %collective-permute-done.2.refs_1_.refs_2_.refs_3_, bf16[64,1536]{1,0:T(8,128)(2,1)S(1)} %collective-permute-done.6.refs_3_.refs_4_, ...), custom_call_target="tpu_custom_call" | custom-call | tf_op jit(solution)/shard_map/pallas_call | solution.py:69
  52.4 3.6 %collective-permute-done.13.refs_1_ = bf16[1,128,768]{2,1,0:T(8,128)(2,1)S(1)} collective-permute-done((bf16[1,128,768]{2,1,0:T(8,128)(2,1)S(1)}, bf16[1,128,768]{2,1,0:T(8,128)(2,1)S(1)}, u32[]{:S(2)}, u32[]{:S(2)}) %collective-permute-start.13) | collective-permute-done | bytes 196640 | tf_op jit(solution)/shard_map/ppermute | solution.py:38
  58.1 4.2 %shard_map.97.refs_2_.refs_5_ = bf16[6144,1536]{1,0:T(8,128)(2,1)} custom-call(s32[1]{0:T(128)} %bitcast.refs_0_, bf16[512,768]{1,0:T(8,128)(2,1)S(1)} %shard_map.96.refs_1_.refs_5_.refs_0_, bf16[32,1536]{1,0:T(8,128)(2,1)S(1)} %copy-done, bf16[32,1536]{1,0:T(8,128)(2,1)S(1)} %collective-permute-done.2.refs_1_.refs_2_.refs_3_, ...), custom_call_target="tpu_custom_call" | custom-call | flops 1207959552 | bytes 9437184 | tf_op jit(solution)/shard_map/pallas_call | solution.py:69
  62.4 1.7 %collective-permute-start.19 = (bf16[256,768]{1,0:T(8,128)(2,1)S(1)}, bf16[256,768]{1,0:T(8,128)(2,1)S(1)}, u32[]{:S(2)}, u32[]{:S(2)}) collective-permute-start(bf16[256,768]{1,0:T(8,128)(2,1)S(1)} %shard_map.98.refs_10_.refs_0_), channel_id=1, source_target_pairs={{0,16},{4,12},{8,24},{12,4},{16,0},{20,28},{24,8},{28,20},{1,17},{... | collective-permute-start | bytes 1179656 | tf_op jit(solution)/shard_map/ppermute | solution.py:38
  64.1 2.8 %shard_map.99 = (bf16[64,1536]{1,0:T(8,128)(2,1)S(1)}, bf16[64,1536]{1,0:T(8,128)(2,1)S(1)}) custom-call(bf16[512,768]{1,0:T(8,128)(2,1)S(1)} %shard_map.96.refs_1_.refs_5_.refs_0_, bf16[512,768]{1,0:T(8,128)(2,1)S(1)} %collective-permute-done.15.refs_1_, bf16[768,1536]{1,0:T(8,128)(2,1)S(1)} %get-tuple-element.65.refs_5_.refs_6_.refs_2_, ...), custom_call_target="tpu_custom_call" | custom-call | flops 2415919104 | bytes 18874368 | tf_op jit(solution)/shard_map/pallas_call | solution.py:69
  67.2 4.2 %shard_map.100.refs_2_ = bf16[6144,1536]{1,0:T(8,128)(2,1)} custom-call(s32[1]{0:T(128)} %bitcast.refs_0_, bf16[512,768]{1,0:T(8,128)(2,1)S(1)} %collective-permute-done.15.refs_1_, bf16[32,1536]{1,0:T(8,128)(2,1)S(1)} %copy-done, bf16[32,1536]{1,0:T(8,128)(2,1)S(1)} %collective-permute-done.2.refs_1_.refs_2_.refs_3_, ...), custom_call_target="tpu_custom_call", output_to_operand_aliasing={{}: (5, {})} | custom-call | flops 1207959552 | bytes 9437184 | tf_op jit(solution)/shard_map/pallas_call | solution.py:69
  71.4 2.3 %collective-permute-done.17.refs_1_ = bf16[64,1536]{1,0:T(8,128)(2,1)S(1)} collective-permute-done((bf16[64,1536]{1,0:T(8,128)(2,1)S(1)}, bf16[64,1536]{1,0:T(8,128)(2,1)S(1)}, u32[]{:S(2)}, u32[]{:S(2)}) %collective-permute-start.17) | collective-permute-done | bytes 196640 | tf_op jit(solution)/shard_map/ppermute | solution.py:28
  73.9 1.8 %collective-permute-start.18 = (bf16[32,1536]{1,0:T(8,128)(2,1)S(1)}, bf16[32,1536]{1,0:T(8,128)(2,1)S(1)}, u32[]{:S(2)}, u32[]{:S(2)}) collective-permute-start(bf16[32,1536]{1,0:T(8,128)(2,1)S(1)} %get-tuple-element.71.refs_2_), channel_id=1, source_target_pairs={{0,2},{1,3},{2,0},{3,1},{4,6},{5,7},{6,4},{7,5},{8,10},{9,11},{10,... | collective-permute-start | bytes 294920 | tf_op jit(solution)/shard_map/ppermute | solution.py:28
  76.2 6.0 %shard_map.103 = (bf16[32,1536]{1,0:T(8,128)(2,1)S(1)}, bf16[32,1536]{1,0:T(8,128)(2,1)S(1)}, bf16[32,1536]{1,0:T(8,128)(2,1)S(1)}, bf16[32,1536]{1,0:T(8,128)(2,1)S(1)}) custom-call(bf16[512,768]{1,0:T(8,128)(2,1)S(1)} %shard_map.102.refs_0_.refs_10_.refs_1_, bf16[512,768]{1,0:T(8,128)(2,1)S(1)} %collective-permute-done.20.refs_1_.refs_2_, ...), custom_call_target="tpu_custom_call" | custom-call | flops 2415919104 | bytes 18874368 | tf_op jit(solution)/shard_map/pallas_call | solution.py:69
  82.2 1.8 %collective-permute-start.22 = (bf16[32,1536]{1,0:T(8,128)(2,1)S(1)}, bf16[32,1536]{1,0:T(8,128)(2,1)S(1)}, u32[]{:S(2)}, u32[]{:S(2)}) collective-permute-start(bf16[32,1536]{1,0:T(8,128)(2,1)S(1)} %get-tuple-element.74), channel_id=1, source_target_pairs={{0,2},{1,3},{2,0},{3,1},{4,6},{5,7},{6,4},{7,5},{8,10},{9,11},{10,... | collective-permute-start | bytes 294920 | tf_op jit(solution)/shard_map/ppermute | solution.py:28
  84.3 2.4 %collective-permute-start.21 = (bf16[32,1536]{1,0:T(8,128)(2,1)S(1)}, bf16[32,1536]{1,0:T(8,128)(2,1)S(1)}, u32[]{:S(2)}, u32[]{:S(2)}) collective-permute-start(bf16[32,1536]{1,0:T(8,128)(2,1)S(1)} %get-tuple-element.72.refs_2_), channel_id=1, source_target_pairs={{0,3},{1,2},{2,1},{3,0},{4,7},{5,6},{6,5},{7,4},{8,11},{9,10},{10,... | collective-permute-start | bytes 294920 | tf_op jit(solution)/shard_map/ppermute | solution.py:28
  87.3 8.8 %shard_map.105 = bf16[1536,6144]{1,0:T(8,128)(2,1)} custom-call(s32[1]{0:T(128)} %bitcast.refs_0_, bf16[512,768]{1,0:T(8,128)(2,1)S(1)} %shard_map.102.refs_0_.refs_10_.refs_1_, bf16[512,768]{1,0:T(8,128)(2,1)S(1)} %collective-permute-done.20.refs_1_.refs_2_, bf16[32,1536]{1,0:T(8,128)(2,1)S(1)} %copy-done.1, ...), custom_call_target="tpu_custom_call" | custom-call | flops 2415919104 | bytes 18874368 | tf_op jit(solution)/shard_map/pallas_call | solution.py:69
  (60 shorter events, 19.4 us)
Async XLA Ops:
  0.6 9.2 %collective-permute-start = (bf16[32,1536]{1,0:T(8,128)(2,1)}, bf16[32,1536]{1,0:T(8,128)(2,1)S(1)}, u32[]{:S(2)}, u32[]{:S(2)}) collective-permute-start(bf16[32,1536]{1,0:T(8,128)(2,1)} %refs_3_.1), channel_id=1, source_target_pairs={{0,2},{1,3},{2,0},{3,1},{4,6},{5,7},{6,4},{7,5},{8,10},{9,11},{10,... | collective-permute-start | bytes 294920 | tf_op jit(solution)/shard_map/ppermute | solution.py:28
  9.9 8.9 %collective-permute-start.1 = (bf16[64,1536]{1,0:T(8,128)(2,1)S(1)}, bf16[64,1536]{1,0:T(8,128)(2,1)S(1)}, u32[]{:S(2)}, u32[]{:S(2)}) collective-permute-start(bf16[64,1536]{1,0:T(8,128)(2,1)S(1)} %shard_map.76.refs_1_), channel_id=1, source_target_pairs={{0,1},{1,0},{2,3},{3,2},{4,5},{5,4},{6,7},{7,6},{8,9},{9,8},{10,11... | collective-permute-start | bytes 589832 | tf_op jit(solution)/shard_map/ppermute | solution.py:28
  11.1 7.7 %collective-permute-start.2 = (bf16[32,1536]{1,0:T(8,128)(2,1)S(1)}, bf16[32,1536]{1,0:T(8,128)(2,1)S(1)}, u32[]{:S(2)}, u32[]{:S(2)}) collective-permute-start(bf16[32,1536]{1,0:T(8,128)(2,1)S(1)} %shard_map.77.refs_3_), channel_id=1, source_target_pairs={{0,2},{1,3},{2,0},{3,1},{4,6},{5,7},{6,4},{7,5},{8,10},{9,11},{10,... | collective-permute-start | bytes 294920 | tf_op jit(solution)/shard_map/ppermute | solution.py:28
  20.2 4.2 %collective-permute-start.4 = (bf16[2,128,768]{2,1,0:T(8,128)(2,1)S(1)}, bf16[2,128,768]{2,1,0:T(8,128)(2,1)S(1)}, u32[]{:S(2)}, u32[]{:S(2)}) collective-permute-start(bf16[2,128,768]{2,1,0:T(8,128)(2,1)S(1)} %get-tuple-element.49.refs_8_), channel_id=1, source_target_pairs={{0,4},{4,0},{8,12},{12,8},{16,20},{20,16},{24,28},{28,24},{1,5},{5... | collective-permute-start | bytes 1179656 | tf_op jit(solution)/shard_map/ppermute | solution.py:28
  20.3 8.2 %collective-permute-start.6 = (bf16[64,1536]{1,0:T(8,128)(2,1)S(1)}, bf16[64,1536]{1,0:T(8,128)(2,1)S(1)}, u32[]{:S(2)}, u32[]{:S(2)}) collective-permute-start(bf16[64,1536]{1,0:T(8,128)(2,1)S(1)} %shard_map.79.refs_8_), channel_id=1, source_target_pairs={{0,1},{1,0},{2,3},{3,2},{4,5},{5,4},{6,7},{7,6},{8,9},{9,8},{10,11... | collective-permute-start | bytes 589832 | tf_op jit(solution)/shard_map/ppermute | solution.py:28
  24.2 7.6 %collective-permute-start.3 = (bf16[2,128,768]{2,1,0:T(8,128)(2,1)S(1)}, bf16[2,128,768]{2,1,0:T(8,128)(2,1)S(1)}, u32[]{:S(2)}, u32[]{:S(2)}) collective-permute-start(bf16[2,128,768]{2,1,0:T(8,128)(2,1)S(1)} %get-tuple-element.51.refs_2_), channel_id=1, source_target_pairs={{0,4},{4,0},{8,12},{12,8},{16,20},{20,16},{24,28},{28,24},{1,5},{5... | collective-permute-start | bytes 1179656 | tf_op jit(solution)/shard_map/ppermute | solution.py:28
  24.5 7.8 %collective-permute-start.5 = (bf16[2,128,768]{2,1,0:T(8,128)(2,1)S(1)}, bf16[2,128,768]{2,1,0:T(8,128)(2,1)S(1)}, u32[]{:S(2)}, u32[]{:S(2)}) collective-permute-start(bf16[2,128,768]{2,1,0:T(8,128)(2,1)S(1)} %shard_map.82.refs_2_), channel_id=1, source_target_pairs={{0,8},{4,20},{8,0},{12,28},{16,24},{20,4},{24,16},{28,12},{1,9},{5... | collective-permute-start | bytes 1179656 | tf_op jit(solution)/shard_map/ppermute | solution.py:38
  31.7 2.4 %collective-permute-start.8 = (bf16[2,128,768]{2,1,0:T(8,128)(2,1)S(1)}, bf16[2,128,768]{2,1,0:T(8,128)(2,1)S(1)}, u32[]{:S(2)}, u32[]{:S(2)}) collective-permute-start(bf16[2,128,768]{2,1,0:T(8,128)(2,1)S(1)} %get-tuple-element.56.refs_3_), channel_id=1, source_target_pairs={{0,4},{4,0},{8,12},{12,8},{16,20},{20,16},{24,28},{28,24},{1,5},{5... | collective-permute-start | bytes 1179656 | tf_op jit(solution)/shard_map/ppermute | solution.py:28
  32.5 7.6 %collective-permute-start.7 = (bf16[1,128,768]{2,1,0:T(8,128)(2,1)S(1)}, bf16[1,128,768]{2,1,0:T(8,128)(2,1)S(1)}, u32[]{:S(2)}, u32[]{:S(2)}) collective-permute-start(bf16[1,128,768]{2,1,0:T(8,128)(2,1)S(1)} %shard_map.85.refs_2_), channel_id=1, source_target_pairs={{0,16},{4,12},{8,24},{12,4},{16,0},{20,28},{24,8},{28,20},{1,17},{... | collective-permute-start | bytes 589832 | tf_op jit(solution)/shard_map/ppermute | solution.py:38
  34.1 13.5 %collective-permute-start.12 = (bf16[2,128,768]{2,1,0:T(8,128)(2,1)S(1)}, bf16[2,128,768]{2,1,0:T(8,128)(2,1)S(1)}, u32[]{:S(2)}, u32[]{:S(2)}) collective-permute-start(bf16[2,128,768]{2,1,0:T(8,128)(2,1)S(1)} %shard_map.86.refs_2_), channel_id=1, source_target_pairs={{0,8},{4,20},{8,0},{12,28},{16,24},{20,4},{24,16},{28,12},{1,9},{5... | collective-permute-start | bytes 1179656 | tf_op jit(solution)/shard_map/ppermute | solution.py:38
  40.3 5.7 %collective-permute-start.9 = (bf16[128,768]{1,0:T(8,128)(2,1)S(1)}, bf16[128,768]{1,0:T(8,128)(2,1)S(1)}, u32[]{:S(2)}, u32[]{:S(2)}) collective-permute-start(bf16[128,768]{1,0:T(8,128)(2,1)S(1)} %get-tuple-element.59.refs_6_.refs_0_), channel_id=1, source_target_pairs={{0,8},{4,20},{8,0},{12,28},{16,24},{20,4},{24,16},{28,12},{1,9},{5... | collective-permute-start | bytes 589832 | tf_op jit(solution)/shard_map/ppermute | solution.py:38
  43.5 4.1 %collective-permute-start.11 = (bf16[1,128,768]{2,1,0:T(8,128)(2,1)S(1)}, bf16[1,128,768]{2,1,0:T(8,128)(2,1)S(1)}, u32[]{:S(2)}, u32[]{:S(2)}) collective-permute-start(bf16[1,128,768]{2,1,0:T(8,128)(2,1)S(1)} %get-tuple-element.61.refs_2_), channel_id=1, source_target_pairs={{0,4},{4,0},{8,12},{12,8},{16,20},{20,16},{24,28},{28,24},{1,5},{5... | collective-permute-start | bytes 589832 | tf_op jit(solution)/shard_map/ppermute | solution.py:28
  46.0 10.3 %collective-permute-start.10 = (bf16[256,768]{1,0:T(8,128)(2,1)S(1)}, bf16[256,768]{1,0:T(8,128)(2,1)S(1)}, u32[]{:S(2)}, u32[]{:S(2)}) collective-permute-start(bf16[256,768]{1,0:T(8,128)(2,1)S(1)} %shard_map.90.refs_3_.refs_0_), channel_id=1, source_target_pairs={{0,16},{4,12},{8,24},{12,4},{16,0},{20,28},{24,8},{28,20},{1,17},{... | collective-permute-start | bytes 1179656 | tf_op jit(solution)/shard_map/ppermute | solution.py:38
  47.7 8.3 %collective-permute-start.13 = (bf16[1,128,768]{2,1,0:T(8,128)(2,1)S(1)}, bf16[1,128,768]{2,1,0:T(8,128)(2,1)S(1)}, u32[]{:S(2)}, u32[]{:S(2)}) collective-permute-start(bf16[1,128,768]{2,1,0:T(8,128)(2,1)S(1)} %shard_map.91.refs_2_), channel_id=1, source_target_pairs={{0,16},{4,12},{8,24},{12,4},{16,0},{20,28},{24,8},{28,20},{1,17},{... | collective-permute-start | bytes 589832 | tf_op jit(solution)/shard_map/ppermute | solution.py:38
  52.3 3.7 %collective-permute-start.14 = (bf16[1,128,768]{2,1,0:T(8,128)(2,1)S(1)}, bf16[1,128,768]{2,1,0:T(8,128)(2,1)S(1)}, u32[]{:S(2)}, u32[]{:S(2)}) collective-permute-start(bf16[1,128,768]{2,1,0:T(8,128)(2,1)S(1)} %get-tuple-element.67.refs_2_), channel_id=1, source_target_pairs={{0,4},{4,0},{8,12},{12,8},{16,20},{20,16},{24,28},{28,24},{1,5},{5... | collective-permute-start | bytes 589832 | tf_op jit(solution)/shard_map/ppermute | solution.py:28
  56.4 7.7 %collective-permute-start.15 = (bf16[512,768]{1,0:T(8,128)(2,1)S(1)}, bf16[512,768]{1,0:T(8,128)(2,1)S(1)}, u32[]{:S(2)}, u32[]{:S(2)}) collective-permute-start(bf16[512,768]{1,0:T(8,128)(2,1)S(1)} %shard_map.96.refs_1_.refs_5_.refs_0_), channel_id=1, source_target_pairs={{0,4},{4,0},{8,12},{12,8},{16,20},{20,16},{24,28},{28,24},{1,5},{5... | collective-permute-start | bytes 2359304 | tf_op jit(solution)/shard_map/ppermute | solution.py:28
  56.5 5.8 %collective-permute-start.16 = (bf16[128,768]{1,0:T(8,128)(2,1)S(1)}, bf16[128,768]{1,0:T(8,128)(2,1)S(1)}, u32[]{:S(2)}, u32[]{:S(2)}) collective-permute-start(bf16[128,768]{1,0:T(8,128)(2,1)S(1)} %shard_map.95.refs_2_.refs_0_), channel_id=1, source_target_pairs={{0,8},{4,20},{8,0},{12,28},{16,24},{20,4},{24,16},{28,12},{1,9},{5... | collective-permute-start | bytes 589832 | tf_op jit(solution)/shard_map/ppermute | solution.py:38
  62.4 11.3 %collective-permute-start.19 = (bf16[256,768]{1,0:T(8,128)(2,1)S(1)}, bf16[256,768]{1,0:T(8,128)(2,1)S(1)}, u32[]{:S(2)}, u32[]{:S(2)}) collective-permute-start(bf16[256,768]{1,0:T(8,128)(2,1)S(1)} %shard_map.98.refs_10_.refs_0_), channel_id=1, source_target_pairs={{0,16},{4,12},{8,24},{12,4},{16,0},{20,28},{24,8},{28,20},{1,17},{... | collective-permute-start | bytes 1179656 | tf_op jit(solution)/shard_map/ppermute | solution.py:38
  67.0 6.7 %collective-permute-start.17 = (bf16[64,1536]{1,0:T(8,128)(2,1)S(1)}, bf16[64,1536]{1,0:T(8,128)(2,1)S(1)}, u32[]{:S(2)}, u32[]{:S(2)}) collective-permute-start(bf16[64,1536]{1,0:T(8,128)(2,1)S(1)} %get-tuple-element.69.refs_6_), channel_id=1, source_target_pairs={{0,1},{1,0},{2,3},{3,2},{4,5},{5,4},{6,7},{7,6},{8,9},{9,8},{10,11... | collective-permute-start | bytes 589832 | tf_op jit(solution)/shard_map/ppermute | solution.py:28
  73.8 2.4 %collective-permute-start.20 = (bf16[512,768]{1,0:T(8,128)(2,1)S(1)}, bf16[512,768]{1,0:T(8,128)(2,1)S(1)}, u32[]{:S(2)}, u32[]{:S(2)}) collective-permute-start(bf16[512,768]{1,0:T(8,128)(2,1)S(1)} %shard_map.102.refs_0_.refs_10_.refs_1_), channel_id=1, source_target_pairs={{0,4},{4,0},{8,12},{12,8},{16,20},{20,16},{24,28},{28,24},{1,5},{5... | collective-permute-start | bytes 2359304 | tf_op jit(solution)/shard_map/ppermute | solution.py:28
  73.9 12.8 %collective-permute-start.18 = (bf16[32,1536]{1,0:T(8,128)(2,1)S(1)}, bf16[32,1536]{1,0:T(8,128)(2,1)S(1)}, u32[]{:S(2)}, u32[]{:S(2)}) collective-permute-start(bf16[32,1536]{1,0:T(8,128)(2,1)S(1)} %get-tuple-element.71.refs_2_), channel_id=1, source_target_pairs={{0,2},{1,3},{2,0},{3,1},{4,6},{5,7},{6,4},{7,5},{8,10},{9,11},{10,... | collective-permute-start | bytes 294920 | tf_op jit(solution)/shard_map/ppermute | solution.py:28
  82.2 14.0 %collective-permute-start.22 = (bf16[32,1536]{1,0:T(8,128)(2,1)S(1)}, bf16[32,1536]{1,0:T(8,128)(2,1)S(1)}, u32[]{:S(2)}, u32[]{:S(2)}) collective-permute-start(bf16[32,1536]{1,0:T(8,128)(2,1)S(1)} %get-tuple-element.74), channel_id=1, source_target_pairs={{0,2},{1,3},{2,0},{3,1},{4,6},{5,7},{6,4},{7,5},{8,10},{9,11},{10,... | collective-permute-start | bytes 294920 | tf_op jit(solution)/shard_map/ppermute | solution.py:28
  84.0 12.2 %collective-permute-start.23 = (bf16[32,1536]{1,0:T(8,128)(2,1)S(1)}, bf16[32,1536]{1,0:T(8,128)(2,1)S(1)}, u32[]{:S(2)}, u32[]{:S(2)}) collective-permute-start(bf16[32,1536]{1,0:T(8,128)(2,1)S(1)} %get-tuple-element.75), channel_id=1, source_target_pairs={{0,1},{1,0},{2,3},{3,2},{4,5},{5,4},{6,7},{7,6},{8,9},{9,8},{10,11... | collective-permute-start | bytes 294920 | tf_op jit(solution)/shard_map/ppermute | solution.py:28
  84.3 11.9 %collective-permute-start.21 = (bf16[32,1536]{1,0:T(8,128)(2,1)S(1)}, bf16[32,1536]{1,0:T(8,128)(2,1)S(1)}, u32[]{:S(2)}, u32[]{:S(2)}) collective-permute-start(bf16[32,1536]{1,0:T(8,128)(2,1)S(1)} %get-tuple-element.72.refs_2_), channel_id=1, source_target_pairs={{0,3},{1,2},{2,1},{3,0},{4,7},{5,6},{6,5},{7,4},{8,11},{9,10},{10,... | collective-permute-start | bytes 294920 | tf_op jit(solution)/shard_map/ppermute | solution.py:28
  (2 other events, 6.8 us)

commit v2 on v1

--- a/solution.py
+++ b/solution.py
@@ -12,7 +12,7 @@
 VMEM_LIMIT = 10 * 1024 * 1024
 WRITES = 6
 READ_CUTS, WRITE_CUTS = 4, 3
-PART_COST = 10**9
+PART_COST = 6 * 10**9
 
 
 def gelu_fn(value):
@@ -106,14 +106,14 @@
             out[to : to + size, :] = piece[at : at + size, :]
 
 
-def joined(pieces, after=()):
+def joined(pieces, after=(), flops=0):
     rows = sum(piece.shape[0] for piece in pieces)
 
     def kernel(*refs):
         join(refs[: len(pieces)], refs[-1])
 
     return call(
-        kernel, in_vmem(pieces), [("vmem", ((rows, pieces[0].shape[1]), BF16))], 0, 0, after
+        kernel, in_vmem(pieces), [("vmem", ((rows, pieces[0].shape[1]), BF16))], flops, 0, after
     )[0]
 
 
@@ -315,8 +315,8 @@
         + in_vmem(pieces)
         + ([("hbm", into)] if into is not None else []),
         [("hbm", (weight.value.shape, BF16))],
-        2 * tokens * width * block * len(keys),
-        2 * width * block * len(keys),
+        2 * tokens * width * block * len(keys) if 1 in odds else 0,
+        2 * width * block * len(keys) if 1 in odds else 0,
         (),
         [
             pltpu.VMEM((tokens, width), BF16),
@@ -373,7 +373,7 @@
 
     shape = terms[0][0].shape[1:]
     outs = [("vmem", (shape, F32)), ("vmem", (shape, BF16))]
-    return call(kernel, in_vmem([array for array, block in terms]), outs, 0, 0)
+    return call(kernel, in_vmem([array for array, block in terms]), outs, PART_COST, 0)
 
 
 def activate_back(hidden, terms):
@@ -404,8 +404,8 @@
     def other_core(value):
         return swap(value, "row", 1, rows)
 
-    def doubled(stack, step):
-        return joined([stack, across(stack, step, rows)])
+    def doubled(stack, step, flops=0):
+        return joined([stack, across(stack, step, rows)], (), flops)
 
     wanted = [(w, key) for w in (w_in, w_out) for part in (first, second, own) for key in keys(part)]
 
@@ -429,28 +429,26 @@
     here, sent = project(w_in, token_shards, second + own, [])
     got_here, came = other_core(sent), across(added([keep, got]), 0, rows)
     load(wanted[5 * min(2, len(flips)) : 12])
-    keep, sent = project(w_out, cot_shards, first, [])
+    keep, sent = project(w_out, cot_shards, first, wanted[12:14])
     got = other_core(sent)
     sent = one_block([(here, 0), (got_here, 0), (came, 1)])
     terms = [(here, 1), (got_here, 1), (came, 0), (across(sent, 1, rows), 0)]
 
     came = across(added([keep, got]), 0, rows)
-    load(wanted[12:14])
+    keep, sent = project(w_out, cot_shards, second, wanted[14:])
+    got = other_core(sent)
     hidden, act = activate(terms)
-    keep, sent = project(w_out, cot_shards, second, [])
+    sent = one_block([(keep, 0), (got, 0), (came, 1)])
+    last = across(sent, 1, rows)
+    keep, sent = project(w_out, cot_shards, own, [])
     got = other_core(sent)
     stack = doubled(act, 0)
-    sent = one_block([(keep, 0), (got, 0), (came, 1)])
-    last = across(sent, 1, rows)
-    load(wanted[14:])
-    keep, sent = project(w_out, cot_shards, own, [])
-    got = other_core(sent)
     part = one_block([(came, 0), (last, 0)], F32, PART_COST)
     grad_hidden = activate_back(hidden, [(keep, 0), (part, 0), (got, 0)])
     stack = doubled(stack, 1)
     act = stack, other_core(stack)
     grad_w_out = weight_grad(w_out, act[:1], (0,), cot_shards)
-    back_stack = doubled(grad_hidden, 0)
+    back_stack = doubled(grad_hidden, 0, PART_COST)
 
     even, odd = range(0, cols, 2), range(1, cols, 2)
     keep, send = block_sum(w_out, act, (0, 1), cols, (even, odd))

time: 97 us -> 95.3 us (0.982)
  waiting for transfers between devices: 11.8 us -> 8.73 us
  starting transfers between devices: 29.9 us -> 31.8 us
    ppermute x16, waiting for transfers between devices: 3.27 us -> 1.41 us  [swap(): return lax.ppermute(value, axis, [(i, i ^ flip) for i in range(count)])]
    ppermute x16, starting transfers between devices: 18.1 us -> 19.9 us  [swap(): return lax.ppermute(value, axis, [(i, i ^ flip) for i in range(count)])]
    ppermute x8, waiting for transfers between devices: 8.54 us -> 7.32 us  [across(): return lax.ppermute(value, 'row', [(i, i ^ flips[i]) for i in range(rows)])]
    pallas_call x31 -> x29, Pallas kernels: 53.5 us -> 53 us  [call(): pl.pallas_call(body, in_specs=[specs[space] for space, value in arrays] +...]
  transfers between devices with their start and end apart: 24 -> 24, of which waited for: 7 -> 8; matrix products, arithmetic and copies ran while one was open for 0% -> 0% of each run, Pallas kernels for 54% -> 54%
where the time goes in v2:
time: 95.3 us; the launch traced here: 95.2 us
  Pallas kernels  53 us (56%)
  starting transfers between devices  31.8 us (33%)
  waiting for transfers between devices  8.73 us (9%)
    pallas_call x29, Pallas kernels, call(): pl.pallas_call(body, in_specs=[specs[space] for space, value in arrays] +...  53 us
    ppermute x16, starting transfers between devices, swap(): return lax.ppermute(value, axis, [(i, i ^ flip) for i in range(count)])  19.9 us
    ppermute x8, starting transfers between devices, across(): return lax.ppermute(value, 'row', [(i, i ^ flips[i]) for i in range(rows)])  11.9 us
    ppermute x8, waiting for transfers between devices, across(): return lax.ppermute(value, 'row', [(i, i ^ flips[i]) for i in range(rows)])  7.32 us
  transfers between devices with their start and end apart: 24, of which 8 were waited for; matrix products, arithmetic and copies ran while one was open for 0% of the time, Pallas kernels for 54%

profile of v2, /device:TPU:0, one launch (start us, length us, event | category | flops | bytes accessed | tf_op | source)
XLA Modules:
  0.0 95.2 jit_solution(5563061214750046124)
XLA Ops:
  0.6 4.1 %collective-permute-start = (bf16[32,1536]{1,0:T(8,128)(2,1)}, bf16[32,1536]{1,0:T(8,128)(2,1)S(1)}, u32[]{:S(2)}, u32[]{:S(2)}) collective-permute-start(bf16[32,1536]{1,0:T(8,128)(2,1)} %refs_3_.1), channel_id=1, source_target_pairs={{0,2},{1,3},{2,0},{3,1},{4,6},{5,7},{6,4},{7,5},{8,10},{9,11},{10,... | collective-permute-start | bytes 294920 | tf_op jit(solution)/shard_map/ppermute | solution.py:28
  4.7 4.6 %shard_map.75 = (bf16[1536,768]{1,0:T(8,128)(2,1)S(1)}, bf16[1536,768]{1,0:T(8,128)(2,1)S(1)}, bf16[1536,768]{1,0:T(8,128)(2,1)S(1)}, bf16[1536,768]{1,0:T(8,128)(2,1)S(1)}, bf16[1536,768]{1,0:T(8,128)(2,1)S(1)}) custom-call(s32[1]{0:T(128)} %bitcast.refs_0_, bf16[1536,6144]{1,0:T(8,128)(2,1)} %refs_1_.9), custom_call_target="tpu_custom_call" | custom-call | tf_op jit(solution)/shard_map/pallas_call | solution.py:69
  11.1 3.0 %collective-permute-start.2 = (bf16[32,1536]{1,0:T(8,128)(2,1)S(1)}, bf16[32,1536]{1,0:T(8,128)(2,1)S(1)}, u32[]{:S(2)}, u32[]{:S(2)}) collective-permute-start(bf16[32,1536]{1,0:T(8,128)(2,1)S(1)} %shard_map.77.refs_3_), channel_id=1, source_target_pairs={{0,2},{1,3},{2,0},{3,1},{4,6},{5,7},{6,4},{7,5},{8,10},{9,11},{10,... | collective-permute-start | bytes 294920 | tf_op jit(solution)/shard_map/ppermute | solution.py:28
  14.1 4.6 %shard_map.78 = (bf16[1536,768]{1,0:T(8,128)(2,1)S(1)}, bf16[1536,768]{1,0:T(8,128)(2,1)S(1)}, bf16[1536,768]{1,0:T(8,128)(2,1)S(1)}, bf16[768,1536]{1,0:T(8,128)(2,1)S(1)}, bf16[768,1536]{1,0:T(8,128)(2,1)S(1)}) custom-call(s32[1]{0:T(128)} %bitcast.refs_0_, bf16[1536,6144]{1,0:T(8,128)(2,1)} %refs_1_.9, bf16[6144,1536]{1,0:T(8,128)(2,1)} %refs_6_.1, ...), custom_call_target="tpu_custom_call" | custom-call | tf_op jit(solution)/shard_map/pallas_call | solution.py:69
  20.3 2.5 %collective-permute-start.6 = (bf16[64,1536]{1,0:T(8,128)(2,1)S(1)}, bf16[64,1536]{1,0:T(8,128)(2,1)S(1)}, u32[]{:S(2)}, u32[]{:S(2)}) collective-permute-start(bf16[64,1536]{1,0:T(8,128)(2,1)S(1)} %shard_map.79.refs_8_), channel_id=1, source_target_pairs={{0,1},{1,0},{2,3},{3,2},{4,5},{5,4},{6,7},{7,6},{8,9},{9,8},{10,11... | collective-permute-start | bytes 589832 | tf_op jit(solution)/shard_map/ppermute | solution.py:28
  24.5 1.6 %collective-permute-start.5 = (bf16[2,128,768]{2,1,0:T(8,128)(2,1)S(1)}, bf16[2,128,768]{2,1,0:T(8,128)(2,1)S(1)}, u32[]{:S(2)}, u32[]{:S(2)}) collective-permute-start(bf16[2,128,768]{2,1,0:T(8,128)(2,1)S(1)} %shard_map.82.refs_2_), channel_id=1, source_target_pairs={{0,8},{4,20},{8,0},{12,28},{16,24},{20,4},{24,16},{28,12},{1,9},{5... | collective-permute-start | bytes 1179656 | tf_op jit(solution)/shard_map/ppermute | solution.py:38
  26.1 2.4 %shard_map.83 = (bf16[768,1536]{1,0:T(8,128)(2,1)S(1)}, bf16[768,1536]{1,0:T(8,128)(2,1)S(1)}) custom-call(s32[1]{0:T(128)} %bitcast.refs_0_, bf16[6144,1536]{1,0:T(8,128)(2,1)} %refs_6_.1, bf16[2,128,768]{2,1,0:T(8,128)(2,1)S(1)} %shard_map.82.refs_2_), custom_call_target="tpu_custom_call" | custom-call | tf_op jit(solution)/shard_map/pallas_call | solution.py:69
  28.5 5.2 %shard_map.84 = (bf16[2,128,768]{2,1,0:T(8,128)(2,1)S(1)}, bf16[2,128,768]{2,1,0:T(8,128)(2,1)S(1)}, bf16[768,1536]{1,0:T(8,128)(2,1)S(1)}, bf16[768,1536]{1,0:T(8,128)(2,1)S(1)}) custom-call(s32[1]{0:T(128)} %bitcast.refs_0_, bf16[32,1536]{1,0:T(8,128)(2,1)S(1)} %copy-done, bf16[32,1536]{1,0:T(8,128)(2,1)S(1)} %collective-permute-done.2.refs_1_.refs_2_.refs_3_, ...), custom_call_target="tpu_custom_call" | custom-call | tf_op jit(solution)/shard_map/pallas_call | solution.py:69
  33.9 1.5 %collective-permute-start.7 = (bf16[1,128,768]{2,1,0:T(8,128)(2,1)S(1)}, bf16[1,128,768]{2,1,0:T(8,128)(2,1)S(1)}, u32[]{:S(2)}, u32[]{:S(2)}) collective-permute-start(bf16[1,128,768]{2,1,0:T(8,128)(2,1)S(1)} %shard_map.85.refs_2_), channel_id=1, source_target_pairs={{0,16},{4,12},{8,24},{12,4},{16,0},{20,28},{24,8},{28,20},{1,17},{... | collective-permute-start | bytes 589832 | tf_op jit(solution)/shard_map/ppermute | solution.py:38
  36.9 3.8 %shard_map.87 = (bf16[1,128,768]{2,1,0:T(8,128)(2,1)S(1)}, bf16[1,128,768]{2,1,0:T(8,128)(2,1)S(1)}, bf16[768,1536]{1,0:T(8,128)(2,1)S(1)}, bf16[768,1536]{1,0:T(8,128)(2,1)S(1)}) custom-call(s32[1]{0:T(128)} %bitcast.refs_0_, bf16[32,1536]{1,0:T(8,128)(2,1)S(1)} %copy-done, bf16[32,1536]{1,0:T(8,128)(2,1)S(1)} %collective-permute-done.2.refs_1_.refs_2_.refs_3_, ...), custom_call_target="tpu_custom_call" | custom-call | tf_op jit(solution)/shard_map/pallas_call | solution.py:69
  41.2 1.6 %collective-permute-start.9 = (bf16[128,768]{1,0:T(8,128)(2,1)S(1)}, bf16[128,768]{1,0:T(8,128)(2,1)S(1)}, u32[]{:S(2)}, u32[]{:S(2)}) collective-permute-start(bf16[128,768]{1,0:T(8,128)(2,1)S(1)} %get-tuple-element.61.refs_3_.refs_0_), channel_id=1, source_target_pairs={{0,8},{4,20},{8,0},{12,28},{16,24},{20,4},{24,16},{28,12},{1,9},{5... | collective-permute-start | bytes 589832 | tf_op jit(solution)/shard_map/ppermute | solution.py:38
  43.5 1.6 %collective-permute-start.13 = (bf16[1,128,768]{2,1,0:T(8,128)(2,1)S(1)}, bf16[1,128,768]{2,1,0:T(8,128)(2,1)S(1)}, u32[]{:S(2)}, u32[]{:S(2)}) collective-permute-start(bf16[1,128,768]{2,1,0:T(8,128)(2,1)S(1)} %shard_map.89.refs_6_), channel_id=1, source_target_pairs={{0,16},{4,12},{8,24},{12,4},{16,0},{20,28},{24,8},{28,20},{1,17},{... | collective-permute-start | bytes 589832 | tf_op jit(solution)/shard_map/ppermute | solution.py:38
  45.1 1.6 %shard_map.90 = (bf16[1,128,768]{2,1,0:T(8,128)(2,1)S(1)}, bf16[1,128,768]{2,1,0:T(8,128)(2,1)S(1)}) custom-call(s32[1]{0:T(128)} %bitcast.refs_0_, bf16[32,1536]{1,0:T(8,128)(2,1)S(1)} %copy-done, bf16[32,1536]{1,0:T(8,128)(2,1)S(1)} %collective-permute-done.2.refs_1_.refs_2_.refs_3_, bf16[64,1536]{1,0:T(8,128)(2,1)S(1)} %collective-permute-done.6.refs_3_.refs_4_, ...), custom_call_target="tpu_custom_call" | custom-call | tf_op jit(solution)/shard_map/pallas_call | solution.py:69
  49.6 5.6 %collective-permute-done.12.refs_1_ = bf16[256,768]{1,0:T(8,128)(2,1)S(1)} collective-permute-done((bf16[256,768]{1,0:T(8,128)(2,1)S(1)}, bf16[256,768]{1,0:T(8,128)(2,1)S(1)}, u32[]{:S(2)}, u32[]{:S(2)}) %collective-permute-start.12) | collective-permute-done | bytes 393248 | tf_op jit(solution)/shard_map/ppermute | solution.py:38
  55.4 1.7 %collective-permute-start.16 = (bf16[128,768]{1,0:T(8,128)(2,1)S(1)}, bf16[128,768]{1,0:T(8,128)(2,1)S(1)}, u32[]{:S(2)}, u32[]{:S(2)}) collective-permute-start(bf16[128,768]{1,0:T(8,128)(2,1)S(1)} %shard_map.93.refs_2_.refs_0_), channel_id=1, source_target_pairs={{0,8},{4,20},{8,0},{12,28},{16,24},{20,4},{24,16},{28,12},{1,9},{5... | collective-permute-start | bytes 589832 | tf_op jit(solution)/shard_map/ppermute | solution.py:38
  57.0 4.2 %shard_map.95.refs_2_.refs_5_ = bf16[6144,1536]{1,0:T(8,128)(2,1)} custom-call(s32[1]{0:T(128)} %bitcast.refs_0_, bf16[512,768]{1,0:T(8,128)(2,1)S(1)} %shard_map.94.refs_1_.refs_5_.refs_0_, bf16[32,1536]{1,0:T(8,128)(2,1)S(1)} %copy-done, bf16[32,1536]{1,0:T(8,128)(2,1)S(1)} %collective-permute-done.2.refs_1_.refs_2_.refs_3_, ...), custom_call_target="tpu_custom_call" | custom-call | tf_op jit(solution)/shard_map/pallas_call | solution.py:69
  62.5 2.8 %shard_map.97 = (bf16[64,1536]{1,0:T(8,128)(2,1)S(1)}, bf16[64,1536]{1,0:T(8,128)(2,1)S(1)}) custom-call(bf16[512,768]{1,0:T(8,128)(2,1)S(1)} %shard_map.94.refs_1_.refs_5_.refs_0_, bf16[512,768]{1,0:T(8,128)(2,1)S(1)} %collective-permute-done.15.refs_1_, bf16[768,1536]{1,0:T(8,128)(2,1)S(1)} %get-tuple-element.60.refs_4_.refs_5_.refs_2_, ...), custom_call_target="tpu_custom_call" | custom-call | flops 2415919104 | bytes 18874368 | tf_op jit(solution)/shard_map/pallas_call | solution.py:69
  65.4 2.0 %collective-permute-start.17 = (bf16[64,1536]{1,0:T(8,128)(2,1)S(1)}, bf16[64,1536]{1,0:T(8,128)(2,1)S(1)}, u32[]{:S(2)}, u32[]{:S(2)}) collective-permute-start(bf16[64,1536]{1,0:T(8,128)(2,1)S(1)} %get-tuple-element.69.refs_6_), channel_id=1, source_target_pairs={{0,1},{1,0},{2,3},{3,2},{4,5},{5,4},{6,7},{7,6},{8,9},{9,8},{10,11... | collective-permute-start | bytes 589832 | tf_op jit(solution)/shard_map/ppermute | solution.py:28
  67.3 4.2 %shard_map.98.refs_2_ = bf16[6144,1536]{1,0:T(8,128)(2,1)} custom-call(s32[1]{0:T(128)} %bitcast.refs_0_, bf16[512,768]{1,0:T(8,128)(2,1)S(1)} %collective-permute-done.15.refs_1_, bf16[32,1536]{1,0:T(8,128)(2,1)S(1)} %copy-done, bf16[32,1536]{1,0:T(8,128)(2,1)S(1)} %collective-permute-done.2.refs_1_.refs_2_.refs_3_, ...), custom_call_target="tpu_custom_call", output_to_operand_aliasing={{}: (5, {})} | custom-call | flops 1207959552 | bytes 9437184 | tf_op jit(solution)/shard_map/pallas_call | solution.py:69
  72.2 1.8 %collective-permute-start.18 = (bf16[32,1536]{1,0:T(8,128)(2,1)S(1)}, bf16[32,1536]{1,0:T(8,128)(2,1)S(1)}, u32[]{:S(2)}, u32[]{:S(2)}) collective-permute-start(bf16[32,1536]{1,0:T(8,128)(2,1)S(1)} %get-tuple-element.71.refs_2_), channel_id=1, source_target_pairs={{0,2},{1,3},{2,0},{3,1},{4,6},{5,7},{6,4},{7,5},{8,10},{9,11},{10,... | collective-permute-start | bytes 294920 | tf_op jit(solution)/shard_map/ppermute | solution.py:28
  74.4 6.0 %shard_map.101 = (bf16[32,1536]{1,0:T(8,128)(2,1)S(1)}, bf16[32,1536]{1,0:T(8,128)(2,1)S(1)}, bf16[32,1536]{1,0:T(8,128)(2,1)S(1)}, bf16[32,1536]{1,0:T(8,128)(2,1)S(1)}) custom-call(bf16[512,768]{1,0:T(8,128)(2,1)S(1)} %shard_map.100.refs_0_.refs_10_.refs_1_, bf16[512,768]{1,0:T(8,128)(2,1)S(1)} %collective-permute-done.20.refs_1_.refs_2_, ...), custom_call_target="tpu_custom_call" | custom-call | flops 2415919104 | bytes 18874368 | tf_op jit(solution)/shard_map/pallas_call | solution.py:69
  80.5 1.8 %collective-permute-start.22 = (bf16[32,1536]{1,0:T(8,128)(2,1)S(1)}, bf16[32,1536]{1,0:T(8,128)(2,1)S(1)}, u32[]{:S(2)}, u32[]{:S(2)}) collective-permute-start(bf16[32,1536]{1,0:T(8,128)(2,1)S(1)} %get-tuple-element.74), channel_id=1, source_target_pairs={{0,2},{1,3},{2,0},{3,1},{4,6},{5,7},{6,4},{7,5},{8,10},{9,11},{10,... | collective-permute-start | bytes 294920 | tf_op jit(solution)/shard_map/ppermute | solution.py:28
  82.3 1.7 %collective-permute-start.23 = (bf16[32,1536]{1,0:T(8,128)(2,1)S(1)}, bf16[32,1536]{1,0:T(8,128)(2,1)S(1)}, u32[]{:S(2)}, u32[]{:S(2)}) collective-permute-start(bf16[32,1536]{1,0:T(8,128)(2,1)S(1)} %get-tuple-element.75), channel_id=1, source_target_pairs={{0,1},{1,0},{2,3},{3,2},{4,5},{5,4},{6,7},{7,6},{8,9},{9,8},{10,11... | collective-permute-start | bytes 294920 | tf_op jit(solution)/shard_map/ppermute | solution.py:28
  85.6 8.8 %shard_map.103 = bf16[1536,6144]{1,0:T(8,128)(2,1)} custom-call(s32[1]{0:T(128)} %bitcast.refs_0_, bf16[512,768]{1,0:T(8,128)(2,1)S(1)} %shard_map.100.refs_0_.refs_10_.refs_1_, bf16[512,768]{1,0:T(8,128)(2,1)S(1)} %collective-permute-done.20.refs_1_.refs_2_, bf16[32,1536]{1,0:T(8,128)(2,1)S(1)} %copy-done.1, ...), custom_call_target="tpu_custom_call" | custom-call | flops 2415919104 | bytes 18874368 | tf_op jit(solution)/shard_map/pallas_call | solution.py:69
  (58 shorter events, 15.3 us)
Async XLA Ops:
  0.6 9.2 %collective-permute-start = (bf16[32,1536]{1,0:T(8,128)(2,1)}, bf16[32,1536]{1,0:T(8,128)(2,1)S(1)}, u32[]{:S(2)}, u32[]{:S(2)}) collective-permute-start(bf16[32,1536]{1,0:T(8,128)(2,1)} %refs_3_.1), channel_id=1, source_target_pairs={{0,2},{1,3},{2,0},{3,1},{4,6},{5,7},{6,4},{7,5},{8,10},{9,11},{10,... | collective-permute-start | bytes 294920 | tf_op jit(solution)/shard_map/ppermute | solution.py:28
  9.9 8.9 %collective-permute-start.1 = (bf16[64,1536]{1,0:T(8,128)(2,1)S(1)}, bf16[64,1536]{1,0:T(8,128)(2,1)S(1)}, u32[]{:S(2)}, u32[]{:S(2)}) collective-permute-start(bf16[64,1536]{1,0:T(8,128)(2,1)S(1)} %shard_map.76.refs_1_), channel_id=1, source_target_pairs={{0,1},{1,0},{2,3},{3,2},{4,5},{5,4},{6,7},{7,6},{8,9},{9,8},{10,11... | collective-permute-start | bytes 589832 | tf_op jit(solution)/shard_map/ppermute | solution.py:28
  11.1 7.7 %collective-permute-start.2 = (bf16[32,1536]{1,0:T(8,128)(2,1)S(1)}, bf16[32,1536]{1,0:T(8,128)(2,1)S(1)}, u32[]{:S(2)}, u32[]{:S(2)}) collective-permute-start(bf16[32,1536]{1,0:T(8,128)(2,1)S(1)} %shard_map.77.refs_3_), channel_id=1, source_target_pairs={{0,2},{1,3},{2,0},{3,1},{4,6},{5,7},{6,4},{7,5},{8,10},{9,11},{10,... | collective-permute-start | bytes 294920 | tf_op jit(solution)/shard_map/ppermute | solution.py:28
  20.2 4.2 %collective-permute-start.4 = (bf16[2,128,768]{2,1,0:T(8,128)(2,1)S(1)}, bf16[2,128,768]{2,1,0:T(8,128)(2,1)S(1)}, u32[]{:S(2)}, u32[]{:S(2)}) collective-permute-start(bf16[2,128,768]{2,1,0:T(8,128)(2,1)S(1)} %get-tuple-element.49.refs_8_), channel_id=1, source_target_pairs={{0,4},{4,0},{8,12},{12,8},{16,20},{20,16},{24,28},{28,24},{1,5},{5... | collective-permute-start | bytes 1179656 | tf_op jit(solution)/shard_map/ppermute | solution.py:28
  20.3 8.2 %collective-permute-start.6 = (bf16[64,1536]{1,0:T(8,128)(2,1)S(1)}, bf16[64,1536]{1,0:T(8,128)(2,1)S(1)}, u32[]{:S(2)}, u32[]{:S(2)}) collective-permute-start(bf16[64,1536]{1,0:T(8,128)(2,1)S(1)} %shard_map.79.refs_8_), channel_id=1, source_target_pairs={{0,1},{1,0},{2,3},{3,2},{4,5},{5,4},{6,7},{7,6},{8,9},{9,8},{10,11... | collective-permute-start | bytes 589832 | tf_op jit(solution)/shard_map/ppermute | solution.py:28
  24.2 9.6 %collective-permute-start.3 = (bf16[2,128,768]{2,1,0:T(8,128)(2,1)S(1)}, bf16[2,128,768]{2,1,0:T(8,128)(2,1)S(1)}, u32[]{:S(2)}, u32[]{:S(2)}) collective-permute-start(bf16[2,128,768]{2,1,0:T(8,128)(2,1)S(1)} %get-tuple-element.51.refs_2_), channel_id=1, source_target_pairs={{0,4},{4,0},{8,12},{12,8},{16,20},{20,16},{24,28},{28,24},{1,5},{5... | collective-permute-start | bytes 1179656 | tf_op jit(solution)/shard_map/ppermute | solution.py:28
  24.5 9.3 %collective-permute-start.5 = (bf16[2,128,768]{2,1,0:T(8,128)(2,1)S(1)}, bf16[2,128,768]{2,1,0:T(8,128)(2,1)S(1)}, u32[]{:S(2)}, u32[]{:S(2)}) collective-permute-start(bf16[2,128,768]{2,1,0:T(8,128)(2,1)S(1)} %shard_map.82.refs_2_), channel_id=1, source_target_pairs={{0,8},{4,20},{8,0},{12,28},{16,24},{20,4},{24,16},{28,12},{1,9},{5... | collective-permute-start | bytes 1179656 | tf_op jit(solution)/shard_map/ppermute | solution.py:38
  33.7 1.8 %collective-permute-start.8 = (bf16[2,128,768]{2,1,0:T(8,128)(2,1)S(1)}, bf16[2,128,768]{2,1,0:T(8,128)(2,1)S(1)}, u32[]{:S(2)}, u32[]{:S(2)}) collective-permute-start(bf16[2,128,768]{2,1,0:T(8,128)(2,1)S(1)} %get-tuple-element.59), channel_id=1, source_target_pairs={{0,4},{4,0},{8,12},{12,8},{16,20},{20,16},{24,28},{28,24},{1,5},{5... | collective-permute-start | bytes 1179656 | tf_op jit(solution)/shard_map/ppermute | solution.py:28
  33.9 7.1 %collective-permute-start.7 = (bf16[1,128,768]{2,1,0:T(8,128)(2,1)S(1)}, bf16[1,128,768]{2,1,0:T(8,128)(2,1)S(1)}, u32[]{:S(2)}, u32[]{:S(2)}) collective-permute-start(bf16[1,128,768]{2,1,0:T(8,128)(2,1)S(1)} %shard_map.85.refs_2_), channel_id=1, source_target_pairs={{0,16},{4,12},{8,24},{12,4},{16,0},{20,28},{24,8},{28,20},{1,17},{... | collective-permute-start | bytes 589832 | tf_op jit(solution)/shard_map/ppermute | solution.py:38
  35.6 7.8 %collective-permute-start.11 = (bf16[2,128,768]{2,1,0:T(8,128)(2,1)S(1)}, bf16[2,128,768]{2,1,0:T(8,128)(2,1)S(1)}, u32[]{:S(2)}, u32[]{:S(2)}) collective-permute-start(bf16[2,128,768]{2,1,0:T(8,128)(2,1)S(1)} %shard_map.86.refs_7_), channel_id=1, source_target_pairs={{0,8},{4,20},{8,0},{12,28},{16,24},{20,4},{24,16},{28,12},{1,9},{5... | collective-permute-start | bytes 1179656 | tf_op jit(solution)/shard_map/ppermute | solution.py:38
  40.7 2.1 %collective-permute-start.10 = (bf16[1,128,768]{2,1,0:T(8,128)(2,1)S(1)}, bf16[1,128,768]{2,1,0:T(8,128)(2,1)S(1)}, u32[]{:S(2)}, u32[]{:S(2)}) collective-permute-start(bf16[1,128,768]{2,1,0:T(8,128)(2,1)S(1)} %get-tuple-element.64), channel_id=1, source_target_pairs={{0,4},{4,0},{8,12},{12,8},{16,20},{20,16},{24,28},{28,24},{1,5},{5... | collective-permute-start | bytes 589832 | tf_op jit(solution)/shard_map/ppermute | solution.py:28
  41.2 6.2 %collective-permute-start.9 = (bf16[128,768]{1,0:T(8,128)(2,1)S(1)}, bf16[128,768]{1,0:T(8,128)(2,1)S(1)}, u32[]{:S(2)}, u32[]{:S(2)}) collective-permute-start(bf16[128,768]{1,0:T(8,128)(2,1)S(1)} %get-tuple-element.61.refs_3_.refs_0_), channel_id=1, source_target_pairs={{0,8},{4,20},{8,0},{12,28},{16,24},{20,4},{24,16},{28,12},{1,9},{5... | collective-permute-start | bytes 589832 | tf_op jit(solution)/shard_map/ppermute | solution.py:38
  43.5 5.7 %collective-permute-start.13 = (bf16[1,128,768]{2,1,0:T(8,128)(2,1)S(1)}, bf16[1,128,768]{2,1,0:T(8,128)(2,1)S(1)}, u32[]{:S(2)}, u32[]{:S(2)}) collective-permute-start(bf16[1,128,768]{2,1,0:T(8,128)(2,1)S(1)} %shard_map.89.refs_6_), channel_id=1, source_target_pairs={{0,16},{4,12},{8,24},{12,4},{16,0},{20,28},{24,8},{28,20},{1,17},{... | collective-permute-start | bytes 589832 | tf_op jit(solution)/shard_map/ppermute | solution.py:38
  46.7 2.5 %collective-permute-start.14 = (bf16[1,128,768]{2,1,0:T(8,128)(2,1)S(1)}, bf16[1,128,768]{2,1,0:T(8,128)(2,1)S(1)}, u32[]{:S(2)}, u32[]{:S(2)}) collective-permute-start(bf16[1,128,768]{2,1,0:T(8,128)(2,1)S(1)} %get-tuple-element.65.refs_2_), channel_id=1, source_target_pairs={{0,4},{4,0},{8,12},{12,8},{16,20},{20,16},{24,28},{28,24},{1,5},{5... | collective-permute-start | bytes 589832 | tf_op jit(solution)/shard_map/ppermute | solution.py:28
  47.4 7.8 %collective-permute-start.12 = (bf16[256,768]{1,0:T(8,128)(2,1)S(1)}, bf16[256,768]{1,0:T(8,128)(2,1)S(1)}, u32[]{:S(2)}, u32[]{:S(2)}) collective-permute-start(bf16[256,768]{1,0:T(8,128)(2,1)S(1)} %shard_map.91.refs_2_.refs_0_), channel_id=1, source_target_pairs={{0,16},{4,12},{8,24},{12,4},{16,0},{20,28},{24,8},{28,20},{1,17},{... | collective-permute-start | bytes 1179656 | tf_op jit(solution)/shard_map/ppermute | solution.py:38
  55.3 7.2 %collective-permute-start.15 = (bf16[512,768]{1,0:T(8,128)(2,1)S(1)}, bf16[512,768]{1,0:T(8,128)(2,1)S(1)}, u32[]{:S(2)}, u32[]{:S(2)}) collective-permute-start(bf16[512,768]{1,0:T(8,128)(2,1)S(1)} %shard_map.94.refs_1_.refs_5_.refs_0_), channel_id=1, source_target_pairs={{0,4},{4,0},{8,12},{12,8},{16,20},{20,16},{24,28},{28,24},{1,5},{5... | collective-permute-start | bytes 2359304 | tf_op jit(solution)/shard_map/ppermute | solution.py:28
  55.4 5.9 %collective-permute-start.16 = (bf16[128,768]{1,0:T(8,128)(2,1)S(1)}, bf16[128,768]{1,0:T(8,128)(2,1)S(1)}, u32[]{:S(2)}, u32[]{:S(2)}) collective-permute-start(bf16[128,768]{1,0:T(8,128)(2,1)S(1)} %shard_map.93.refs_2_.refs_0_), channel_id=1, source_target_pairs={{0,8},{4,20},{8,0},{12,28},{16,24},{20,4},{24,16},{28,12},{1,9},{5... | collective-permute-start | bytes 589832 | tf_op jit(solution)/shard_map/ppermute | solution.py:38
  61.3 10.7 %collective-permute-start.19 = (bf16[256,768]{1,0:T(8,128)(2,1)S(1)}, bf16[256,768]{1,0:T(8,128)(2,1)S(1)}, u32[]{:S(2)}, u32[]{:S(2)}) collective-permute-start(bf16[256,768]{1,0:T(8,128)(2,1)S(1)} %shard_map.96.refs_10_.refs_0_), channel_id=1, source_target_pairs={{0,16},{4,12},{8,24},{12,4},{16,0},{20,28},{24,8},{28,20},{1,17},{... | collective-permute-start | bytes 1179656 | tf_op jit(solution)/shard_map/ppermute | solution.py:38
  65.4 6.6 %collective-permute-start.17 = (bf16[64,1536]{1,0:T(8,128)(2,1)S(1)}, bf16[64,1536]{1,0:T(8,128)(2,1)S(1)}, u32[]{:S(2)}, u32[]{:S(2)}) collective-permute-start(bf16[64,1536]{1,0:T(8,128)(2,1)S(1)} %get-tuple-element.69.refs_6_), channel_id=1, source_target_pairs={{0,1},{1,0},{2,3},{3,2},{4,5},{5,4},{6,7},{7,6},{8,9},{9,8},{10,11... | collective-permute-start | bytes 589832 | tf_op jit(solution)/shard_map/ppermute | solution.py:28
  72.1 2.4 %collective-permute-start.20 = (bf16[512,768]{1,0:T(8,128)(2,1)S(1)}, bf16[512,768]{1,0:T(8,128)(2,1)S(1)}, u32[]{:S(2)}, u32[]{:S(2)}) collective-permute-start(bf16[512,768]{1,0:T(8,128)(2,1)S(1)} %shard_map.100.refs_0_.refs_10_.refs_1_), channel_id=1, source_target_pairs={{0,4},{4,0},{8,12},{12,8},{16,20},{20,16},{24,28},{28,24},{1,5},{5... | collective-permute-start | bytes 2359304 | tf_op jit(solution)/shard_map/ppermute | solution.py:28
  72.2 12.8 %collective-permute-start.18 = (bf16[32,1536]{1,0:T(8,128)(2,1)S(1)}, bf16[32,1536]{1,0:T(8,128)(2,1)S(1)}, u32[]{:S(2)}, u32[]{:S(2)}) collective-permute-start(bf16[32,1536]{1,0:T(8,128)(2,1)S(1)} %get-tuple-element.71.refs_2_), channel_id=1, source_target_pairs={{0,2},{1,3},{2,0},{3,1},{4,6},{5,7},{6,4},{7,5},{8,10},{9,11},{10,... | collective-permute-start | bytes 294920 | tf_op jit(solution)/shard_map/ppermute | solution.py:28
  80.5 14.0 %collective-permute-start.22 = (bf16[32,1536]{1,0:T(8,128)(2,1)S(1)}, bf16[32,1536]{1,0:T(8,128)(2,1)S(1)}, u32[]{:S(2)}, u32[]{:S(2)}) collective-permute-start(bf16[32,1536]{1,0:T(8,128)(2,1)S(1)} %get-tuple-element.74), channel_id=1, source_target_pairs={{0,2},{1,3},{2,0},{3,1},{4,6},{5,7},{6,4},{7,5},{8,10},{9,11},{10,... | collective-permute-start | bytes 294920 | tf_op jit(solution)/shard_map/ppermute | solution.py:28
  82.3 12.2 %collective-permute-start.23 = (bf16[32,1536]{1,0:T(8,128)(2,1)S(1)}, bf16[32,1536]{1,0:T(8,128)(2,1)S(1)}, u32[]{:S(2)}, u32[]{:S(2)}) collective-permute-start(bf16[32,1536]{1,0:T(8,128)(2,1)S(1)} %get-tuple-element.75), channel_id=1, source_target_pairs={{0,1},{1,0},{2,3},{3,2},{4,5},{5,4},{6,7},{7,6},{8,9},{9,8},{10,11... | collective-permute-start | bytes 294920 | tf_op jit(solution)/shard_map/ppermute | solution.py:28
  84.0 10.4 %collective-permute-start.21 = (bf16[32,1536]{1,0:T(8,128)(2,1)S(1)}, bf16[32,1536]{1,0:T(8,128)(2,1)S(1)}, u32[]{:S(2)}, u32[]{:S(2)}) collective-permute-start(bf16[32,1536]{1,0:T(8,128)(2,1)S(1)} %get-tuple-element.72.refs_2_), channel_id=1, source_target_pairs={{0,3},{1,2},{2,1},{3,0},{4,7},{5,6},{6,5},{7,4},{8,11},{9,10},{10,... | collective-permute-start | bytes 294920 | tf_op jit(solution)/shard_map/ppermute | solution.py:28
  (2 other events, 6.8 us)

commit v3 on v2

--- a/solution.py
+++ b/solution.py
@@ -198,10 +198,14 @@
             copies = coming.copies(sources, refs[: len(blocks)], refs[-1], me_ref[0])
         for copy in copies:
             copy.start()
-        place(piece_refs, order, left)
-        for i, part in enumerate(parts):
-            out = dot(left[...], part[...], 1, 1 if by_rows else 0).astype(BF16)
-            (send if i < n else keep)[i % n] = out
+
+        @pl.when(me_ref[0] >= 0)
+        def _():
+            place(piece_refs, order, left)
+            for i, part in enumerate(parts):
+                out = dot(left[...], part[...], 1, 1 if by_rows else 0).astype(BF16)
+                (send if i < n else keep)[i % n] = out
+
         for copy in copies:
             copy.wait()
 
@@ -294,14 +298,18 @@
             if step >= WRITES:
                 for write in writes(step - WRITES):
                     write.wait()
-            i, p, key = keys[step // halves]
-            stack, of = stack_refs[i], slice(p * tokens, (p + 1) * tokens)
-            at = slice(step % halves * size, (step % halves + 1) * size)
-            if by_rows:
-                out = dot(stack[of, at], other[...], 0, 0)
-            else:
-                out = dot(turned[at, :], stack[of, :], 1, 0)
-            ready[step % WRITES] = out.astype(BF16)
+
+            @pl.when(me >= 0)
+            def _():
+                i, p, key = keys[step // halves]
+                stack, of = stack_refs[i], slice(p * tokens, (p + 1) * tokens)
+                at = slice(step % halves * size, (step % halves + 1) * size)
+                if by_rows:
+                    out = dot(stack[of, at], other[...], 0, 0)
+                else:
+                    out = dot(turned[at, :], stack[of, :], 1, 0)
+                ready[step % WRITES] = out.astype(BF16)
+
             for write in writes(step):
                 write.start()
         for step in range(max(0, steps - WRITES), steps):
@@ -418,17 +426,17 @@
             sent = joined(cot_pieces, (token_pieces[hop],))
             cot_pieces.append(swap(sent, "col", flips[hop - 1], cols))
         if hop < 2:
-            load(wanted[5 * hop : 5 * hop + 5])
+            load(wanted[5 * hop : 5 + 3 * hop])
         order += [q ^ flip for q in order]
     sent = joined(cot_pieces, (token_pieces[-1],))
     cot_pieces.append(swap(sent, "col", flips[-1], cols))
     token_shards, cot_shards = (token_pieces, order), (cot_pieces, order)
 
-    keep, sent = project(w_in, token_shards, first, [])
+    keep, sent = project(w_in, token_shards, first, wanted[8:10])
     got = other_core(sent)
     here, sent = project(w_in, token_shards, second + own, [])
     got_here, came = other_core(sent), across(added([keep, got]), 0, rows)
-    load(wanted[5 * min(2, len(flips)) : 12])
+    load(wanted[10:12])
     keep, sent = project(w_out, cot_shards, first, wanted[12:14])
     got = other_core(sent)
     sent = one_block([(here, 0), (got_here, 0), (came, 1)])
@@ -489,7 +497,7 @@
 
     def shards(tokens, cotangent, w_in, w_out):
         powers = rows & (rows - 1) == 0 and cols & (cols - 1) == 0
-        if powers and rows == 8 and cols > 1 and w_in.shape[1] % (rows * 128) == 0:
+        if powers and rows == 8 and cols > 2 and w_in.shape[1] % (rows * 128) == 0:
             return blocked(rows, cols, tokens, cotangent, w_in, w_out)
         return collective(tokens, cotangent, w_in, w_out)
 

time: 95.3 us -> 97.2 us (1.020)
  waiting for transfers between devices: 8.73 us -> 13.3 us
  Pallas kernels: 53 us -> 50.6 us
    ppermute x8, waiting for transfers between devices: 7.32 us -> 9.89 us  [across(): return lax.ppermute(value, 'row', [(i, i ^ flips[i]) for i in range(rows)])]
    pallas_call x29, Pallas kernels: 53 us -> 50.6 us  [call(): pl.pallas_call(body, in_specs=[specs[space] for space, value in arrays] +...]
    ppermute x16, waiting for transfers between devices: 1.41 us -> 3.42 us  [swap(): return lax.ppermute(value, axis, [(i, i ^ flip) for i in range(count)])]
    ppermute x16, starting transfers between devices: 19.9 us -> 18.5 us  [swap(): return lax.ppermute(value, axis, [(i, i ^ flip) for i in range(count)])]
    ppermute x8, starting transfers between devices: 11.9 us -> 13 us  [across(): return lax.ppermute(value, 'row', [(i, i ^ flips[i]) for i in range(rows)])]
  transfers between devices with their start and end apart: 24 -> 24, of which waited for: 8 -> 9; matrix products, arithmetic and copies ran while one was open for 0% -> 0% of each run, Pallas kernels for 54% -> 50%
where the time goes in v3:
time: 97.2 us; the launch traced here: 97 us
  Pallas kernels  50.6 us (52%)
  starting transfers between devices  31.5 us (32%)
  waiting for transfers between devices  13.3 us (14%)
    pallas_call x29, Pallas kernels, call(): pl.pallas_call(body, in_specs=[specs[space] for space, value in arrays] +...  50.6 us
    ppermute x16, starting transfers between devices, swap(): return lax.ppermute(value, axis, [(i, i ^ flip) for i in range(count)])  18.5 us
    ppermute x8, starting transfers between devices, across(): return lax.ppermute(value, 'row', [(i, i ^ flips[i]) for i in range(rows)])  13 us
    ppermute x8, waiting for transfers between devices, across(): return lax.ppermute(value, 'row', [(i, i ^ flips[i]) for i in range(rows)])  9.89 us
    ppermute x16, waiting for transfers between devices, swap(): return lax.ppermute(value, axis, [(i, i ^ flip) for i in range(count)])  3.42 us
  transfers between devices with their start and end apart: 24, of which 9 were waited for; matrix products, arithmetic and copies ran while one was open for 0% of the time, Pallas kernels for 50%

profile of v3, /device:TPU:0, one launch (start us, length us, event | category | flops | bytes accessed | tf_op | source)
XLA Modules:
  0.0 97.0 jit_solution(13533827301895734958)
XLA Ops:
  0.6 4.1 %collective-permute-start = (bf16[32,1536]{1,0:T(8,128)(2,1)}, bf16[32,1536]{1,0:T(8,128)(2,1)S(1)}, u32[]{:S(2)}, u32[]{:S(2)}) collective-permute-start(bf16[32,1536]{1,0:T(8,128)(2,1)} %refs_3_.1), channel_id=1, source_target_pairs={{0,2},{1,3},{2,0},{3,1},{4,6},{5,7},{6,4},{7,5},{8,10},{9,11},{10,... | collective-permute-start | bytes 294920 | tf_op jit(solution)/shard_map/ppermute | solution.py:28
  4.7 4.6 %shard_map.75 = (bf16[1536,768]{1,0:T(8,128)(2,1)S(1)}, bf16[1536,768]{1,0:T(8,128)(2,1)S(1)}, bf16[1536,768]{1,0:T(8,128)(2,1)S(1)}, bf16[1536,768]{1,0:T(8,128)(2,1)S(1)}, bf16[1536,768]{1,0:T(8,128)(2,1)S(1)}) custom-call(s32[1]{0:T(128)} %bitcast.refs_0_, bf16[1536,6144]{1,0:T(8,128)(2,1)} %refs_1_.9), custom_call_target="tpu_custom_call" | custom-call | tf_op jit(solution)/shard_map/pallas_call | solution.py:69
  11.1 3.0 %collective-permute-start.2 = (bf16[32,1536]{1,0:T(8,128)(2,1)S(1)}, bf16[32,1536]{1,0:T(8,128)(2,1)S(1)}, u32[]{:S(2)}, u32[]{:S(2)}) collective-permute-start(bf16[32,1536]{1,0:T(8,128)(2,1)S(1)} %shard_map.77.refs_2_), channel_id=1, source_target_pairs={{0,2},{1,3},{2,0},{3,1},{4,6},{5,7},{6,4},{7,5},{8,10},{9,11},{10,... | collective-permute-start | bytes 294920 | tf_op jit(solution)/shard_map/ppermute | solution.py:28
  14.1 3.1 %shard_map.78 = (bf16[1536,768]{1,0:T(8,128)(2,1)S(1)}, bf16[1536,768]{1,0:T(8,128)(2,1)S(1)}, bf16[1536,768]{1,0:T(8,128)(2,1)S(1)}) custom-call(s32[1]{0:T(128)} %bitcast.refs_0_, bf16[1536,6144]{1,0:T(8,128)(2,1)} %refs_1_.9, bf16[32,1536]{1,0:T(8,128)(2,1)S(1)} %shard_map.77.refs_2_), custom_call_target="tpu_custom_call" | custom-call | tf_op jit(solution)/shard_map/pallas_call | solution.py:69
  18.1 2.4 %shard_map.80 = (bf16[2,128,768]{2,1,0:T(8,128)(2,1)S(1)}, bf16[2,128,768]{2,1,0:T(8,128)(2,1)S(1)}, bf16[768,1536]{1,0:T(8,128)(2,1)S(1)}, bf16[768,1536]{1,0:T(8,128)(2,1)S(1)}) custom-call(s32[1]{0:T(128)} %bitcast.refs_0_, bf16[32,1536]{1,0:T(8,128)(2,1)S(1)} %copy-done.1, bf16[32,1536]{1,0:T(8,128)(2,1)S(1)} %collective-permute-done.refs_1_.refs_2_.refs_4_, ...), custom_call_target="tpu_custom_call" | custom-call | tf_op jit(solution)/shard_map/pallas_call | solution.py:69
  20.6 3.2 %collective-permute-start.6 = (bf16[64,1536]{1,0:T(8,128)(2,1)S(1)}, bf16[64,1536]{1,0:T(8,128)(2,1)S(1)}, u32[]{:S(2)}, u32[]{:S(2)}) collective-permute-start(bf16[64,1536]{1,0:T(8,128)(2,1)S(1)} %shard_map.79.refs_9_), channel_id=1, source_target_pairs={{0,1},{1,0},{2,3},{3,2},{4,5},{5,4},{6,7},{7,6},{8,9},{9,8},{10,11... | collective-permute-start | bytes 589832 | tf_op jit(solution)/shard_map/ppermute | solution.py:28
  27.1 2.4 %shard_map.83 = (bf16[768,1536]{1,0:T(8,128)(2,1)S(1)}, bf16[768,1536]{1,0:T(8,128)(2,1)S(1)}) custom-call(s32[1]{0:T(128)} %bitcast.refs_0_, bf16[6144,1536]{1,0:T(8,128)(2,1)} %refs_6_.1, bf16[2,128,768]{2,1,0:T(8,128)(2,1)S(1)} %shard_map.82.refs_2_), custom_call_target="tpu_custom_call" | custom-call | tf_op jit(solution)/shard_map/pallas_call | solution.py:69
  29.5 3.2 %shard_map.84 = (bf16[2,128,768]{2,1,0:T(8,128)(2,1)S(1)}, bf16[2,128,768]{2,1,0:T(8,128)(2,1)S(1)}, bf16[768,1536]{1,0:T(8,128)(2,1)S(1)}, bf16[768,1536]{1,0:T(8,128)(2,1)S(1)}) custom-call(s32[1]{0:T(128)} %bitcast.refs_0_, bf16[32,1536]{1,0:T(8,128)(2,1)S(1)} %copy-done, bf16[32,1536]{1,0:T(8,128)(2,1)S(1)} %collective-permute-done.2.refs_1_.refs_2_.refs_3_, ...), custom_call_target="tpu_custom_call" | custom-call | tf_op jit(solution)/shard_map/pallas_call | solution.py:69
  33.4 1.6 %collective-permute-start.7 = (bf16[1,128,768]{2,1,0:T(8,128)(2,1)S(1)}, bf16[1,128,768]{2,1,0:T(8,128)(2,1)S(1)}, u32[]{:S(2)}, u32[]{:S(2)}) collective-permute-start(bf16[1,128,768]{2,1,0:T(8,128)(2,1)S(1)} %shard_map.85.refs_2_), channel_id=1, source_target_pairs={{0,16},{4,12},{8,24},{12,4},{16,0},{20,28},{24,8},{28,20},{1,17},{... | collective-permute-start | bytes 589832 | tf_op jit(solution)/shard_map/ppermute | solution.py:38
  36.7 2.4 %shard_map.87 = (bf16[1,128,768]{2,1,0:T(8,128)(2,1)S(1)}, bf16[1,128,768]{2,1,0:T(8,128)(2,1)S(1)}, bf16[768,1536]{1,0:T(8,128)(2,1)S(1)}, bf16[768,1536]{1,0:T(8,128)(2,1)S(1)}) custom-call(s32[1]{0:T(128)} %bitcast.refs_0_, bf16[32,1536]{1,0:T(8,128)(2,1)S(1)} %copy-done, bf16[32,1536]{1,0:T(8,128)(2,1)S(1)} %collective-permute-done.2.refs_1_.refs_2_.refs_3_, ...), custom_call_target="tpu_custom_call" | custom-call | tf_op jit(solution)/shard_map/pallas_call | solution.py:69
  39.1 1.8 %collective-permute-done.7.refs_3_ = bf16[1,128,768]{2,1,0:T(8,128)(2,1)S(1)} collective-permute-done((bf16[1,128,768]{2,1,0:T(8,128)(2,1)S(1)}, bf16[1,128,768]{2,1,0:T(8,128)(2,1)S(1)}, u32[]{:S(2)}, u32[]{:S(2)}) %collective-permute-start.7) | collective-permute-done | bytes 196640 | tf_op jit(solution)/shard_map/ppermute | solution.py:38
  44.6 1.6 %shard_map.90 = (bf16[1,128,768]{2,1,0:T(8,128)(2,1)S(1)}, bf16[1,128,768]{2,1,0:T(8,128)(2,1)S(1)}) custom-call(s32[1]{0:T(128)} %bitcast.refs_0_, bf16[32,1536]{1,0:T(8,128)(2,1)S(1)} %copy-done, bf16[32,1536]{1,0:T(8,128)(2,1)S(1)} %collective-permute-done.2.refs_1_.refs_2_.refs_3_, bf16[64,1536]{1,0:T(8,128)(2,1)S(1)} %collective-permute-done.6.refs_3_.refs_4_, ...), custom_call_target="tpu_custom_call" | custom-call | tf_op jit(solution)/shard_map/pallas_call | solution.py:69
  47.9 1.6 %collective-permute-start.12 = (bf16[256,768]{1,0:T(8,128)(2,1)S(1)}, bf16[256,768]{1,0:T(8,128)(2,1)S(1)}, u32[]{:S(2)}, u32[]{:S(2)}) collective-permute-start(bf16[256,768]{1,0:T(8,128)(2,1)S(1)} %shard_map.91.refs_2_.refs_0_), channel_id=1, source_target_pairs={{0,16},{4,12},{8,24},{12,4},{16,0},{20,28},{24,8},{28,20},{1,17},{... | collective-permute-start | bytes 1179656 | tf_op jit(solution)/shard_map/ppermute | solution.py:38
  49.8 5.9 %collective-permute-done.12.refs_1_ = bf16[256,768]{1,0:T(8,128)(2,1)S(1)} collective-permute-done((bf16[256,768]{1,0:T(8,128)(2,1)S(1)}, bf16[256,768]{1,0:T(8,128)(2,1)S(1)}, u32[]{:S(2)}, u32[]{:S(2)}) %collective-permute-start.12) | collective-permute-done | bytes 393248 | tf_op jit(solution)/shard_map/ppermute | solution.py:38
  55.8 1.6 %collective-permute-start.16 = (bf16[128,768]{1,0:T(8,128)(2,1)S(1)}, bf16[128,768]{1,0:T(8,128)(2,1)S(1)}, u32[]{:S(2)}, u32[]{:S(2)}) collective-permute-start(bf16[128,768]{1,0:T(8,128)(2,1)S(1)} %shard_map.93.refs_2_.refs_0_), channel_id=1, source_target_pairs={{0,8},{4,20},{8,0},{12,28},{16,24},{20,4},{24,16},{28,12},{1,9},{5... | collective-permute-start | bytes 589832 | tf_op jit(solution)/shard_map/ppermute | solution.py:38
  57.4 5.3 %shard_map.95.refs_2_.refs_5_ = bf16[6144,1536]{1,0:T(8,128)(2,1)} custom-call(s32[1]{0:T(128)} %bitcast.refs_0_, bf16[512,768]{1,0:T(8,128)(2,1)S(1)} %shard_map.94.refs_1_.refs_5_.refs_0_, bf16[32,1536]{1,0:T(8,128)(2,1)S(1)} %copy-done, bf16[32,1536]{1,0:T(8,128)(2,1)S(1)} %collective-permute-done.2.refs_1_.refs_2_.refs_3_, ...), custom_call_target="tpu_custom_call" | custom-call | tf_op jit(solution)/shard_map/pallas_call | solution.py:69
  62.8 2.0 %collective-permute-start.19 = (bf16[256,768]{1,0:T(8,128)(2,1)S(1)}, bf16[256,768]{1,0:T(8,128)(2,1)S(1)}, u32[]{:S(2)}, u32[]{:S(2)}) collective-permute-start(bf16[256,768]{1,0:T(8,128)(2,1)S(1)} %shard_map.96.refs_10_.refs_0_), channel_id=1, source_target_pairs={{0,16},{4,12},{8,24},{12,4},{16,0},{20,28},{24,8},{28,20},{1,17},{... | collective-permute-start | bytes 1179656 | tf_op jit(solution)/shard_map/ppermute | solution.py:38
  64.7 2.6 %shard_map.97 = (bf16[64,1536]{1,0:T(8,128)(2,1)S(1)}, bf16[64,1536]{1,0:T(8,128)(2,1)S(1)}) custom-call(bf16[512,768]{1,0:T(8,128)(2,1)S(1)} %shard_map.94.refs_1_.refs_5_.refs_0_, bf16[512,768]{1,0:T(8,128)(2,1)S(1)} %collective-permute-done.15.refs_1_, bf16[768,1536]{1,0:T(8,128)(2,1)S(1)} %get-tuple-element.60.refs_4_.refs_5_.refs_2_, ...), custom_call_target="tpu_custom_call" | custom-call | flops 2415919104 | bytes 18874368 | tf_op jit(solution)/shard_map/pallas_call | solution.py:69
  67.4 5.1 %shard_map.98.refs_2_ = bf16[6144,1536]{1,0:T(8,128)(2,1)} custom-call(s32[1]{0:T(128)} %bitcast.refs_0_, bf16[512,768]{1,0:T(8,128)(2,1)S(1)} %collective-permute-done.15.refs_1_, bf16[32,1536]{1,0:T(8,128)(2,1)S(1)} %copy-done, bf16[32,1536]{1,0:T(8,128)(2,1)S(1)} %collective-permute-done.2.refs_1_.refs_2_.refs_3_, ...), custom_call_target="tpu_custom_call", output_to_operand_aliasing={{}: (5, {})} | custom-call | flops 1207959552 | bytes 9437184 | tf_op jit(solution)/shard_map/pallas_call | solution.py:69
  74.3 1.8 %collective-permute-start.18 = (bf16[32,1536]{1,0:T(8,128)(2,1)S(1)}, bf16[32,1536]{1,0:T(8,128)(2,1)S(1)}, u32[]{:S(2)}, u32[]{:S(2)}) collective-permute-start(bf16[32,1536]{1,0:T(8,128)(2,1)S(1)} %get-tuple-element.71.refs_2_), channel_id=1, source_target_pairs={{0,2},{1,3},{2,0},{3,1},{4,6},{5,7},{6,4},{7,5},{8,10},{9,11},{10,... | collective-permute-start | bytes 294920 | tf_op jit(solution)/shard_map/ppermute | solution.py:28
  76.6 6.0 %shard_map.101 = (bf16[32,1536]{1,0:T(8,128)(2,1)S(1)}, bf16[32,1536]{1,0:T(8,128)(2,1)S(1)}, bf16[32,1536]{1,0:T(8,128)(2,1)S(1)}, bf16[32,1536]{1,0:T(8,128)(2,1)S(1)}) custom-call(bf16[512,768]{1,0:T(8,128)(2,1)S(1)} %shard_map.100.refs_0_.refs_10_.refs_1_, bf16[512,768]{1,0:T(8,128)(2,1)S(1)} %collective-permute-done.20.refs_1_.refs_2_, ...), custom_call_target="tpu_custom_call" | custom-call | flops 2415919104 | bytes 18874368 | tf_op jit(solution)/shard_map/pallas_call | solution.py:69
  82.6 1.8 %collective-permute-start.22 = (bf16[32,1536]{1,0:T(8,128)(2,1)S(1)}, bf16[32,1536]{1,0:T(8,128)(2,1)S(1)}, u32[]{:S(2)}, u32[]{:S(2)}) collective-permute-start(bf16[32,1536]{1,0:T(8,128)(2,1)S(1)} %get-tuple-element.74), channel_id=1, source_target_pairs={{0,2},{1,3},{2,0},{3,1},{4,6},{5,7},{6,4},{7,5},{8,10},{9,11},{10,... | collective-permute-start | bytes 294920 | tf_op jit(solution)/shard_map/ppermute | solution.py:28
  84.8 2.2 %collective-permute-start.21 = (bf16[32,1536]{1,0:T(8,128)(2,1)S(1)}, bf16[32,1536]{1,0:T(8,128)(2,1)S(1)}, u32[]{:S(2)}, u32[]{:S(2)}) collective-permute-start(bf16[32,1536]{1,0:T(8,128)(2,1)S(1)} %get-tuple-element.72.refs_2_), channel_id=1, source_target_pairs={{0,3},{1,2},{2,1},{3,0},{4,7},{5,6},{6,5},{7,4},{8,11},{9,10},{10,... | collective-permute-start | bytes 294920 | tf_op jit(solution)/shard_map/ppermute | solution.py:28
  87.7 8.6 %shard_map.103 = bf16[1536,6144]{1,0:T(8,128)(2,1)} custom-call(s32[1]{0:T(128)} %bitcast.refs_0_, bf16[512,768]{1,0:T(8,128)(2,1)S(1)} %shard_map.100.refs_0_.refs_10_.refs_1_, bf16[512,768]{1,0:T(8,128)(2,1)S(1)} %collective-permute-done.20.refs_1_.refs_2_, bf16[32,1536]{1,0:T(8,128)(2,1)S(1)} %copy-done.1, ...), custom_call_target="tpu_custom_call" | custom-call | flops 2415919104 | bytes 18874368 | tf_op jit(solution)/shard_map/pallas_call | solution.py:69
  (58 shorter events, 18.2 us)
Async XLA Ops:
  0.6 9.2 %collective-permute-start = (bf16[32,1536]{1,0:T(8,128)(2,1)}, bf16[32,1536]{1,0:T(8,128)(2,1)S(1)}, u32[]{:S(2)}, u32[]{:S(2)}) collective-permute-start(bf16[32,1536]{1,0:T(8,128)(2,1)} %refs_3_.1), channel_id=1, source_target_pairs={{0,2},{1,3},{2,0},{3,1},{4,6},{5,7},{6,4},{7,5},{8,10},{9,11},{10,... | collective-permute-start | bytes 294920 | tf_op jit(solution)/shard_map/ppermute | solution.py:28
  9.9 8.3 %collective-permute-start.1 = (bf16[64,1536]{1,0:T(8,128)(2,1)S(1)}, bf16[64,1536]{1,0:T(8,128)(2,1)S(1)}, u32[]{:S(2)}, u32[]{:S(2)}) collective-permute-start(bf16[64,1536]{1,0:T(8,128)(2,1)S(1)} %shard_map.76.refs_1_), channel_id=1, source_target_pairs={{0,1},{1,0},{2,3},{3,2},{4,5},{5,4},{6,7},{7,6},{8,9},{9,8},{10,11... | collective-permute-start | bytes 589832 | tf_op jit(solution)/shard_map/ppermute | solution.py:28
  11.1 6.2 %collective-permute-start.2 = (bf16[32,1536]{1,0:T(8,128)(2,1)S(1)}, bf16[32,1536]{1,0:T(8,128)(2,1)S(1)}, u32[]{:S(2)}, u32[]{:S(2)}) collective-permute-start(bf16[32,1536]{1,0:T(8,128)(2,1)S(1)} %shard_map.77.refs_2_), channel_id=1, source_target_pairs={{0,2},{1,3},{2,0},{3,1},{4,6},{5,7},{6,4},{7,5},{8,10},{9,11},{10,... | collective-permute-start | bytes 294920 | tf_op jit(solution)/shard_map/ppermute | solution.py:28
  20.5 4.9 %collective-permute-start.4 = (bf16[2,128,768]{2,1,0:T(8,128)(2,1)S(1)}, bf16[2,128,768]{2,1,0:T(8,128)(2,1)S(1)}, u32[]{:S(2)}, u32[]{:S(2)}) collective-permute-start(bf16[2,128,768]{2,1,0:T(8,128)(2,1)S(1)} %get-tuple-element.52), channel_id=1, source_target_pairs={{0,4},{4,0},{8,12},{12,8},{16,20},{20,16},{24,28},{28,24},{1,5},{5... | collective-permute-start | bytes 1179656 | tf_op jit(solution)/shard_map/ppermute | solution.py:28
  20.6 8.8 %collective-permute-start.6 = (bf16[64,1536]{1,0:T(8,128)(2,1)S(1)}, bf16[64,1536]{1,0:T(8,128)(2,1)S(1)}, u32[]{:S(2)}, u32[]{:S(2)}) collective-permute-start(bf16[64,1536]{1,0:T(8,128)(2,1)S(1)} %shard_map.79.refs_9_), channel_id=1, source_target_pairs={{0,1},{1,0},{2,3},{3,2},{4,5},{5,4},{6,7},{7,6},{8,9},{9,8},{10,11... | collective-permute-start | bytes 589832 | tf_op jit(solution)/shard_map/ppermute | solution.py:28
  25.2 7.7 %collective-permute-start.3 = (bf16[2,128,768]{2,1,0:T(8,128)(2,1)S(1)}, bf16[2,128,768]{2,1,0:T(8,128)(2,1)S(1)}, u32[]{:S(2)}, u32[]{:S(2)}) collective-permute-start(bf16[2,128,768]{2,1,0:T(8,128)(2,1)S(1)} %get-tuple-element.50.refs_2_), channel_id=1, source_target_pairs={{0,4},{4,0},{8,12},{12,8},{16,20},{20,16},{24,28},{28,24},{1,5},{5... | collective-permute-start | bytes 1179656 | tf_op jit(solution)/shard_map/ppermute | solution.py:28
  25.5 7.8 %collective-permute-start.5 = (bf16[2,128,768]{2,1,0:T(8,128)(2,1)S(1)}, bf16[2,128,768]{2,1,0:T(8,128)(2,1)S(1)}, u32[]{:S(2)}, u32[]{:S(2)}) collective-permute-start(bf16[2,128,768]{2,1,0:T(8,128)(2,1)S(1)} %shard_map.82.refs_2_), channel_id=1, source_target_pairs={{0,8},{4,20},{8,0},{12,28},{16,24},{20,4},{24,16},{28,12},{1,9},{5... | collective-permute-start | bytes 1179656 | tf_op jit(solution)/shard_map/ppermute | solution.py:38
  32.7 2.3 %collective-permute-start.8 = (bf16[2,128,768]{2,1,0:T(8,128)(2,1)S(1)}, bf16[2,128,768]{2,1,0:T(8,128)(2,1)S(1)}, u32[]{:S(2)}, u32[]{:S(2)}) collective-permute-start(bf16[2,128,768]{2,1,0:T(8,128)(2,1)S(1)} %get-tuple-element.59), channel_id=1, source_target_pairs={{0,4},{4,0},{8,12},{12,8},{16,20},{20,16},{24,28},{28,24},{1,5},{5... | collective-permute-start | bytes 1179656 | tf_op jit(solution)/shard_map/ppermute | solution.py:28
  33.4 7.5 %collective-permute-start.7 = (bf16[1,128,768]{2,1,0:T(8,128)(2,1)S(1)}, bf16[1,128,768]{2,1,0:T(8,128)(2,1)S(1)}, u32[]{:S(2)}, u32[]{:S(2)}) collective-permute-start(bf16[1,128,768]{2,1,0:T(8,128)(2,1)S(1)} %shard_map.85.refs_2_), channel_id=1, source_target_pairs={{0,16},{4,12},{8,24},{12,4},{16,0},{20,28},{24,8},{28,20},{1,17},{... | collective-permute-start | bytes 589832 | tf_op jit(solution)/shard_map/ppermute | solution.py:38
  35.1 7.8 %collective-permute-start.11 = (bf16[2,128,768]{2,1,0:T(8,128)(2,1)S(1)}, bf16[2,128,768]{2,1,0:T(8,128)(2,1)S(1)}, u32[]{:S(2)}, u32[]{:S(2)}) collective-permute-start(bf16[2,128,768]{2,1,0:T(8,128)(2,1)S(1)} %shard_map.86.refs_7_), channel_id=1, source_target_pairs={{0,8},{4,20},{8,0},{12,28},{16,24},{20,4},{24,16},{28,12},{1,9},{5... | collective-permute-start | bytes 1179656 | tf_op jit(solution)/shard_map/ppermute | solution.py:38
  39.1 3.7 %collective-permute-start.10 = (bf16[1,128,768]{2,1,0:T(8,128)(2,1)S(1)}, bf16[1,128,768]{2,1,0:T(8,128)(2,1)S(1)}, u32[]{:S(2)}, u32[]{:S(2)}) collective-permute-start(bf16[1,128,768]{2,1,0:T(8,128)(2,1)S(1)} %get-tuple-element.64), channel_id=1, source_target_pairs={{0,4},{4,0},{8,12},{12,8},{16,20},{20,16},{24,28},{28,24},{1,5},{5... | collective-permute-start | bytes 589832 | tf_op jit(solution)/shard_map/ppermute | solution.py:28
  41.2 6.7 %collective-permute-start.9 = (bf16[128,768]{1,0:T(8,128)(2,1)S(1)}, bf16[128,768]{1,0:T(8,128)(2,1)S(1)}, u32[]{:S(2)}, u32[]{:S(2)}) collective-permute-start(bf16[128,768]{1,0:T(8,128)(2,1)S(1)} %get-tuple-element.61.refs_3_.refs_0_), channel_id=1, source_target_pairs={{0,8},{4,20},{8,0},{12,28},{16,24},{20,4},{24,16},{28,12},{1,9},{5... | collective-permute-start | bytes 589832 | tf_op jit(solution)/shard_map/ppermute | solution.py:38
  43.0 6.4 %collective-permute-start.13 = (bf16[1,128,768]{2,1,0:T(8,128)(2,1)S(1)}, bf16[1,128,768]{2,1,0:T(8,128)(2,1)S(1)}, u32[]{:S(2)}, u32[]{:S(2)}) collective-permute-start(bf16[1,128,768]{2,1,0:T(8,128)(2,1)S(1)} %shard_map.89.refs_6_), channel_id=1, source_target_pairs={{0,16},{4,12},{8,24},{12,4},{16,0},{20,28},{24,8},{28,20},{1,17},{... | collective-permute-start | bytes 589832 | tf_op jit(solution)/shard_map/ppermute | solution.py:38
  46.2 3.3 %collective-permute-start.14 = (bf16[1,128,768]{2,1,0:T(8,128)(2,1)S(1)}, bf16[1,128,768]{2,1,0:T(8,128)(2,1)S(1)}, u32[]{:S(2)}, u32[]{:S(2)}) collective-permute-start(bf16[1,128,768]{2,1,0:T(8,128)(2,1)S(1)} %get-tuple-element.65.refs_2_), channel_id=1, source_target_pairs={{0,4},{4,0},{8,12},{12,8},{16,20},{20,16},{24,28},{28,24},{1,5},{5... | collective-permute-start | bytes 589832 | tf_op jit(solution)/shard_map/ppermute | solution.py:28
  47.9 7.8 %collective-permute-start.12 = (bf16[256,768]{1,0:T(8,128)(2,1)S(1)}, bf16[256,768]{1,0:T(8,128)(2,1)S(1)}, u32[]{:S(2)}, u32[]{:S(2)}) collective-permute-start(bf16[256,768]{1,0:T(8,128)(2,1)S(1)} %shard_map.91.refs_2_.refs_0_), channel_id=1, source_target_pairs={{0,16},{4,12},{8,24},{12,4},{16,0},{20,28},{24,8},{28,20},{1,17},{... | collective-permute-start | bytes 1179656 | tf_op jit(solution)/shard_map/ppermute | solution.py:38
  55.8 9.0 %collective-permute-start.15 = (bf16[512,768]{1,0:T(8,128)(2,1)S(1)}, bf16[512,768]{1,0:T(8,128)(2,1)S(1)}, u32[]{:S(2)}, u32[]{:S(2)}) collective-permute-start(bf16[512,768]{1,0:T(8,128)(2,1)S(1)} %shard_map.94.refs_1_.refs_5_.refs_0_), channel_id=1, source_target_pairs={{0,4},{4,0},{8,12},{12,8},{16,20},{20,16},{24,28},{28,24},{1,5},{5... | collective-permute-start | bytes 2359304 | tf_op jit(solution)/shard_map/ppermute | solution.py:28
  55.8 6.9 %collective-permute-start.16 = (bf16[128,768]{1,0:T(8,128)(2,1)S(1)}, bf16[128,768]{1,0:T(8,128)(2,1)S(1)}, u32[]{:S(2)}, u32[]{:S(2)}) collective-permute-start(bf16[128,768]{1,0:T(8,128)(2,1)S(1)} %shard_map.93.refs_2_.refs_0_), channel_id=1, source_target_pairs={{0,8},{4,20},{8,0},{12,28},{16,24},{20,4},{24,16},{28,12},{1,9},{5... | collective-permute-start | bytes 589832 | tf_op jit(solution)/shard_map/ppermute | solution.py:38
  62.8 11.4 %collective-permute-start.19 = (bf16[256,768]{1,0:T(8,128)(2,1)S(1)}, bf16[256,768]{1,0:T(8,128)(2,1)S(1)}, u32[]{:S(2)}, u32[]{:S(2)}) collective-permute-start(bf16[256,768]{1,0:T(8,128)(2,1)S(1)} %shard_map.96.refs_10_.refs_0_), channel_id=1, source_target_pairs={{0,16},{4,12},{8,24},{12,4},{16,0},{20,28},{24,8},{28,20},{1,17},{... | collective-permute-start | bytes 1179656 | tf_op jit(solution)/shard_map/ppermute | solution.py:38
  67.3 6.7 %collective-permute-start.17 = (bf16[64,1536]{1,0:T(8,128)(2,1)S(1)}, bf16[64,1536]{1,0:T(8,128)(2,1)S(1)}, u32[]{:S(2)}, u32[]{:S(2)}) collective-permute-start(bf16[64,1536]{1,0:T(8,128)(2,1)S(1)} %get-tuple-element.69.refs_6_), channel_id=1, source_target_pairs={{0,1},{1,0},{2,3},{3,2},{4,5},{5,4},{6,7},{7,6},{8,9},{9,8},{10,11... | collective-permute-start | bytes 589832 | tf_op jit(solution)/shard_map/ppermute | solution.py:28
  74.2 2.4 %collective-permute-start.20 = (bf16[512,768]{1,0:T(8,128)(2,1)S(1)}, bf16[512,768]{1,0:T(8,128)(2,1)S(1)}, u32[]{:S(2)}, u32[]{:S(2)}) collective-permute-start(bf16[512,768]{1,0:T(8,128)(2,1)S(1)} %shard_map.100.refs_0_.refs_10_.refs_1_), channel_id=1, source_target_pairs={{0,4},{4,0},{8,12},{12,8},{16,20},{20,16},{24,28},{28,24},{1,5},{5... | collective-permute-start | bytes 2359304 | tf_op jit(solution)/shard_map/ppermute | solution.py:28
  74.3 12.8 %collective-permute-start.18 = (bf16[32,1536]{1,0:T(8,128)(2,1)S(1)}, bf16[32,1536]{1,0:T(8,128)(2,1)S(1)}, u32[]{:S(2)}, u32[]{:S(2)}) collective-permute-start(bf16[32,1536]{1,0:T(8,128)(2,1)S(1)} %get-tuple-element.71.refs_2_), channel_id=1, source_target_pairs={{0,2},{1,3},{2,0},{3,1},{4,6},{5,7},{6,4},{7,5},{8,10},{9,11},{10,... | collective-permute-start | bytes 294920 | tf_op jit(solution)/shard_map/ppermute | solution.py:28
  82.6 13.7 %collective-permute-start.22 = (bf16[32,1536]{1,0:T(8,128)(2,1)S(1)}, bf16[32,1536]{1,0:T(8,128)(2,1)S(1)}, u32[]{:S(2)}, u32[]{:S(2)}) collective-permute-start(bf16[32,1536]{1,0:T(8,128)(2,1)S(1)} %get-tuple-element.74), channel_id=1, source_target_pairs={{0,2},{1,3},{2,0},{3,1},{4,6},{5,7},{6,4},{7,5},{8,10},{9,11},{10,... | collective-permute-start | bytes 294920 | tf_op jit(solution)/shard_map/ppermute | solution.py:28
  84.4 11.9 %collective-permute-start.23 = (bf16[32,1536]{1,0:T(8,128)(2,1)S(1)}, bf16[32,1536]{1,0:T(8,128)(2,1)S(1)}, u32[]{:S(2)}, u32[]{:S(2)}) collective-permute-start(bf16[32,1536]{1,0:T(8,128)(2,1)S(1)} %get-tuple-element.75), channel_id=1, source_target_pairs={{0,1},{1,0},{2,3},{3,2},{4,5},{5,4},{6,7},{7,6},{8,9},{9,8},{10,11... | collective-permute-start | bytes 294920 | tf_op jit(solution)/shard_map/ppermute | solution.py:28
  84.8 11.5 %collective-permute-start.21 = (bf16[32,1536]{1,0:T(8,128)(2,1)S(1)}, bf16[32,1536]{1,0:T(8,128)(2,1)S(1)}, u32[]{:S(2)}, u32[]{:S(2)}) collective-permute-start(bf16[32,1536]{1,0:T(8,128)(2,1)S(1)} %get-tuple-element.72.refs_2_), channel_id=1, source_target_pairs={{0,3},{1,2},{2,1},{3,0},{4,7},{5,6},{6,5},{7,4},{8,11},{9,10},{10,... | collective-permute-start | bytes 294920 | tf_op jit(solution)/shard_map/ppermute | solution.py:28
  (2 other events, 6.8 us)

commit v4 on v3

--- a/solution.py
+++ b/solution.py
@@ -47,7 +47,7 @@
 LAST = []
 
 
-def call(kernel, arrays, outs, flops, moved, after=(), scratch=(), in_place=False):
+def call(kernel, arrays, outs, flops, moved, after=(), scratch=()):
     unread, count = [*LAST, *after], len(arrays)
 
     def body(*refs):
@@ -72,7 +72,6 @@
         + [pl.BlockSpec(memory_space=pl.ANY)] * len(unread),
         out_specs=[specs[space] for space, value in outs],
         scratch_shapes=list(scratch),
-        input_output_aliases={count - 1: 0} if in_place else {},
         out_shape=[
             pltpu.VMEM(shape, dtype) if space == "vmem" else jax.ShapeDtypeStruct(shape, dtype)
             for space, (shape, dtype) in outs
@@ -259,30 +258,37 @@
     )
 
 
-def weight_grad(weight, stacks, odds, shards, into=None):
+def block_keys(weight):
+    chips = len(weight.held) // 2
+    return [(reverse(p, weight.bits) if odd else p, odd) for odd in range(2) for p in range(chips)]
+
+
+def weight_grad(weight, stacks, shards, cols=1, groups=()):
     pieces, order = shards
     width, by_rows, block = weight.width, weight.by_rows, weight.block
     chips = len(weight.held) // 2
     tokens = stacks[0].shape[0] // chips
     halves = 2
     size = (block if by_rows else width) // halves
-    keys = [
-        (i, p, (reverse(p, weight.bits) if odd else p, odd))
-        for p in range(chips)
-        for i, odd in enumerate(odds)
-    ]
+    keys = block_keys(weight)
+    order_of = [i for p in range(chips) for i in (p, chips + p)]
+    parts = [weight.held[key] for key in keys] if groups else []
 
     def kernel(me_ref, *refs):
-        stack_refs, refs = refs[: len(stacks)], refs[len(stacks) :]
+        stack_refs, refs = refs[:2], refs[2:]
         piece_refs, refs = refs[: len(pieces)], refs[len(pieces) :]
-        grad, other, turned, ready, sent = refs[-5:]
+        part_refs, refs = refs[: len(parts)], refs[len(parts) :]
+        sums, (grad, other, turned, ready, sent, total) = refs[: len(groups)], refs[len(groups) :]
         place(piece_refs, order, other)
         if not by_rows:
             turned[...] = other[...].T
         me = me_ref[0]
 
+        def value(i):
+            return stack_refs[i // chips], slice(i % chips * tokens, (i % chips + 1) * tokens)
+
         def writes(step):
-            to = weight.part(grad, me, keys[step // halves][2])
+            to = weight.part(grad, me, keys[order_of[step // halves]])
             at = step % halves * size
             to = to.at[at : at + size, :]
             slot = step % WRITES
@@ -293,47 +299,58 @@
                 for i in range(WRITE_CUTS)
             ]
 
+        def product(step):
+            stack, of = value(order_of[step // halves])
+            at = slice(step % halves * size, (step % halves + 1) * size)
+            if by_rows:
+                out = dot(stack[of, at], other[...], 0, 0)
+            else:
+                out = dot(turned[at, :], stack[of, :], 1, 0)
+            ready[step % WRITES] = out.astype(BF16)
+
         steps = len(keys) * halves
         for step in range(steps):
             if step >= WRITES:
                 for write in writes(step - WRITES):
                     write.wait()
-
-            @pl.when(me >= 0)
-            def _():
-                i, p, key = keys[step // halves]
-                stack, of = stack_refs[i], slice(p * tokens, (p + 1) * tokens)
-                at = slice(step % halves * size, (step % halves + 1) * size)
-                if by_rows:
-                    out = dot(stack[of, at], other[...], 0, 0)
-                else:
-                    out = dot(turned[at, :], stack[of, :], 1, 0)
-                ready[step % WRITES] = out.astype(BF16)
-
+            if by_rows:
+                product(step)
+            else:
+                pl.when(me >= 0)(functools.partial(product, step))
             for write in writes(step):
                 write.start()
+
+        @pl.when(me >= 0)
+        def _():
+            for i, part in enumerate(part_refs):
+                stack, of = value(i)
+                term = dot(stack[of, :], part[...], 1, 0)
+                total[...] = term if i == 0 else total[...] + term
+            rows = tokens // cols
+            for group, out in zip(groups, sums):
+                for i, q in enumerate(group):
+                    out[i * rows : (i + 1) * rows, :] = total[q * rows : (q + 1) * rows, :].astype(BF16)
+
         for step in range(max(0, steps - WRITES), steps):
             for write in writes(step):
                 write.wait()
 
     return call(
         kernel,
-        [("smem", weight.me)]
-        + in_vmem(stacks)
-        + in_vmem(pieces)
-        + ([("hbm", into)] if into is not None else []),
-        [("hbm", (weight.value.shape, BF16))],
-        2 * tokens * width * block * len(keys) if 1 in odds else 0,
-        2 * width * block * len(keys) if 1 in odds else 0,
+        [("smem", weight.me)] + in_vmem(stacks) + in_vmem(pieces) + in_vmem(parts),
+        [("vmem", ((len(group) * tokens // cols, width), BF16)) for group in groups]
+        + [("hbm", (weight.value.shape, BF16))],
+        2 * tokens * width * block * len(keys),
+        2 * width * block * len(keys),
         (),
         [
             pltpu.VMEM((tokens, width), BF16),
             pltpu.VMEM((width, tokens), BF16),
             pltpu.VMEM((WRITES, size, width if by_rows else block), BF16),
             pltpu.SemaphoreType.DMA((WRITES, WRITE_CUTS)),
+            pltpu.VMEM((tokens, width), F32),
         ],
-        into is not None,
-    )[0]
+    )
 
 
 def summed_half(keep, got, count, after=()):
@@ -350,11 +367,15 @@
     return call(kernel, in_vmem([keep, got]), outs, 0, 0, after)
 
 
-def added(terms, space="vmem"):
+def added(*sums, space="vmem"):
     def kernel(*refs):
-        refs[-1][...] = sum(ref[...].astype(F32) for ref in refs[: len(terms)]).astype(BF16)
-
-    return call(kernel, in_vmem(terms), [(space, (terms[0].shape, BF16))], 0, 0)[0]
+        refs, outs = refs[: -len(sums)], refs[-len(sums) :]
+        for terms, out in zip(sums, outs):
+            out[...] = sum(ref[...].astype(F32) for ref in refs[: len(terms)]).astype(BF16)
+            refs = refs[len(terms) :]
+
+    arrays = in_vmem([term for terms in sums for term in terms])
+    return call(kernel, arrays, [(space, (terms[0].shape, BF16)) for terms in sums], 0, 0)
 
 
 def block_of(terms):
@@ -394,10 +415,6 @@
 
 def exchange_col(parts, cols):
     return [parts[0]] + [swap(parts[q], "col", q, cols) for q in range(cols - 1, 0, -1)]
-
-
-def summed(parts):
-    return sum(part.astype(F32) for part in parts).astype(BF16)
 
 
 def blocked(rows, cols, tokens, cotangent, w_in, w_out):
@@ -435,14 +452,14 @@
     keep, sent = project(w_in, token_shards, first, wanted[8:10])
     got = other_core(sent)
     here, sent = project(w_in, token_shards, second + own, [])
-    got_here, came = other_core(sent), across(added([keep, got]), 0, rows)
+    got_here, came = other_core(sent), across(added([keep, got])[0], 0, rows)
     load(wanted[10:12])
     keep, sent = project(w_out, cot_shards, first, wanted[12:14])
     got = other_core(sent)
     sent = one_block([(here, 0), (got_here, 0), (came, 1)])
     terms = [(here, 1), (got_here, 1), (came, 0), (across(sent, 1, rows), 0)]
 
-    came = across(added([keep, got]), 0, rows)
+    came = across(added([keep, got])[0], 0, rows)
     keep, sent = project(w_out, cot_shards, second, wanted[14:])
     got = other_core(sent)
     hidden, act = activate(terms)
@@ -455,23 +472,20 @@
     grad_hidden = activate_back(hidden, [(keep, 0), (part, 0), (got, 0)])
     stack = doubled(stack, 1)
     act = stack, other_core(stack)
-    grad_w_out = weight_grad(w_out, act[:1], (0,), cot_shards)
     back_stack = doubled(grad_hidden, 0, PART_COST)
 
     even, odd = range(0, cols, 2), range(1, cols, 2)
-    keep, send = block_sum(w_out, act, (0, 1), cols, (even, odd))
-    got = swap(send, "col", 1, cols)
-    grad_w_out = weight_grad(w_out, act[1:], (1,), cot_shards, grad_w_out)
+    keep, sent, grad_w_out = weight_grad(w_out, act, cot_shards, cols, (even, odd))
+    got = swap(sent, "col", 1, cols)
+    back_stack = doubled(back_stack, 1)
+    grad_hidden = back_stack, other_core(back_stack)
+    token_parts = block_sum(w_in, grad_hidden, (0, 1), cols, [[q] for q in range(cols)])
     layer_out, *sums = summed_half(keep, got, len(even))
     layer_parts = [swap(part, "col", q, cols) for part, q in zip(sums, even[1:])]
-    back_stack = doubled(back_stack, 1)
-    grad_hidden = back_stack, other_core(back_stack)
-
-    token_parts = block_sum(w_in, grad_hidden, (0, 1), cols, [[q] for q in range(cols)])
-    layer_out = added([layer_out, *layer_parts], "window")
-    grad_w_in = weight_grad(w_in, grad_hidden, (0, 1), token_shards)
     token_parts = exchange_col(token_parts, cols)
-    return (layer_out, summed(token_parts), grad_w_in, grad_w_out)
+    (grad_w_in,) = weight_grad(w_in, grad_hidden, token_shards)
+    layer_out, grad_tokens = added([layer_out, *layer_parts], token_parts, space="window")
+    return (layer_out, grad_tokens, grad_w_in, grad_w_out)
 
 
 def collective(tokens, cotangent, w_in, w_out):

time: 97.2 us -> 94.8 us (0.975)
  Pallas kernels: 50.6 us -> 47.9 us
  waiting for transfers between devices: 13.3 us -> 15.1 us
    pallas_call x29 -> x27, Pallas kernels: 50.6 us -> 47.9 us  [call(): pl.pallas_call(body, in_specs=[specs[space] for space, value in arrays] +...]
    ppermute x16, waiting for transfers between devices: 3.42 us -> 5.34 us  [swap(): return lax.ppermute(value, axis, [(i, i ^ flip) for i in range(count)])]
  transfers between devices with their start and end apart: 24 -> 24, of which waited for: 9 -> 10; matrix products, arithmetic and copies ran while one was open for 0% -> 0% of each run, Pallas kernels for 50% -> 47%
where the time goes in v4:
time: 94.8 us; the launch traced here: 94.7 us
  Pallas kernels  47.9 us (51%)
  starting transfers between devices  30.8 us (32%)
  waiting for transfers between devices  15.1 us (16%)
    pallas_call x27, Pallas kernels, call(): pl.pallas_call(body, in_specs=[specs[space] for space, value in arrays] +...  47.9 us
    ppermute x16, starting transfers between devices, swap(): return lax.ppermute(value, axis, [(i, i ^ flip) for i in range(count)])  17.8 us
    ppermute x8, starting transfers between devices, across(): return lax.ppermute(value, 'row', [(i, i ^ flips[i]) for i in range(rows)])  13 us
    ppermute x8, waiting for transfers between devices, across(): return lax.ppermute(value, 'row', [(i, i ^ flips[i]) for i in range(rows)])  9.77 us
    ppermute x16, waiting for transfers between devices, swap(): return lax.ppermute(value, axis, [(i, i ^ flip) for i in range(count)])  5.34 us
  transfers between devices with their start and end apart: 24, of which 10 were waited for; matrix products, arithmetic and copies ran while one was open for 0% of the time, Pallas kernels for 47%

profile of v4, /device:TPU:0, one launch (start us, length us, event | category | flops | bytes accessed | tf_op | source)
XLA Modules:
  0.0 94.7 jit_solution(14529588968825049454)
XLA Ops:
  0.6 4.1 %collective-permute-start = (bf16[32,1536]{1,0:T(8,128)(2,1)}, bf16[32,1536]{1,0:T(8,128)(2,1)S(1)}, u32[]{:S(2)}, u32[]{:S(2)}) collective-permute-start(bf16[32,1536]{1,0:T(8,128)(2,1)} %refs_3_.3), channel_id=1, source_target_pairs={{0,2},{1,3},{2,0},{3,1},{4,6},{5,7},{6,4},{7,5},{8,10},{9,11},{10,... | collective-permute-start | bytes 294920 | tf_op jit(solution)/shard_map/ppermute | solution.py:28
  4.7 4.6 %shard_map.75 = (bf16[1536,768]{1,0:T(8,128)(2,1)S(1)}, bf16[1536,768]{1,0:T(8,128)(2,1)S(1)}, bf16[1536,768]{1,0:T(8,128)(2,1)S(1)}, bf16[1536,768]{1,0:T(8,128)(2,1)S(1)}, bf16[1536,768]{1,0:T(8,128)(2,1)S(1)}) custom-call(s32[1]{0:T(128)} %bitcast.refs_0_, bf16[1536,6144]{1,0:T(8,128)(2,1)} %refs_1_.9), custom_call_target="tpu_custom_call" | custom-call | tf_op jit(solution)/shard_map/pallas_call | solution.py:69
  11.1 3.0 %collective-permute-start.2 = (bf16[32,1536]{1,0:T(8,128)(2,1)S(1)}, bf16[32,1536]{1,0:T(8,128)(2,1)S(1)}, u32[]{:S(2)}, u32[]{:S(2)}) collective-permute-start(bf16[32,1536]{1,0:T(8,128)(2,1)S(1)} %shard_map.77.refs_2_), channel_id=1, source_target_pairs={{0,2},{1,3},{2,0},{3,1},{4,6},{5,7},{6,4},{7,5},{8,10},{9,11},{10,... | collective-permute-start | bytes 294920 | tf_op jit(solution)/shard_map/ppermute | solution.py:28
  14.1 3.1 %shard_map.78 = (bf16[1536,768]{1,0:T(8,128)(2,1)S(1)}, bf16[1536,768]{1,0:T(8,128)(2,1)S(1)}, bf16[1536,768]{1,0:T(8,128)(2,1)S(1)}) custom-call(s32[1]{0:T(128)} %bitcast.refs_0_, bf16[1536,6144]{1,0:T(8,128)(2,1)} %refs_1_.9, bf16[32,1536]{1,0:T(8,128)(2,1)S(1)} %shard_map.77.refs_2_), custom_call_target="tpu_custom_call" | custom-call | tf_op jit(solution)/shard_map/pallas_call | solution.py:69
  18.1 2.4 %shard_map.80 = (bf16[2,128,768]{2,1,0:T(8,128)(2,1)S(1)}, bf16[2,128,768]{2,1,0:T(8,128)(2,1)S(1)}, bf16[768,1536]{1,0:T(8,128)(2,1)S(1)}, bf16[768,1536]{1,0:T(8,128)(2,1)S(1)}) custom-call(s32[1]{0:T(128)} %bitcast.refs_0_, bf16[32,1536]{1,0:T(8,128)(2,1)S(1)} %copy-done.1, bf16[32,1536]{1,0:T(8,128)(2,1)S(1)} %collective-permute-done.refs_1_.refs_2_.refs_4_, ...), custom_call_target="tpu_custom_call" | custom-call | tf_op jit(solution)/shard_map/pallas_call | solution.py:69
  20.6 3.2 %collective-permute-start.6 = (bf16[64,1536]{1,0:T(8,128)(2,1)S(1)}, bf16[64,1536]{1,0:T(8,128)(2,1)S(1)}, u32[]{:S(2)}, u32[]{:S(2)}) collective-permute-start(bf16[64,1536]{1,0:T(8,128)(2,1)S(1)} %shard_map.79.refs_9_), channel_id=1, source_target_pairs={{0,1},{1,0},{2,3},{3,2},{4,5},{5,4},{6,7},{7,6},{8,9},{9,8},{10,11... | collective-permute-start | bytes 589832 | tf_op jit(solution)/shard_map/ppermute | solution.py:28
  25.5 1.6 %collective-permute-start.5 = (bf16[2,128,768]{2,1,0:T(8,128)(2,1)S(1)}, bf16[2,128,768]{2,1,0:T(8,128)(2,1)S(1)}, u32[]{:S(2)}, u32[]{:S(2)}) collective-permute-start(bf16[2,128,768]{2,1,0:T(8,128)(2,1)S(1)} %shard_map.82.refs_2_), channel_id=1, source_target_pairs={{0,8},{4,20},{8,0},{12,28},{16,24},{20,4},{24,16},{28,12},{1,9},{5... | collective-permute-start | bytes 1179656 | tf_op jit(solution)/shard_map/ppermute | solution.py:38
  27.1 2.4 %shard_map.83 = (bf16[768,1536]{1,0:T(8,128)(2,1)S(1)}, bf16[768,1536]{1,0:T(8,128)(2,1)S(1)}) custom-call(s32[1]{0:T(128)} %bitcast.refs_0_, bf16[6144,1536]{1,0:T(8,128)(2,1)} %refs_6_.1, bf16[2,128,768]{2,1,0:T(8,128)(2,1)S(1)} %shard_map.82.refs_2_), custom_call_target="tpu_custom_call" | custom-call | tf_op jit(solution)/shard_map/pallas_call | solution.py:69
  29.5 3.3 %shard_map.84 = (bf16[2,128,768]{2,1,0:T(8,128)(2,1)S(1)}, bf16[2,128,768]{2,1,0:T(8,128)(2,1)S(1)}, bf16[768,1536]{1,0:T(8,128)(2,1)S(1)}, bf16[768,1536]{1,0:T(8,128)(2,1)S(1)}) custom-call(s32[1]{0:T(128)} %bitcast.refs_0_, bf16[32,1536]{1,0:T(8,128)(2,1)S(1)} %copy-done, bf16[32,1536]{1,0:T(8,128)(2,1)S(1)} %collective-permute-done.2.refs_1_.refs_2_.refs_4_, ...), custom_call_target="tpu_custom_call" | custom-call | tf_op jit(solution)/shard_map/pallas_call | solution.py:69
  33.4 1.6 %collective-permute-start.7 = (bf16[1,128,768]{2,1,0:T(8,128)(2,1)S(1)}, bf16[1,128,768]{2,1,0:T(8,128)(2,1)S(1)}, u32[]{:S(2)}, u32[]{:S(2)}) collective-permute-start(bf16[1,128,768]{2,1,0:T(8,128)(2,1)S(1)} %shard_map.85.refs_2_), channel_id=1, source_target_pairs={{0,16},{4,12},{8,24},{12,4},{16,0},{20,28},{24,8},{28,20},{1,17},{... | collective-permute-start | bytes 589832 | tf_op jit(solution)/shard_map/ppermute | solution.py:38
  35.1 1.6 %collective-permute-start.11 = (bf16[2,128,768]{2,1,0:T(8,128)(2,1)S(1)}, bf16[2,128,768]{2,1,0:T(8,128)(2,1)S(1)}, u32[]{:S(2)}, u32[]{:S(2)}) collective-permute-start(bf16[2,128,768]{2,1,0:T(8,128)(2,1)S(1)} %shard_map.86.refs_7_), channel_id=1, source_target_pairs={{0,8},{4,20},{8,0},{12,28},{16,24},{20,4},{24,16},{28,12},{1,9},{5... | collective-permute-start | bytes 1179656 | tf_op jit(solution)/shard_map/ppermute | solution.py:38
  36.7 2.4 %shard_map.87 = (bf16[1,128,768]{2,1,0:T(8,128)(2,1)S(1)}, bf16[1,128,768]{2,1,0:T(8,128)(2,1)S(1)}, bf16[768,1536]{1,0:T(8,128)(2,1)S(1)}, bf16[768,1536]{1,0:T(8,128)(2,1)S(1)}) custom-call(s32[1]{0:T(128)} %bitcast.refs_0_, bf16[32,1536]{1,0:T(8,128)(2,1)S(1)} %copy-done, bf16[32,1536]{1,0:T(8,128)(2,1)S(1)} %collective-permute-done.2.refs_1_.refs_2_.refs_4_, ...), custom_call_target="tpu_custom_call" | custom-call | tf_op jit(solution)/shard_map/pallas_call | solution.py:69
  39.1 1.8 %collective-permute-done.7.refs_3_ = bf16[1,128,768]{2,1,0:T(8,128)(2,1)S(1)} collective-permute-done((bf16[1,128,768]{2,1,0:T(8,128)(2,1)S(1)}, bf16[1,128,768]{2,1,0:T(8,128)(2,1)S(1)}, u32[]{:S(2)}, u32[]{:S(2)}) %collective-permute-start.7) | collective-permute-done | bytes 196640 | tf_op jit(solution)/shard_map/ppermute | solution.py:38
  41.2 1.6 %collective-permute-start.9 = (bf16[128,768]{1,0:T(8,128)(2,1)S(1)}, bf16[128,768]{1,0:T(8,128)(2,1)S(1)}, u32[]{:S(2)}, u32[]{:S(2)}) collective-permute-start(bf16[128,768]{1,0:T(8,128)(2,1)S(1)} %get-tuple-element.64.refs_3_.refs_0_), channel_id=1, source_target_pairs={{0,8},{4,20},{8,0},{12,28},{16,24},{20,4},{24,16},{28,12},{1,9},{5... | collective-permute-start | bytes 589832 | tf_op jit(solution)/shard_map/ppermute | solution.py:38
  44.6 1.8 %shard_map.90 = (bf16[1,128,768]{2,1,0:T(8,128)(2,1)S(1)}, bf16[1,128,768]{2,1,0:T(8,128)(2,1)S(1)}) custom-call(s32[1]{0:T(128)} %bitcast.refs_0_, bf16[32,1536]{1,0:T(8,128)(2,1)S(1)} %copy-done, bf16[32,1536]{1,0:T(8,128)(2,1)S(1)} %collective-permute-done.2.refs_1_.refs_2_.refs_4_, bf16[64,1536]{1,0:T(8,128)(2,1)S(1)} %collective-permute-done.6.refs_3_.refs_5_, ...), custom_call_target="tpu_custom_call" | custom-call | tf_op jit(solution)/shard_map/pallas_call | solution.py:69
  47.8 1.6 %collective-permute-start.12 = (bf16[256,768]{1,0:T(8,128)(2,1)S(1)}, bf16[256,768]{1,0:T(8,128)(2,1)S(1)}, u32[]{:S(2)}, u32[]{:S(2)}) collective-permute-start(bf16[256,768]{1,0:T(8,128)(2,1)S(1)} %shard_map.91.refs_2_.refs_0_), channel_id=1, source_target_pairs={{0,16},{4,12},{8,24},{12,4},{16,0},{20,28},{24,8},{28,20},{1,17},{... | collective-permute-start | bytes 1179656 | tf_op jit(solution)/shard_map/ppermute | solution.py:38
  49.8 2.0 %collective-permute-start.16 = (bf16[128,768]{1,0:T(8,128)(2,1)S(1)}, bf16[128,768]{1,0:T(8,128)(2,1)S(1)}, u32[]{:S(2)}, u32[]{:S(2)}) collective-permute-start(bf16[128,768]{1,0:T(8,128)(2,1)S(1)} %shard_map.93.refs_2_.refs_0_), channel_id=1, source_target_pairs={{0,8},{4,20},{8,0},{12,28},{16,24},{20,4},{24,16},{28,12},{1,9},{5... | collective-permute-start | bytes 589832 | tf_op jit(solution)/shard_map/ppermute | solution.py:38
  51.8 6.0 %collective-permute-done.12.refs_1_ = bf16[256,768]{1,0:T(8,128)(2,1)S(1)} collective-permute-done((bf16[256,768]{1,0:T(8,128)(2,1)S(1)}, bf16[256,768]{1,0:T(8,128)(2,1)S(1)}, u32[]{:S(2)}, u32[]{:S(2)}) %collective-permute-start.12) | collective-permute-done | bytes 393248 | tf_op jit(solution)/shard_map/ppermute | solution.py:38
  58.0 1.6 %collective-permute-start.18 = (bf16[256,768]{1,0:T(8,128)(2,1)S(1)}, bf16[256,768]{1,0:T(8,128)(2,1)S(1)}, u32[]{:S(2)}, u32[]{:S(2)}) collective-permute-start(bf16[256,768]{1,0:T(8,128)(2,1)S(1)} %shard_map.95.refs_14_.refs_0_), channel_id=1, source_target_pairs={{0,16},{4,12},{8,24},{12,4},{16,0},{20,28},{24,8},{28,20},{1,17},{... | collective-permute-start | bytes 1179656 | tf_op jit(solution)/shard_map/ppermute | solution.py:38
  60.2 9.8 %shard_map.96 = (bf16[64,1536]{1,0:T(8,128)(2,1)S(1)}, bf16[64,1536]{1,0:T(8,128)(2,1)S(1)}, bf16[6144,1536]{1,0:T(8,128)(2,1)}) custom-call(s32[1]{0:T(128)} %bitcast.refs_0_, bf16[512,768]{1,0:T(8,128)(2,1)S(1)} %shard_map.94.refs_2_.refs_1_, bf16[512,768]{1,0:T(8,128)(2,1)S(1)} %collective-permute-done.15.refs_2_, bf16[32,1536]{1,0:T(8,128)(2,1)S(1)} %copy-done, ...), custom_call_target="tpu_custom_call" | custom-call | flops 2415919104 | bytes 18874368 | tf_op jit(solution)/shard_map/pallas_call | solution.py:69
  70.3 2.1 %collective-permute-done.19.refs_1_.refs_2_ = bf16[512,768]{1,0:T(8,128)(2,1)S(1)} collective-permute-done((bf16[512,768]{1,0:T(8,128)(2,1)S(1)}, bf16[512,768]{1,0:T(8,128)(2,1)S(1)}, u32[]{:S(2)}, u32[]{:S(2)}) %collective-permute-start.19) | collective-permute-done | bytes 786464 | tf_op jit(solution)/shard_map/ppermute | solution.py:28
  72.4 6.1 %shard_map.98 = (bf16[32,1536]{1,0:T(8,128)(2,1)S(1)}, bf16[32,1536]{1,0:T(8,128)(2,1)S(1)}, bf16[32,1536]{1,0:T(8,128)(2,1)S(1)}, bf16[32,1536]{1,0:T(8,128)(2,1)S(1)}) custom-call(bf16[512,768]{1,0:T(8,128)(2,1)S(1)} %shard_map.97.refs_0_.refs_10_.refs_1_, bf16[512,768]{1,0:T(8,128)(2,1)S(1)} %collective-permute-done.19.refs_1_.refs_2_, ...), custom_call_target="tpu_custom_call" | custom-call | flops 2415919104 | bytes 18874368 | tf_op jit(solution)/shard_map/pallas_call | solution.py:69
  80.5 2.3 %collective-permute-start.22 = (bf16[32,1536]{1,0:T(8,128)(2,1)S(1)}, bf16[32,1536]{1,0:T(8,128)(2,1)S(1)}, u32[]{:S(2)}, u32[]{:S(2)}) collective-permute-start(bf16[32,1536]{1,0:T(8,128)(2,1)S(1)} %get-tuple-element.78), channel_id=1, source_target_pairs={{0,2},{1,3},{2,0},{3,1},{4,6},{5,7},{6,4},{7,5},{8,10},{9,11},{10,... | collective-permute-start | bytes 294920 | tf_op jit(solution)/shard_map/ppermute | solution.py:28
  84.0 8.8 %shard_map.100.refs_6_ = bf16[1536,6144]{1,0:T(8,128)(2,1)} custom-call(s32[1]{0:T(128)} %bitcast.refs_0_, bf16[512,768]{1,0:T(8,128)(2,1)S(1)} %shard_map.97.refs_0_.refs_10_.refs_1_, bf16[512,768]{1,0:T(8,128)(2,1)S(1)} %collective-permute-done.19.refs_1_.refs_2_, bf16[32,1536]{1,0:T(8,128)(2,1)S(1)} %copy-done.1, ...), custom_call_target="tpu_custom_call" | custom-call | flops 2415919104 | bytes 18874368 | tf_op jit(solution)/shard_map/pallas_call | solution.py:69
  (55 shorter events, 15.2 us)
Async XLA Ops:
  0.6 9.2 %collective-permute-start = (bf16[32,1536]{1,0:T(8,128)(2,1)}, bf16[32,1536]{1,0:T(8,128)(2,1)S(1)}, u32[]{:S(2)}, u32[]{:S(2)}) collective-permute-start(bf16[32,1536]{1,0:T(8,128)(2,1)} %refs_3_.3), channel_id=1, source_target_pairs={{0,2},{1,3},{2,0},{3,1},{4,6},{5,7},{6,4},{7,5},{8,10},{9,11},{10,... | collective-permute-start | bytes 294920 | tf_op jit(solution)/shard_map/ppermute | solution.py:28
  9.9 8.3 %collective-permute-start.1 = (bf16[64,1536]{1,0:T(8,128)(2,1)S(1)}, bf16[64,1536]{1,0:T(8,128)(2,1)S(1)}, u32[]{:S(2)}, u32[]{:S(2)}) collective-permute-start(bf16[64,1536]{1,0:T(8,128)(2,1)S(1)} %shard_map.76.refs_1_), channel_id=1, source_target_pairs={{0,1},{1,0},{2,3},{3,2},{4,5},{5,4},{6,7},{7,6},{8,9},{9,8},{10,11... | collective-permute-start | bytes 589832 | tf_op jit(solution)/shard_map/ppermute | solution.py:28
  11.1 6.2 %collective-permute-start.2 = (bf16[32,1536]{1,0:T(8,128)(2,1)S(1)}, bf16[32,1536]{1,0:T(8,128)(2,1)S(1)}, u32[]{:S(2)}, u32[]{:S(2)}) collective-permute-start(bf16[32,1536]{1,0:T(8,128)(2,1)S(1)} %shard_map.77.refs_2_), channel_id=1, source_target_pairs={{0,2},{1,3},{2,0},{3,1},{4,6},{5,7},{6,4},{7,5},{8,10},{9,11},{10,... | collective-permute-start | bytes 294920 | tf_op jit(solution)/shard_map/ppermute | solution.py:28
  20.5 4.9 %collective-permute-start.4 = (bf16[2,128,768]{2,1,0:T(8,128)(2,1)S(1)}, bf16[2,128,768]{2,1,0:T(8,128)(2,1)S(1)}, u32[]{:S(2)}, u32[]{:S(2)}) collective-permute-start(bf16[2,128,768]{2,1,0:T(8,128)(2,1)S(1)} %get-tuple-element.55), channel_id=1, source_target_pairs={{0,4},{4,0},{8,12},{12,8},{16,20},{20,16},{24,28},{28,24},{1,5},{5... | collective-permute-start | bytes 1179656 | tf_op jit(solution)/shard_map/ppermute | solution.py:28
  20.6 8.8 %collective-permute-start.6 = (bf16[64,1536]{1,0:T(8,128)(2,1)S(1)}, bf16[64,1536]{1,0:T(8,128)(2,1)S(1)}, u32[]{:S(2)}, u32[]{:S(2)}) collective-permute-start(bf16[64,1536]{1,0:T(8,128)(2,1)S(1)} %shard_map.79.refs_9_), channel_id=1, source_target_pairs={{0,1},{1,0},{2,3},{3,2},{4,5},{5,4},{6,7},{7,6},{8,9},{9,8},{10,11... | collective-permute-start | bytes 589832 | tf_op jit(solution)/shard_map/ppermute | solution.py:28
  25.2 7.7 %collective-permute-start.3 = (bf16[2,128,768]{2,1,0:T(8,128)(2,1)S(1)}, bf16[2,128,768]{2,1,0:T(8,128)(2,1)S(1)}, u32[]{:S(2)}, u32[]{:S(2)}) collective-permute-start(bf16[2,128,768]{2,1,0:T(8,128)(2,1)S(1)} %get-tuple-element.53.refs_2_), channel_id=1, source_target_pairs={{0,4},{4,0},{8,12},{12,8},{16,20},{20,16},{24,28},{28,24},{1,5},{5... | collective-permute-start | bytes 1179656 | tf_op jit(solution)/shard_map/ppermute | solution.py:28
  25.5 7.8 %collective-permute-start.5 = (bf16[2,128,768]{2,1,0:T(8,128)(2,1)S(1)}, bf16[2,128,768]{2,1,0:T(8,128)(2,1)S(1)}, u32[]{:S(2)}, u32[]{:S(2)}) collective-permute-start(bf16[2,128,768]{2,1,0:T(8,128)(2,1)S(1)} %shard_map.82.refs_2_), channel_id=1, source_target_pairs={{0,8},{4,20},{8,0},{12,28},{16,24},{20,4},{24,16},{28,12},{1,9},{5... | collective-permute-start | bytes 1179656 | tf_op jit(solution)/shard_map/ppermute | solution.py:38
  32.7 2.3 %collective-permute-start.8 = (bf16[2,128,768]{2,1,0:T(8,128)(2,1)S(1)}, bf16[2,128,768]{2,1,0:T(8,128)(2,1)S(1)}, u32[]{:S(2)}, u32[]{:S(2)}) collective-permute-start(bf16[2,128,768]{2,1,0:T(8,128)(2,1)S(1)} %get-tuple-element.62), channel_id=1, source_target_pairs={{0,4},{4,0},{8,12},{12,8},{16,20},{20,16},{24,28},{28,24},{1,5},{5... | collective-permute-start | bytes 1179656 | tf_op jit(solution)/shard_map/ppermute | solution.py:28
  33.4 7.5 %collective-permute-start.7 = (bf16[1,128,768]{2,1,0:T(8,128)(2,1)S(1)}, bf16[1,128,768]{2,1,0:T(8,128)(2,1)S(1)}, u32[]{:S(2)}, u32[]{:S(2)}) collective-permute-start(bf16[1,128,768]{2,1,0:T(8,128)(2,1)S(1)} %shard_map.85.refs_2_), channel_id=1, source_target_pairs={{0,16},{4,12},{8,24},{12,4},{16,0},{20,28},{24,8},{28,20},{1,17},{... | collective-permute-start | bytes 589832 | tf_op jit(solution)/shard_map/ppermute | solution.py:38
  35.1 7.8 %collective-permute-start.11 = (bf16[2,128,768]{2,1,0:T(8,128)(2,1)S(1)}, bf16[2,128,768]{2,1,0:T(8,128)(2,1)S(1)}, u32[]{:S(2)}, u32[]{:S(2)}) collective-permute-start(bf16[2,128,768]{2,1,0:T(8,128)(2,1)S(1)} %shard_map.86.refs_7_), channel_id=1, source_target_pairs={{0,8},{4,20},{8,0},{12,28},{16,24},{20,4},{24,16},{28,12},{1,9},{5... | collective-permute-start | bytes 1179656 | tf_op jit(solution)/shard_map/ppermute | solution.py:38
  39.1 3.7 %collective-permute-start.10 = (bf16[1,128,768]{2,1,0:T(8,128)(2,1)S(1)}, bf16[1,128,768]{2,1,0:T(8,128)(2,1)S(1)}, u32[]{:S(2)}, u32[]{:S(2)}) collective-permute-start(bf16[1,128,768]{2,1,0:T(8,128)(2,1)S(1)} %get-tuple-element.67), channel_id=1, source_target_pairs={{0,4},{4,0},{8,12},{12,8},{16,20},{20,16},{24,28},{28,24},{1,5},{5... | collective-permute-start | bytes 589832 | tf_op jit(solution)/shard_map/ppermute | solution.py:28
  41.2 6.7 %collective-permute-start.9 = (bf16[128,768]{1,0:T(8,128)(2,1)S(1)}, bf16[128,768]{1,0:T(8,128)(2,1)S(1)}, u32[]{:S(2)}, u32[]{:S(2)}) collective-permute-start(bf16[128,768]{1,0:T(8,128)(2,1)S(1)} %get-tuple-element.64.refs_3_.refs_0_), channel_id=1, source_target_pairs={{0,8},{4,20},{8,0},{12,28},{16,24},{20,4},{24,16},{28,12},{1,9},{5... | collective-permute-start | bytes 589832 | tf_op jit(solution)/shard_map/ppermute | solution.py:38
  43.0 6.4 %collective-permute-start.13 = (bf16[1,128,768]{2,1,0:T(8,128)(2,1)S(1)}, bf16[1,128,768]{2,1,0:T(8,128)(2,1)S(1)}, u32[]{:S(2)}, u32[]{:S(2)}) collective-permute-start(bf16[1,128,768]{2,1,0:T(8,128)(2,1)S(1)} %shard_map.89.refs_6_), channel_id=1, source_target_pairs={{0,16},{4,12},{8,24},{12,4},{16,0},{20,28},{24,8},{28,20},{1,17},{... | collective-permute-start | bytes 589832 | tf_op jit(solution)/shard_map/ppermute | solution.py:38
  46.4 3.1 %collective-permute-start.14 = (bf16[1,128,768]{2,1,0:T(8,128)(2,1)S(1)}, bf16[1,128,768]{2,1,0:T(8,128)(2,1)S(1)}, u32[]{:S(2)}, u32[]{:S(2)}) collective-permute-start(bf16[1,128,768]{2,1,0:T(8,128)(2,1)S(1)} %get-tuple-element.68.refs_2_), channel_id=1, source_target_pairs={{0,4},{4,0},{8,12},{12,8},{16,20},{20,16},{24,28},{28,24},{1,5},{5... | collective-permute-start | bytes 589832 | tf_op jit(solution)/shard_map/ppermute | solution.py:28
  47.8 9.9 %collective-permute-start.12 = (bf16[256,768]{1,0:T(8,128)(2,1)S(1)}, bf16[256,768]{1,0:T(8,128)(2,1)S(1)}, u32[]{:S(2)}, u32[]{:S(2)}) collective-permute-start(bf16[256,768]{1,0:T(8,128)(2,1)S(1)} %shard_map.91.refs_2_.refs_0_), channel_id=1, source_target_pairs={{0,16},{4,12},{8,24},{12,4},{16,0},{20,28},{24,8},{28,20},{1,17},{... | collective-permute-start | bytes 1179656 | tf_op jit(solution)/shard_map/ppermute | solution.py:38
  49.8 8.1 %collective-permute-start.16 = (bf16[128,768]{1,0:T(8,128)(2,1)S(1)}, bf16[128,768]{1,0:T(8,128)(2,1)S(1)}, u32[]{:S(2)}, u32[]{:S(2)}) collective-permute-start(bf16[128,768]{1,0:T(8,128)(2,1)S(1)} %shard_map.93.refs_2_.refs_0_), channel_id=1, source_target_pairs={{0,8},{4,20},{8,0},{12,28},{16,24},{20,4},{24,16},{28,12},{1,9},{5... | collective-permute-start | bytes 589832 | tf_op jit(solution)/shard_map/ppermute | solution.py:38
  57.9 2.4 %collective-permute-start.15 = (bf16[512,768]{1,0:T(8,128)(2,1)S(1)}, bf16[512,768]{1,0:T(8,128)(2,1)S(1)}, u32[]{:S(2)}, u32[]{:S(2)}) collective-permute-start(bf16[512,768]{1,0:T(8,128)(2,1)S(1)} %shard_map.94.refs_2_.refs_1_), channel_id=1, source_target_pairs={{0,4},{4,0},{8,12},{12,8},{16,20},{20,16},{24,28},{28,24},{1,5},{5... | collective-permute-start | bytes 2359304 | tf_op jit(solution)/shard_map/ppermute | solution.py:28
  58.0 12.0 %collective-permute-start.18 = (bf16[256,768]{1,0:T(8,128)(2,1)S(1)}, bf16[256,768]{1,0:T(8,128)(2,1)S(1)}, u32[]{:S(2)}, u32[]{:S(2)}) collective-permute-start(bf16[256,768]{1,0:T(8,128)(2,1)S(1)} %shard_map.95.refs_14_.refs_0_), channel_id=1, source_target_pairs={{0,16},{4,12},{8,24},{12,4},{16,0},{20,28},{24,8},{28,20},{1,17},{... | collective-permute-start | bytes 1179656 | tf_op jit(solution)/shard_map/ppermute | solution.py:38
  70.1 2.4 %collective-permute-start.19 = (bf16[512,768]{1,0:T(8,128)(2,1)S(1)}, bf16[512,768]{1,0:T(8,128)(2,1)S(1)}, u32[]{:S(2)}, u32[]{:S(2)}) collective-permute-start(bf16[512,768]{1,0:T(8,128)(2,1)S(1)} %shard_map.97.refs_0_.refs_10_.refs_1_), channel_id=1, source_target_pairs={{0,4},{4,0},{8,12},{12,8},{16,20},{20,16},{24,28},{28,24},{1,5},{5... | collective-permute-start | bytes 2359304 | tf_op jit(solution)/shard_map/ppermute | solution.py:28
  70.3 9.4 %collective-permute-start.17 = (bf16[64,1536]{1,0:T(8,128)(2,1)S(1)}, bf16[64,1536]{1,0:T(8,128)(2,1)S(1)}, u32[]{:S(2)}, u32[]{:S(2)}) collective-permute-start(bf16[64,1536]{1,0:T(8,128)(2,1)S(1)} %get-tuple-element.72), channel_id=1, source_target_pairs={{0,1},{1,0},{2,3},{3,2},{4,5},{5,4},{6,7},{7,6},{8,9},{9,8},{10,11... | collective-permute-start | bytes 589832 | tf_op jit(solution)/shard_map/ppermute | solution.py:28
  78.5 14.3 %collective-permute-start.21 = (bf16[32,1536]{1,0:T(8,128)(2,1)S(1)}, bf16[32,1536]{1,0:T(8,128)(2,1)S(1)}, u32[]{:S(2)}, u32[]{:S(2)}) collective-permute-start(bf16[32,1536]{1,0:T(8,128)(2,1)S(1)} %get-tuple-element.74.refs_2_), channel_id=1, source_target_pairs={{0,3},{1,2},{2,1},{3,0},{4,7},{5,6},{6,5},{7,4},{8,11},{9,10},{10,... | collective-permute-start | bytes 294920 | tf_op jit(solution)/shard_map/ppermute | solution.py:28
  79.8 13.0 %collective-permute-start.20 = (bf16[32,1536]{1,0:T(8,128)(2,1)S(1)}, bf16[32,1536]{1,0:T(8,128)(2,1)S(1)}, u32[]{:S(2)}, u32[]{:S(2)}) collective-permute-start(bf16[32,1536]{1,0:T(8,128)(2,1)S(1)} %get-tuple-element.76.refs_6_), channel_id=1, source_target_pairs={{0,2},{1,3},{2,0},{3,1},{4,6},{5,7},{6,4},{7,5},{8,10},{9,11},{10,... | collective-permute-start | bytes 294920 | tf_op jit(solution)/shard_map/ppermute | solution.py:28
  80.5 13.5 %collective-permute-start.22 = (bf16[32,1536]{1,0:T(8,128)(2,1)S(1)}, bf16[32,1536]{1,0:T(8,128)(2,1)S(1)}, u32[]{:S(2)}, u32[]{:S(2)}) collective-permute-start(bf16[32,1536]{1,0:T(8,128)(2,1)S(1)} %get-tuple-element.78), channel_id=1, source_target_pairs={{0,2},{1,3},{2,0},{3,1},{4,6},{5,7},{6,4},{7,5},{8,10},{9,11},{10,... | collective-permute-start | bytes 294920 | tf_op jit(solution)/shard_map/ppermute | solution.py:28
  82.7 11.2 %collective-permute-start.23 = (bf16[32,1536]{1,0:T(8,128)(2,1)S(1)}, bf16[32,1536]{1,0:T(8,128)(2,1)S(1)}, u32[]{:S(2)}, u32[]{:S(2)}) collective-permute-start(bf16[32,1536]{1,0:T(8,128)(2,1)S(1)} %get-tuple-element.79), channel_id=1, source_target_pairs={{0,1},{1,0},{2,3},{3,2},{4,5},{5,4},{6,7},{7,6},{8,9},{9,8},{10,11... | collective-permute-start | bytes 294920 | tf_op jit(solution)/shard_map/ppermute | solution.py:28
  (2 other events, 6.8 us)

commit v5 on v4

--- a/solution.py
+++ b/solution.py
@@ -47,7 +47,7 @@
 LAST = []
 
 
-def call(kernel, arrays, outs, flops, moved, after=(), scratch=()):
+def call(kernel, arrays, outs, flops, moved, after=(), scratch=(), in_place=False):
     unread, count = [*LAST, *after], len(arrays)
 
     def body(*refs):
@@ -72,6 +72,7 @@
         + [pl.BlockSpec(memory_space=pl.ANY)] * len(unread),
         out_specs=[specs[space] for space, value in outs],
         scratch_shapes=list(scratch),
+        input_output_aliases={count - 1: len(outs) - 1} if in_place else {},
         out_shape=[
             pltpu.VMEM(shape, dtype) if space == "vmem" else jax.ShapeDtypeStruct(shape, dtype)
             for space, (shape, dtype) in outs
@@ -224,7 +225,7 @@
     return keep, send
 
 
-def block_sum(weight, stacks, odds, cols, groups, after=()):
+def block_sum(weight, stacks, odds, cols, groups, so_far=()):
     width, by_rows, block = weight.width, weight.by_rows, weight.block
     chips = len(weight.held) // 2
     tokens = stacks[0].shape[0] // chips
@@ -237,23 +238,28 @@
 
     def kernel(*refs):
         stack_refs, part_refs, refs = refs[:n], refs[n : n + len(parts)], refs[n + len(parts) :]
-        outs, total = refs[:-1], refs[-1]
+        before, outs, total = refs[: len(so_far)], refs[len(so_far) : -1], refs[-1]
+        for ref in before:
+            total[...] = ref[...]
         for i, part in enumerate(part_refs):
             p = i % chips
             value = stack_refs[i // chips][p * tokens : (p + 1) * tokens, :]
             term = dot(value, part[...], 1, 0 if by_rows else 1)
-            total[...] = term if i == 0 else total[...] + term
+            total[...] = total[...] + term if i or before else term
+        if not groups:
+            outs[0][...] = total[...]
         for group, out in zip(groups, outs):
             for i, q in enumerate(group):
                 out[i * size : (i + 1) * size, :] = total[q * size : (q + 1) * size, :].astype(BF16)
 
     return call(
         kernel,
-        in_vmem(stacks) + in_vmem(parts),
-        [("vmem", ((len(group) * size, width), BF16)) for group in groups],
+        in_vmem(stacks) + in_vmem(parts) + in_vmem(so_far),
+        [("vmem", ((len(group) * size, width), BF16)) for group in groups]
+        or [("vmem", ((tokens, width), F32))],
         2 * tokens * width * block * chips * n,
         2 * width * block * chips * n,
-        after,
+        (),
         [pltpu.VMEM((tokens, width), F32)],
     )
 
@@ -263,21 +269,21 @@
     return [(reverse(p, weight.bits) if odd else p, odd) for odd in range(2) for p in range(chips)]
 
 
-def weight_grad(weight, stacks, shards, cols=1, groups=()):
+def weight_grad(weight, stacks, shards, odds=(0, 1), cols=1, groups=(), into=None):
     pieces, order = shards
     width, by_rows, block = weight.width, weight.by_rows, weight.block
-    chips = len(weight.held) // 2
+    chips, n = len(weight.held) // 2, len(stacks)
     tokens = stacks[0].shape[0] // chips
     halves = 2
     size = (block if by_rows else width) // halves
     keys = block_keys(weight)
-    order_of = [i for p in range(chips) for i in (p, chips + p)]
+    order_of = [odd * chips + p for p in range(chips) for odd in odds]
     parts = [weight.held[key] for key in keys] if groups else []
 
     def kernel(me_ref, *refs):
-        stack_refs, refs = refs[:2], refs[2:]
+        stack_refs, refs = refs[:n], refs[n:]
         piece_refs, refs = refs[: len(pieces)], refs[len(pieces) :]
-        part_refs, refs = refs[: len(parts)], refs[len(parts) :]
+        part_refs, refs = refs[: len(parts)], refs[len(parts) + (into is not None) :]
         sums, (grad, other, turned, ready, sent, total) = refs[: len(groups)], refs[len(groups) :]
         place(piece_refs, order, other)
         if not by_rows:
@@ -308,7 +314,7 @@
                 out = dot(turned[at, :], stack[of, :], 1, 0)
             ready[step % WRITES] = out.astype(BF16)
 
-        steps = len(keys) * halves
+        steps = len(order_of) * halves
         for step in range(steps):
             if step >= WRITES:
                 for write in writes(step - WRITES):
@@ -337,11 +343,15 @@
 
     return call(
         kernel,
-        [("smem", weight.me)] + in_vmem(stacks) + in_vmem(pieces) + in_vmem(parts),
+        [("smem", weight.me)]
+        + in_vmem(stacks)
+        + in_vmem(pieces)
+        + in_vmem(parts)
+        + ([("hbm", into)] if into is not None else []),
         [("vmem", ((len(group) * tokens // cols, width), BF16)) for group in groups]
         + [("hbm", (weight.value.shape, BF16))],
-        2 * tokens * width * block * len(keys),
-        2 * width * block * len(keys),
+        2 * tokens * width * block * len(order_of) if 1 in odds else 0,
+        2 * width * block * len(order_of) if 1 in odds else 0,
         (),
         [
             pltpu.VMEM((tokens, width), BF16),
@@ -350,6 +360,7 @@
             pltpu.SemaphoreType.DMA((WRITES, WRITE_CUTS)),
             pltpu.VMEM((tokens, width), F32),
         ],
+        into is not None,
     )
 
 
@@ -445,41 +456,46 @@
         if hop < 2:
             load(wanted[5 * hop : 5 + 3 * hop])
         order += [q ^ flip for q in order]
-    sent = joined(cot_pieces, (token_pieces[-1],))
-    cot_pieces.append(swap(sent, "col", flips[-1], cols))
-    token_shards, cot_shards = (token_pieces, order), (cot_pieces, order)
+    token_shards = token_pieces, order
+    cot_sent = joined(cot_pieces, (token_pieces[-1],))
 
     keep, sent = project(w_in, token_shards, first, wanted[8:10])
     got = other_core(sent)
     here, sent = project(w_in, token_shards, second + own, [])
     got_here, came = other_core(sent), across(added([keep, got])[0], 0, rows)
+    cot_pieces.append(swap(joined([cot_sent]), "col", flips[-1], cols))
+    cot_shards = cot_pieces, order
     load(wanted[10:12])
+    sent = one_block([(here, 0), (got_here, 0), (came, 1)])
+    terms = [(here, 1), (got_here, 1), (came, 0), (across(sent, 1, rows), 0)]
+
     keep, sent = project(w_out, cot_shards, first, wanted[12:14])
     got = other_core(sent)
-    sent = one_block([(here, 0), (got_here, 0), (came, 1)])
-    terms = [(here, 1), (got_here, 1), (came, 0), (across(sent, 1, rows), 0)]
-
+    hidden, act = activate(terms)
     came = across(added([keep, got])[0], 0, rows)
     keep, sent = project(w_out, cot_shards, second, wanted[14:])
     got = other_core(sent)
-    hidden, act = activate(terms)
+    stack = doubled(act, 0, PART_COST)
     sent = one_block([(keep, 0), (got, 0), (came, 1)])
     last = across(sent, 1, rows)
     keep, sent = project(w_out, cot_shards, own, [])
     got = other_core(sent)
-    stack = doubled(act, 0)
-    part = one_block([(came, 0), (last, 0)], F32, PART_COST)
+    part = one_block([(came, 0), (last, 0)], F32, PART_COST // 6)
     grad_hidden = activate_back(hidden, [(keep, 0), (part, 0), (got, 0)])
     stack = doubled(stack, 1)
     act = stack, other_core(stack)
-    back_stack = doubled(grad_hidden, 0, PART_COST)
+    (grad_w_out,) = weight_grad(w_out, act[:1], cot_shards, (0,))
+    back_stack = doubled(grad_hidden, 0)
 
     even, odd = range(0, cols, 2), range(1, cols, 2)
-    keep, sent, grad_w_out = weight_grad(w_out, act, cot_shards, cols, (even, odd))
+    keep, sent, grad_w_out = weight_grad(
+        w_out, act, cot_shards, (1,), cols, (even, odd), grad_w_out
+    )
     got = swap(sent, "col", 1, cols)
     back_stack = doubled(back_stack, 1)
     grad_hidden = back_stack, other_core(back_stack)
-    token_parts = block_sum(w_in, grad_hidden, (0, 1), cols, [[q] for q in range(cols)])
+    so_far = block_sum(w_in, grad_hidden[:1], (0,), cols, [])
+    token_parts = block_sum(w_in, grad_hidden[1:], (1,), cols, [[q] for q in range(cols)], so_far)
     layer_out, *sums = summed_half(keep, got, len(even))
     layer_parts = [swap(part, "col", q, cols) for part, q in zip(sums, even[1:])]
     token_parts = exchange_col(token_parts, cols)

time: 94.8 us -> 95 us (level)
  waiting for transfers between devices: 15.1 us -> 13.6 us
  starting transfers between devices: 30.8 us -> 32 us
    ppermute x16, starting transfers between devices: 17.8 us -> 21.3 us  [swap(): return lax.ppermute(value, axis, [(i, i ^ flip) for i in range(count)])]
    ppermute x8, starting transfers between devices: 13 us -> 10.8 us  [across(): return lax.ppermute(value, 'row', [(i, i ^ flips[i]) for i in range(rows)])]
    ppermute x16, waiting for transfers between devices: 5.34 us -> 3.49 us  [swap(): return lax.ppermute(value, axis, [(i, i ^ flip) for i in range(count)])]
    pallas_call x27 -> x30, Pallas kernels: 47.9 us -> 48.3 us  [call(): pl.pallas_call(body, in_specs=[specs[space] for space, value in arrays] +...]
  transfers between devices with their start and end apart: 24 -> 24, of which waited for: 10 -> 11; matrix products, arithmetic and copies ran while one was open for 0% -> 0% of each run, Pallas kernels for 47% -> 47%
where the time goes in v5:
time: 95 us; the launch traced here: 94.9 us
  Pallas kernels  48.3 us (51%)
  starting transfers between devices  32 us (34%)
  waiting for transfers between devices  13.6 us (14%)
    pallas_call x30, Pallas kernels, call(): pl.pallas_call(body, in_specs=[specs[space] for space, value in arrays] +...  48.3 us
    ppermute x16, starting transfers between devices, swap(): return lax.ppermute(value, axis, [(i, i ^ flip) for i in range(count)])  21.3 us
    ppermute x8, starting transfers between devices, across(): return lax.ppermute(value, 'row', [(i, i ^ flips[i]) for i in range(rows)])  10.8 us
    ppermute x8, waiting for transfers between devices, across(): return lax.ppermute(value, 'row', [(i, i ^ flips[i]) for i in range(rows)])  10.1 us
    ppermute x16, waiting for transfers between devices, swap(): return lax.ppermute(value, axis, [(i, i ^ flip) for i in range(count)])  3.49 us
  transfers between devices with their start and end apart: 24, of which 11 were waited for; matrix products, arithmetic and copies ran while one was open for 0% of the time, Pallas kernels for 47%

profile of v5, /device:TPU:0, one launch (start us, length us, event | category | flops | bytes accessed | tf_op | source)
XLA Modules:
  0.0 94.9 jit_solution(16214998231026498399)
XLA Ops:
  0.6 4.1 %collective-permute-start = (bf16[32,1536]{1,0:T(8,128)(2,1)}, bf16[32,1536]{1,0:T(8,128)(2,1)S(1)}, u32[]{:S(2)}, u32[]{:S(2)}) collective-permute-start(bf16[32,1536]{1,0:T(8,128)(2,1)} %refs_3_.3), channel_id=1, source_target_pairs={{0,2},{1,3},{2,0},{3,1},{4,6},{5,7},{6,4},{7,5},{8,10},{9,11},{10,... | collective-permute-start | bytes 294920 | tf_op jit(solution)/shard_map/ppermute | solution.py:28
  4.7 4.6 %shard_map.75 = (bf16[1536,768]{1,0:T(8,128)(2,1)S(1)}, bf16[1536,768]{1,0:T(8,128)(2,1)S(1)}, bf16[1536,768]{1,0:T(8,128)(2,1)S(1)}, bf16[1536,768]{1,0:T(8,128)(2,1)S(1)}, bf16[1536,768]{1,0:T(8,128)(2,1)S(1)}) custom-call(s32[1]{0:T(128)} %bitcast.refs_0_, bf16[1536,6144]{1,0:T(8,128)(2,1)} %refs_1_.9), custom_call_target="tpu_custom_call" | custom-call | tf_op jit(solution)/shard_map/pallas_call | solution.py:69
  11.1 3.0 %collective-permute-start.2 = (bf16[32,1536]{1,0:T(8,128)(2,1)S(1)}, bf16[32,1536]{1,0:T(8,128)(2,1)S(1)}, u32[]{:S(2)}, u32[]{:S(2)}) collective-permute-start(bf16[32,1536]{1,0:T(8,128)(2,1)S(1)} %shard_map.77.refs_2_), channel_id=1, source_target_pairs={{0,2},{1,3},{2,0},{3,1},{4,6},{5,7},{6,4},{7,5},{8,10},{9,11},{10,... | collective-permute-start | bytes 294920 | tf_op jit(solution)/shard_map/ppermute | solution.py:28
  14.1 3.1 %shard_map.78 = (bf16[1536,768]{1,0:T(8,128)(2,1)S(1)}, bf16[1536,768]{1,0:T(8,128)(2,1)S(1)}, bf16[1536,768]{1,0:T(8,128)(2,1)S(1)}) custom-call(s32[1]{0:T(128)} %bitcast.refs_0_, bf16[1536,6144]{1,0:T(8,128)(2,1)} %refs_1_.9, bf16[32,1536]{1,0:T(8,128)(2,1)S(1)} %shard_map.77.refs_2_), custom_call_target="tpu_custom_call" | custom-call | tf_op jit(solution)/shard_map/pallas_call | solution.py:69
  18.1 2.4 %shard_map.80 = (bf16[2,128,768]{2,1,0:T(8,128)(2,1)S(1)}, bf16[2,128,768]{2,1,0:T(8,128)(2,1)S(1)}, bf16[768,1536]{1,0:T(8,128)(2,1)S(1)}, bf16[768,1536]{1,0:T(8,128)(2,1)S(1)}) custom-call(s32[1]{0:T(128)} %bitcast.refs_0_, bf16[32,1536]{1,0:T(8,128)(2,1)S(1)} %copy-done.1, bf16[32,1536]{1,0:T(8,128)(2,1)S(1)} %collective-permute-done.refs_1_.refs_2_.refs_4_, ...), custom_call_target="tpu_custom_call" | custom-call | tf_op jit(solution)/shard_map/pallas_call | solution.py:69
  24.1 3.3 %collective-permute-start.7 = (bf16[64,1536]{1,0:T(8,128)(2,1)S(1)}, bf16[64,1536]{1,0:T(8,128)(2,1)S(1)}, u32[]{:S(2)}, u32[]{:S(2)}) collective-permute-start(bf16[64,1536]{1,0:T(8,128)(2,1)S(1)} %shard_map.83.refs_2_), channel_id=1, source_target_pairs={{0,1},{1,0},{2,3},{3,2},{4,5},{5,4},{6,7},{7,6},{8,9},{9,8},{10,11... | collective-permute-start | bytes 589832 | tf_op jit(solution)/shard_map/ppermute | solution.py:28
  27.4 2.4 %shard_map.84 = (bf16[768,1536]{1,0:T(8,128)(2,1)S(1)}, bf16[768,1536]{1,0:T(8,128)(2,1)S(1)}) custom-call(s32[1]{0:T(128)} %bitcast.refs_0_, bf16[6144,1536]{1,0:T(8,128)(2,1)} %refs_6_.1, bf16[64,1536]{1,0:T(8,128)(2,1)S(1)} %shard_map.83.refs_2_), custom_call_target="tpu_custom_call" | custom-call | tf_op jit(solution)/shard_map/pallas_call | solution.py:69
  32.3 3.2 %shard_map.86 = (bf16[2,128,768]{2,1,0:T(8,128)(2,1)S(1)}, bf16[2,128,768]{2,1,0:T(8,128)(2,1)S(1)}, bf16[768,1536]{1,0:T(8,128)(2,1)S(1)}, bf16[768,1536]{1,0:T(8,128)(2,1)S(1)}) custom-call(s32[1]{0:T(128)} %bitcast.refs_0_, bf16[32,1536]{1,0:T(8,128)(2,1)S(1)} %copy-done, bf16[32,1536]{1,0:T(8,128)(2,1)S(1)} %collective-permute-done.2.refs_1_.refs_2_.refs_3_.refs_4_, ...), custom_call_target="tpu_custom_call" | custom-call | tf_op jit(solution)/shard_map/pallas_call | solution.py:69
  38.9 2.4 %shard_map.89 = (bf16[1,128,768]{2,1,0:T(8,128)(2,1)S(1)}, bf16[1,128,768]{2,1,0:T(8,128)(2,1)S(1)}, bf16[768,1536]{1,0:T(8,128)(2,1)S(1)}, bf16[768,1536]{1,0:T(8,128)(2,1)S(1)}) custom-call(s32[1]{0:T(128)} %bitcast.refs_0_, bf16[32,1536]{1,0:T(8,128)(2,1)S(1)} %copy-done, bf16[32,1536]{1,0:T(8,128)(2,1)S(1)} %collective-permute-done.2.refs_1_.refs_2_.refs_3_.refs_4_, ...), custom_call_target="tpu_custom_call" | custom-call | tf_op jit(solution)/shard_map/pallas_call | solution.py:69
  43.7 4.7 %collective-permute-done.12.refs_2_.refs_0_ = bf16[2,128,768]{2,1,0:T(8,128)(2,1)S(1)} collective-permute-done((bf16[2,128,768]{2,1,0:T(8,128)(2,1)S(1)}, bf16[2,128,768]{2,1,0:T(8,128)(2,1)S(1)}, u32[]{:S(2)}, u32[]{:S(2)}) %collective-permute-start.12) | collective-permute-done | bytes 393248 | tf_op jit(solution)/shard_map/ppermute | solution.py:38
  48.5 1.4 %collective-permute-start.13 = (bf16[1,128,768]{2,1,0:T(8,128)(2,1)S(1)}, bf16[1,128,768]{2,1,0:T(8,128)(2,1)S(1)}, u32[]{:S(2)}, u32[]{:S(2)}) collective-permute-start(bf16[1,128,768]{2,1,0:T(8,128)(2,1)S(1)} %shard_map.91.refs_6_), channel_id=1, source_target_pairs={{0,16},{4,12},{8,24},{12,4},{16,0},{20,28},{24,8},{28,20},{1,17},{... | collective-permute-start | bytes 589832 | tf_op jit(solution)/shard_map/ppermute | solution.py:38
  50.0 1.8 %shard_map.92 = (bf16[1,128,768]{2,1,0:T(8,128)(2,1)S(1)}, bf16[1,128,768]{2,1,0:T(8,128)(2,1)S(1)}) custom-call(s32[1]{0:T(128)} %bitcast.refs_0_, bf16[32,1536]{1,0:T(8,128)(2,1)S(1)} %copy-done, bf16[32,1536]{1,0:T(8,128)(2,1)S(1)} %collective-permute-done.2.refs_1_.refs_2_.refs_3_.refs_4_, ...), custom_call_target="tpu_custom_call" | custom-call | tf_op jit(solution)/shard_map/pallas_call | solution.py:69
  51.9 2.4 %collective-permute-done.13.refs_1_ = bf16[1,128,768]{2,1,0:T(8,128)(2,1)S(1)} collective-permute-done((bf16[1,128,768]{2,1,0:T(8,128)(2,1)S(1)}, bf16[1,128,768]{2,1,0:T(8,128)(2,1)S(1)}, u32[]{:S(2)}, u32[]{:S(2)}) %collective-permute-start.13) | collective-permute-done | bytes 196640 | tf_op jit(solution)/shard_map/ppermute | solution.py:38
  54.8 1.4 %collective-permute-start.16 = (bf16[128,768]{1,0:T(8,128)(2,1)S(1)}, bf16[128,768]{1,0:T(8,128)(2,1)S(1)}, u32[]{:S(2)}, u32[]{:S(2)}) collective-permute-start(bf16[128,768]{1,0:T(8,128)(2,1)S(1)} %shard_map.94.refs_2_.refs_0_), channel_id=1, source_target_pairs={{0,8},{4,20},{8,0},{12,28},{16,24},{20,4},{24,16},{28,12},{1,9},{5... | collective-permute-start | bytes 589832 | tf_op jit(solution)/shard_map/ppermute | solution.py:38
  56.2 4.2 %shard_map.96.refs_2_.refs_14_ = bf16[6144,1536]{1,0:T(8,128)(2,1)} custom-call(s32[1]{0:T(128)} %bitcast.refs_0_, bf16[512,768]{1,0:T(8,128)(2,1)S(1)} %shard_map.95.refs_1_.refs_5_, bf16[32,1536]{1,0:T(8,128)(2,1)S(1)} %copy-done, bf16[32,1536]{1,0:T(8,128)(2,1)S(1)} %collective-permute-done.2.refs_1_.refs_2_.refs_3_.refs_4_, ...), custom_call_target="tpu_custom_call" | custom-call | tf_op jit(solution)/shard_map/pallas_call | solution.py:69
  60.6 1.5 %collective-permute-start.18 = (bf16[256,768]{1,0:T(8,128)(2,1)S(1)}, bf16[256,768]{1,0:T(8,128)(2,1)S(1)}, u32[]{:S(2)}, u32[]{:S(2)}) collective-permute-start(bf16[256,768]{1,0:T(8,128)(2,1)S(1)} %shard_map.97.refs_15_.refs_0_), channel_id=1, source_target_pairs={{0,16},{4,12},{8,24},{12,4},{16,0},{20,28},{24,8},{28,20},{1,17},{... | collective-permute-start | bytes 1179656 | tf_op jit(solution)/shard_map/ppermute | solution.py:38
  62.1 5.8 %shard_map.98 = (bf16[64,1536]{1,0:T(8,128)(2,1)S(1)}, bf16[64,1536]{1,0:T(8,128)(2,1)S(1)}, bf16[6144,1536]{1,0:T(8,128)(2,1)}) custom-call(s32[1]{0:T(128)} %bitcast.refs_0_, bf16[512,768]{1,0:T(8,128)(2,1)S(1)} %shard_map.95.refs_1_.refs_5_, bf16[512,768]{1,0:T(8,128)(2,1)S(1)} %collective-permute-done.15.refs_2_, ...), custom_call_target="tpu_custom_call", output_to_operand_aliasing={{2}: (14, {})} | custom-call | flops 1207959552 | bytes 9437184 | tf_op jit(solution)/shard_map/pallas_call | solution.py:69
  68.5 3.3 %collective-permute-start.17 = (bf16[64,1536]{1,0:T(8,128)(2,1)S(1)}, bf16[64,1536]{1,0:T(8,128)(2,1)S(1)}, u32[]{:S(2)}, u32[]{:S(2)}) collective-permute-start(bf16[64,1536]{1,0:T(8,128)(2,1)S(1)} %get-tuple-element.72), channel_id=1, source_target_pairs={{0,1},{1,0},{2,3},{3,2},{4,5},{5,4},{6,7},{7,6},{8,9},{9,8},{10,11... | collective-permute-start | bytes 589832 | tf_op jit(solution)/shard_map/ppermute | solution.py:28
  71.8 3.1 %shard_map.100.refs_5_.refs_6_ = f32[128,1536]{1,0:T(8,128)S(1)} custom-call(bf16[512,768]{1,0:T(8,128)(2,1)S(1)} %shard_map.99.refs_0_.refs_5_.refs_1_, bf16[1536,768]{1,0:T(8,128)(2,1)S(1)} %get-tuple-element.46.refs_2_.refs_7_.refs_1_, bf16[1536,768]{1,0:T(8,128)(2,1)S(1)} %get-tuple-element.49.refs_6_.refs_2_, ...), custom_call_target="tpu_custom_call" | custom-call | flops 1207959552 | bytes 9437184 | tf_op jit(solution)/shard_map/pallas_call | solution.py:69
  74.9 3.1 %shard_map.101 = (bf16[32,1536]{1,0:T(8,128)(2,1)S(1)}, bf16[32,1536]{1,0:T(8,128)(2,1)S(1)}, bf16[32,1536]{1,0:T(8,128)(2,1)S(1)}, bf16[32,1536]{1,0:T(8,128)(2,1)S(1)}) custom-call(bf16[512,768]{1,0:T(8,128)(2,1)S(1)} %collective-permute-done.19.refs_0_.refs_2_, bf16[1536,768]{1,0:T(8,128)(2,1)S(1)} %get-tuple-element.44.refs_5_.refs_1_, ...), custom_call_target="tpu_custom_call" | custom-call | flops 1207959552 | bytes 9437184 | tf_op jit(solution)/shard_map/pallas_call | solution.py:69
  78.0 1.8 %collective-permute-start.22 = (bf16[32,1536]{1,0:T(8,128)(2,1)S(1)}, bf16[32,1536]{1,0:T(8,128)(2,1)S(1)}, u32[]{:S(2)}, u32[]{:S(2)}) collective-permute-start(bf16[32,1536]{1,0:T(8,128)(2,1)S(1)} %get-tuple-element.78), channel_id=1, source_target_pairs={{0,2},{1,3},{2,0},{3,1},{4,6},{5,7},{6,4},{7,5},{8,10},{9,11},{10,... | collective-permute-start | bytes 294920 | tf_op jit(solution)/shard_map/ppermute | solution.py:28
  79.8 2.6 %collective-permute-start.21 = (bf16[32,1536]{1,0:T(8,128)(2,1)S(1)}, bf16[32,1536]{1,0:T(8,128)(2,1)S(1)}, u32[]{:S(2)}, u32[]{:S(2)}) collective-permute-start(bf16[32,1536]{1,0:T(8,128)(2,1)S(1)} %get-tuple-element.74.refs_2_), channel_id=1, source_target_pairs={{0,3},{1,2},{2,1},{3,0},{4,7},{5,6},{6,5},{7,4},{8,11},{9,10},{10,... | collective-permute-start | bytes 294920 | tf_op jit(solution)/shard_map/ppermute | solution.py:28
  83.4 8.8 %shard_map.103.refs_6_ = bf16[1536,6144]{1,0:T(8,128)(2,1)} custom-call(s32[1]{0:T(128)} %bitcast.refs_0_, bf16[512,768]{1,0:T(8,128)(2,1)S(1)} %shard_map.99.refs_0_.refs_5_.refs_1_, bf16[512,768]{1,0:T(8,128)(2,1)S(1)} %collective-permute-done.19.refs_0_.refs_2_, bf16[32,1536]{1,0:T(8,128)(2,1)S(1)} %copy-done.1, ...), custom_call_target="tpu_custom_call" | custom-call | flops 2415919104 | bytes 18874368 | tf_op jit(solution)/shard_map/pallas_call | solution.py:69
  92.3 1.9 %collective-permute-done.20.refs_1_ = bf16[32,1536]{1,0:T(8,128)(2,1)S(1)} collective-permute-done((bf16[32,1536]{1,0:T(8,128)(2,1)S(1)}, bf16[32,1536]{1,0:T(8,128)(2,1)S(1)}, u32[]{:S(2)}, u32[]{:S(2)}) %collective-permute-start.20) | collective-permute-done | bytes 98336 | tf_op jit(solution)/shard_map/ppermute | solution.py:28
  (58 shorter events, 17.4 us)
Async XLA Ops:
  0.6 9.2 %collective-permute-start = (bf16[32,1536]{1,0:T(8,128)(2,1)}, bf16[32,1536]{1,0:T(8,128)(2,1)S(1)}, u32[]{:S(2)}, u32[]{:S(2)}) collective-permute-start(bf16[32,1536]{1,0:T(8,128)(2,1)} %refs_3_.3), channel_id=1, source_target_pairs={{0,2},{1,3},{2,0},{3,1},{4,6},{5,7},{6,4},{7,5},{8,10},{9,11},{10,... | collective-permute-start | bytes 294920 | tf_op jit(solution)/shard_map/ppermute | solution.py:28
  9.9 8.3 %collective-permute-start.1 = (bf16[64,1536]{1,0:T(8,128)(2,1)S(1)}, bf16[64,1536]{1,0:T(8,128)(2,1)S(1)}, u32[]{:S(2)}, u32[]{:S(2)}) collective-permute-start(bf16[64,1536]{1,0:T(8,128)(2,1)S(1)} %shard_map.76.refs_1_), channel_id=1, source_target_pairs={{0,1},{1,0},{2,3},{3,2},{4,5},{5,4},{6,7},{7,6},{8,9},{9,8},{10,11... | collective-permute-start | bytes 589832 | tf_op jit(solution)/shard_map/ppermute | solution.py:28
  11.1 6.2 %collective-permute-start.2 = (bf16[32,1536]{1,0:T(8,128)(2,1)S(1)}, bf16[32,1536]{1,0:T(8,128)(2,1)S(1)}, u32[]{:S(2)}, u32[]{:S(2)}) collective-permute-start(bf16[32,1536]{1,0:T(8,128)(2,1)S(1)} %shard_map.77.refs_2_), channel_id=1, source_target_pairs={{0,2},{1,3},{2,0},{3,1},{4,6},{5,7},{6,4},{7,5},{8,10},{9,11},{10,... | collective-permute-start | bytes 294920 | tf_op jit(solution)/shard_map/ppermute | solution.py:28
  20.5 2.0 %collective-permute-start.4 = (bf16[2,128,768]{2,1,0:T(8,128)(2,1)S(1)}, bf16[2,128,768]{2,1,0:T(8,128)(2,1)S(1)}, u32[]{:S(2)}, u32[]{:S(2)}) collective-permute-start(bf16[2,128,768]{2,1,0:T(8,128)(2,1)S(1)} %get-tuple-element.55), channel_id=1, source_target_pairs={{0,4},{4,0},{8,12},{12,8},{16,20},{20,16},{24,28},{28,24},{1,5},{5... | collective-permute-start | bytes 1179656 | tf_op jit(solution)/shard_map/ppermute | solution.py:28
  22.0 7.8 %collective-permute-start.3 = (bf16[2,128,768]{2,1,0:T(8,128)(2,1)S(1)}, bf16[2,128,768]{2,1,0:T(8,128)(2,1)S(1)}, u32[]{:S(2)}, u32[]{:S(2)}) collective-permute-start(bf16[2,128,768]{2,1,0:T(8,128)(2,1)S(1)} %get-tuple-element.53.refs_2_), channel_id=1, source_target_pairs={{0,4},{4,0},{8,12},{12,8},{16,20},{20,16},{24,28},{28,24},{1,5},{5... | collective-permute-start | bytes 1179656 | tf_op jit(solution)/shard_map/ppermute | solution.py:28
  22.7 7.8 %collective-permute-start.5 = (bf16[2,128,768]{2,1,0:T(8,128)(2,1)S(1)}, bf16[2,128,768]{2,1,0:T(8,128)(2,1)S(1)}, u32[]{:S(2)}, u32[]{:S(2)}) collective-permute-start(bf16[2,128,768]{2,1,0:T(8,128)(2,1)S(1)} %shard_map.82.refs_1_), channel_id=1, source_target_pairs={{0,8},{4,20},{8,0},{12,28},{16,24},{20,4},{24,16},{28,12},{1,9},{5... | collective-permute-start | bytes 1179656 | tf_op jit(solution)/shard_map/ppermute | solution.py:38
  24.1 8.2 %collective-permute-start.7 = (bf16[64,1536]{1,0:T(8,128)(2,1)S(1)}, bf16[64,1536]{1,0:T(8,128)(2,1)S(1)}, u32[]{:S(2)}, u32[]{:S(2)}) collective-permute-start(bf16[64,1536]{1,0:T(8,128)(2,1)S(1)} %shard_map.83.refs_2_), channel_id=1, source_target_pairs={{0,1},{1,0},{2,3},{3,2},{4,5},{5,4},{6,7},{7,6},{8,9},{9,8},{10,11... | collective-permute-start | bytes 589832 | tf_op jit(solution)/shard_map/ppermute | solution.py:28
  30.6 5.7 %collective-permute-start.6 = (bf16[1,128,768]{2,1,0:T(8,128)(2,1)S(1)}, bf16[1,128,768]{2,1,0:T(8,128)(2,1)S(1)}, u32[]{:S(2)}, u32[]{:S(2)}) collective-permute-start(bf16[1,128,768]{2,1,0:T(8,128)(2,1)S(1)} %shard_map.85.refs_9_), channel_id=1, source_target_pairs={{0,16},{4,12},{8,24},{12,4},{16,0},{20,28},{24,8},{28,20},{1,17},{... | collective-permute-start | bytes 589832 | tf_op jit(solution)/shard_map/ppermute | solution.py:38
  35.5 2.4 %collective-permute-start.9 = (bf16[2,128,768]{2,1,0:T(8,128)(2,1)S(1)}, bf16[2,128,768]{2,1,0:T(8,128)(2,1)S(1)}, u32[]{:S(2)}, u32[]{:S(2)}) collective-permute-start(bf16[2,128,768]{2,1,0:T(8,128)(2,1)S(1)} %get-tuple-element.63), channel_id=1, source_target_pairs={{0,4},{4,0},{8,12},{12,8},{16,20},{20,16},{24,28},{28,24},{1,5},{5... | collective-permute-start | bytes 1179656 | tf_op jit(solution)/shard_map/ppermute | solution.py:28
  36.6 5.7 %collective-permute-start.8 = (bf16[128,768]{1,0:T(8,128)(2,1)S(1)}, bf16[128,768]{1,0:T(8,128)(2,1)S(1)}, u32[]{:S(2)}, u32[]{:S(2)}) collective-permute-start(bf16[128,768]{1,0:T(8,128)(2,1)S(1)} %get-tuple-element.60.refs_2_.refs_0_), channel_id=1, source_target_pairs={{0,8},{4,20},{8,0},{12,28},{16,24},{20,4},{24,16},{28,12},{1,9},{5... | collective-permute-start | bytes 589832 | tf_op jit(solution)/shard_map/ppermute | solution.py:38
  38.0 10.4 %collective-permute-start.12 = (bf16[2,128,768]{2,1,0:T(8,128)(2,1)S(1)}, bf16[2,128,768]{2,1,0:T(8,128)(2,1)S(1)}, u32[]{:S(2)}, u32[]{:S(2)}) collective-permute-start(bf16[2,128,768]{2,1,0:T(8,128)(2,1)S(1)} %shard_map.88.refs_7_), channel_id=1, source_target_pairs={{0,8},{4,20},{8,0},{12,28},{16,24},{20,4},{24,16},{28,12},{1,9},{5... | collective-permute-start | bytes 1179656 | tf_op jit(solution)/shard_map/ppermute | solution.py:38
  41.2 2.5 %collective-permute-start.11 = (bf16[1,128,768]{2,1,0:T(8,128)(2,1)S(1)}, bf16[1,128,768]{2,1,0:T(8,128)(2,1)S(1)}, u32[]{:S(2)}, u32[]{:S(2)}) collective-permute-start(bf16[1,128,768]{2,1,0:T(8,128)(2,1)S(1)} %get-tuple-element.68), channel_id=1, source_target_pairs={{0,4},{4,0},{8,12},{12,8},{16,20},{20,16},{24,28},{28,24},{1,5},{5... | collective-permute-start | bytes 589832 | tf_op jit(solution)/shard_map/ppermute | solution.py:28
  42.3 12.3 %collective-permute-start.10 = (bf16[256,768]{1,0:T(8,128)(2,1)S(1)}, bf16[256,768]{1,0:T(8,128)(2,1)S(1)}, u32[]{:S(2)}, u32[]{:S(2)}) collective-permute-start(bf16[256,768]{1,0:T(8,128)(2,1)S(1)} %shard_map.90.refs_3_.refs_0_), channel_id=1, source_target_pairs={{0,16},{4,12},{8,24},{12,4},{16,0},{20,28},{24,8},{28,20},{1,17},{... | collective-permute-start | bytes 1179656 | tf_op jit(solution)/shard_map/ppermute | solution.py:38
  48.5 5.7 %collective-permute-start.13 = (bf16[1,128,768]{2,1,0:T(8,128)(2,1)S(1)}, bf16[1,128,768]{2,1,0:T(8,128)(2,1)S(1)}, u32[]{:S(2)}, u32[]{:S(2)}) collective-permute-start(bf16[1,128,768]{2,1,0:T(8,128)(2,1)S(1)} %shard_map.91.refs_6_), channel_id=1, source_target_pairs={{0,16},{4,12},{8,24},{12,4},{16,0},{20,28},{24,8},{28,20},{1,17},{... | collective-permute-start | bytes 589832 | tf_op jit(solution)/shard_map/ppermute | solution.py:38
  51.8 2.5 %collective-permute-start.14 = (bf16[1,128,768]{2,1,0:T(8,128)(2,1)S(1)}, bf16[1,128,768]{2,1,0:T(8,128)(2,1)S(1)}, u32[]{:S(2)}, u32[]{:S(2)}) collective-permute-start(bf16[1,128,768]{2,1,0:T(8,128)(2,1)S(1)} %get-tuple-element.70.refs_2_), channel_id=1, source_target_pairs={{0,4},{4,0},{8,12},{12,8},{16,20},{20,16},{24,28},{28,24},{1,5},{5... | collective-permute-start | bytes 589832 | tf_op jit(solution)/shard_map/ppermute | solution.py:28
  54.7 7.4 %collective-permute-start.15 = (bf16[512,768]{1,0:T(8,128)(2,1)S(1)}, bf16[512,768]{1,0:T(8,128)(2,1)S(1)}, u32[]{:S(2)}, u32[]{:S(2)}) collective-permute-start(bf16[512,768]{1,0:T(8,128)(2,1)S(1)} %shard_map.95.refs_1_.refs_5_), channel_id=1, source_target_pairs={{0,4},{4,0},{8,12},{12,8},{16,20},{20,16},{24,28},{28,24},{1,5},{5... | collective-permute-start | bytes 2359304 | tf_op jit(solution)/shard_map/ppermute | solution.py:28
  54.8 5.7 %collective-permute-start.16 = (bf16[128,768]{1,0:T(8,128)(2,1)S(1)}, bf16[128,768]{1,0:T(8,128)(2,1)S(1)}, u32[]{:S(2)}, u32[]{:S(2)}) collective-permute-start(bf16[128,768]{1,0:T(8,128)(2,1)S(1)} %shard_map.94.refs_2_.refs_0_), channel_id=1, source_target_pairs={{0,8},{4,20},{8,0},{12,28},{16,24},{20,4},{24,16},{28,12},{1,9},{5... | collective-permute-start | bytes 589832 | tf_op jit(solution)/shard_map/ppermute | solution.py:38
  60.6 7.8 %collective-permute-start.18 = (bf16[256,768]{1,0:T(8,128)(2,1)S(1)}, bf16[256,768]{1,0:T(8,128)(2,1)S(1)}, u32[]{:S(2)}, u32[]{:S(2)}) collective-permute-start(bf16[256,768]{1,0:T(8,128)(2,1)S(1)} %shard_map.97.refs_15_.refs_0_), channel_id=1, source_target_pairs={{0,16},{4,12},{8,24},{12,4},{16,0},{20,28},{24,8},{28,20},{1,17},{... | collective-permute-start | bytes 1179656 | tf_op jit(solution)/shard_map/ppermute | solution.py:38
  68.5 6.5 %collective-permute-start.19 = (bf16[512,768]{1,0:T(8,128)(2,1)S(1)}, bf16[512,768]{1,0:T(8,128)(2,1)S(1)}, u32[]{:S(2)}, u32[]{:S(2)}) collective-permute-start(bf16[512,768]{1,0:T(8,128)(2,1)S(1)} %shard_map.99.refs_0_.refs_5_.refs_1_), channel_id=1, source_target_pairs={{0,4},{4,0},{8,12},{12,8},{16,20},{20,16},{24,28},{28,24},{1,5},{5... | collective-permute-start | bytes 2359304 | tf_op jit(solution)/shard_map/ppermute | solution.py:28
  68.5 14.0 %collective-permute-start.17 = (bf16[64,1536]{1,0:T(8,128)(2,1)S(1)}, bf16[64,1536]{1,0:T(8,128)(2,1)S(1)}, u32[]{:S(2)}, u32[]{:S(2)}) collective-permute-start(bf16[64,1536]{1,0:T(8,128)(2,1)S(1)} %get-tuple-element.72), channel_id=1, source_target_pairs={{0,1},{1,0},{2,3},{3,2},{4,5},{5,4},{6,7},{7,6},{8,9},{9,8},{10,11... | collective-permute-start | bytes 589832 | tf_op jit(solution)/shard_map/ppermute | solution.py:28
  78.0 14.2 %collective-permute-start.22 = (bf16[32,1536]{1,0:T(8,128)(2,1)S(1)}, bf16[32,1536]{1,0:T(8,128)(2,1)S(1)}, u32[]{:S(2)}, u32[]{:S(2)}) collective-permute-start(bf16[32,1536]{1,0:T(8,128)(2,1)S(1)} %get-tuple-element.78), channel_id=1, source_target_pairs={{0,2},{1,3},{2,0},{3,1},{4,6},{5,7},{6,4},{7,5},{8,10},{9,11},{10,... | collective-permute-start | bytes 294920 | tf_op jit(solution)/shard_map/ppermute | solution.py:28
  79.8 12.4 %collective-permute-start.23 = (bf16[32,1536]{1,0:T(8,128)(2,1)S(1)}, bf16[32,1536]{1,0:T(8,128)(2,1)S(1)}, u32[]{:S(2)}, u32[]{:S(2)}) collective-permute-start(bf16[32,1536]{1,0:T(8,128)(2,1)S(1)} %get-tuple-element.79), channel_id=1, source_target_pairs={{0,1},{1,0},{2,3},{3,2},{4,5},{5,4},{6,7},{7,6},{8,9},{9,8},{10,11... | collective-permute-start | bytes 294920 | tf_op jit(solution)/shard_map/ppermute | solution.py:28
  79.8 14.3 %collective-permute-start.21 = (bf16[32,1536]{1,0:T(8,128)(2,1)S(1)}, bf16[32,1536]{1,0:T(8,128)(2,1)S(1)}, u32[]{:S(2)}, u32[]{:S(2)}) collective-permute-start(bf16[32,1536]{1,0:T(8,128)(2,1)S(1)} %get-tuple-element.74.refs_2_), channel_id=1, source_target_pairs={{0,3},{1,2},{2,1},{3,0},{4,7},{5,6},{6,5},{7,4},{8,11},{9,10},{10,... | collective-permute-start | bytes 294920 | tf_op jit(solution)/shard_map/ppermute | solution.py:28
  82.5 11.6 %collective-permute-start.20 = (bf16[32,1536]{1,0:T(8,128)(2,1)S(1)}, bf16[32,1536]{1,0:T(8,128)(2,1)S(1)}, u32[]{:S(2)}, u32[]{:S(2)}) collective-permute-start(bf16[32,1536]{1,0:T(8,128)(2,1)S(1)} %get-tuple-element.76.refs_6_), channel_id=1, source_target_pairs={{0,2},{1,3},{2,0},{3,1},{4,6},{5,7},{6,4},{7,5},{8,10},{9,11},{10,... | collective-permute-start | bytes 294920 | tf_op jit(solution)/shard_map/ppermute | solution.py:28
  (2 other events, 6.8 us)

commit v6 on v5

--- a/solution.py
+++ b/solution.py
@@ -421,7 +421,7 @@
         refs[-1][...] = gelu_back(hidden_ref[...], block_of(terms)(refs))
 
     arrays = [hidden] + [array for array, block in terms]
-    return call(kernel, in_vmem(arrays), [("vmem", (hidden.shape, BF16))], 0, 0)[0]
+    return call(kernel, in_vmem(arrays), [("vmem", (hidden.shape, BF16))], PART_COST, 0)[0]
 
 
 def exchange_col(parts, cols):
@@ -475,22 +475,18 @@
     came = across(added([keep, got])[0], 0, rows)
     keep, sent = project(w_out, cot_shards, second, wanted[14:])
     got = other_core(sent)
-    stack = doubled(act, 0, PART_COST)
+    own_keep, sent = project(w_out, cot_shards, own, [])
+    own_got = other_core(sent)
     sent = one_block([(keep, 0), (got, 0), (came, 1)])
     last = across(sent, 1, rows)
-    keep, sent = project(w_out, cot_shards, own, [])
-    got = other_core(sent)
-    part = one_block([(came, 0), (last, 0)], F32, PART_COST // 6)
-    grad_hidden = activate_back(hidden, [(keep, 0), (part, 0), (got, 0)])
+    stack = doubled(act, 0)
+    grad_hidden = activate_back(hidden, [(own_keep, 0), (own_got, 0), (came, 0), (last, 0)])
     stack = doubled(stack, 1)
     act = stack, other_core(stack)
-    (grad_w_out,) = weight_grad(w_out, act[:1], cot_shards, (0,))
-    back_stack = doubled(grad_hidden, 0)
+    back_stack = doubled(grad_hidden, 0, PART_COST)
 
     even, odd = range(0, cols, 2), range(1, cols, 2)
-    keep, sent, grad_w_out = weight_grad(
-        w_out, act, cot_shards, (1,), cols, (even, odd), grad_w_out
-    )
+    keep, sent, grad_w_out = weight_grad(w_out, act, cot_shards, (0, 1), cols, (even, odd))
     got = swap(sent, "col", 1, cols)
     back_stack = doubled(back_stack, 1)
     grad_hidden = back_stack, other_core(back_stack)

time: 95 us -> 96.5 us (1.016)
  waiting for transfers between devices: 13.6 us -> 19.2 us
  starting transfers between devices: 32 us -> 28.2 us
    ppermute x16, waiting for transfers between devices: 3.49 us -> 8.26 us  [swap(): return lax.ppermute(value, axis, [(i, i ^ flip) for i in range(count)])]
    ppermute x8, starting transfers between devices: 10.8 us -> 8.13 us  [across(): return lax.ppermute(value, 'row', [(i, i ^ flips[i]) for i in range(rows)])]
    ppermute x16, starting transfers between devices: 21.3 us -> 20 us  [swap(): return lax.ppermute(value, axis, [(i, i ^ flip) for i in range(count)])]
    pallas_call x30 -> x28, Pallas kernels: 48.3 us -> 48.1 us  [call(): pl.pallas_call(body, in_specs=[specs[space] for space, value in arrays] +...]
  transfers between devices with their start and end apart: 24 -> 24, of which waited for: 11 -> 11; matrix products, arithmetic and copies ran while one was open for 0% -> 0% of each run, Pallas kernels for 47% -> 46%
where the time goes in v6:
time: 96.5 us; the launch traced here: 96.4 us
  Pallas kernels  48.1 us (50%)
  starting transfers between devices  28.2 us (29%)
  waiting for transfers between devices  19.2 us (20%)
    pallas_call x28, Pallas kernels, call(): pl.pallas_call(body, in_specs=[specs[space] for space, value in arrays] +...  48.1 us
    ppermute x16, starting transfers between devices, swap(): return lax.ppermute(value, axis, [(i, i ^ flip) for i in range(count)])  20 us
    ppermute x8, waiting for transfers between devices, across(): return lax.ppermute(value, 'row', [(i, i ^ flips[i]) for i in range(rows)])  11 us
    ppermute x16, waiting for transfers between devices, swap(): return lax.ppermute(value, axis, [(i, i ^ flip) for i in range(count)])  8.26 us
    ppermute x8, starting transfers between devices, across(): return lax.ppermute(value, 'row', [(i, i ^ flips[i]) for i in range(rows)])  8.13 us
  transfers between devices with their start and end apart: 24, of which 11 were waited for; matrix products, arithmetic and copies ran while one was open for 0% of the time, Pallas kernels for 46%

profile of v6, /device:TPU:0, one launch (start us, length us, event | category | flops | bytes accessed | tf_op | source)
XLA Modules:
  0.0 96.4 jit_solution(10644254355395016051)
XLA Ops:
  0.6 4.1 %collective-permute-start = (bf16[32,1536]{1,0:T(8,128)(2,1)}, bf16[32,1536]{1,0:T(8,128)(2,1)S(1)}, u32[]{:S(2)}, u32[]{:S(2)}) collective-permute-start(bf16[32,1536]{1,0:T(8,128)(2,1)} %refs_3_.3), channel_id=1, source_target_pairs={{0,2},{1,3},{2,0},{3,1},{4,6},{5,7},{6,4},{7,5},{8,10},{9,11},{10,... | collective-permute-start | bytes 294920 | tf_op jit(solution)/shard_map/ppermute | solution.py:28
  4.7 4.6 %shard_map.75 = (bf16[1536,768]{1,0:T(8,128)(2,1)S(1)}, bf16[1536,768]{1,0:T(8,128)(2,1)S(1)}, bf16[1536,768]{1,0:T(8,128)(2,1)S(1)}, bf16[1536,768]{1,0:T(8,128)(2,1)S(1)}, bf16[1536,768]{1,0:T(8,128)(2,1)S(1)}) custom-call(s32[1]{0:T(128)} %bitcast.refs_0_, bf16[1536,6144]{1,0:T(8,128)(2,1)} %refs_1_.9), custom_call_target="tpu_custom_call" | custom-call | tf_op jit(solution)/shard_map/pallas_call | solution.py:69
  11.1 3.0 %collective-permute-start.2 = (bf16[32,1536]{1,0:T(8,128)(2,1)S(1)}, bf16[32,1536]{1,0:T(8,128)(2,1)S(1)}, u32[]{:S(2)}, u32[]{:S(2)}) collective-permute-start(bf16[32,1536]{1,0:T(8,128)(2,1)S(1)} %shard_map.77.refs_2_), channel_id=1, source_target_pairs={{0,2},{1,3},{2,0},{3,1},{4,6},{5,7},{6,4},{7,5},{8,10},{9,11},{10,... | collective-permute-start | bytes 294920 | tf_op jit(solution)/shard_map/ppermute | solution.py:28
  14.1 3.1 %shard_map.78 = (bf16[1536,768]{1,0:T(8,128)(2,1)S(1)}, bf16[1536,768]{1,0:T(8,128)(2,1)S(1)}, bf16[1536,768]{1,0:T(8,128)(2,1)S(1)}) custom-call(s32[1]{0:T(128)} %bitcast.refs_0_, bf16[1536,6144]{1,0:T(8,128)(2,1)} %refs_1_.9, bf16[32,1536]{1,0:T(8,128)(2,1)S(1)} %shard_map.77.refs_2_), custom_call_target="tpu_custom_call" | custom-call | tf_op jit(solution)/shard_map/pallas_call | solution.py:69
  18.1 2.4 %shard_map.80 = (bf16[2,128,768]{2,1,0:T(8,128)(2,1)S(1)}, bf16[2,128,768]{2,1,0:T(8,128)(2,1)S(1)}, bf16[768,1536]{1,0:T(8,128)(2,1)S(1)}, bf16[768,1536]{1,0:T(8,128)(2,1)S(1)}) custom-call(s32[1]{0:T(128)} %bitcast.refs_0_, bf16[32,1536]{1,0:T(8,128)(2,1)S(1)} %copy-done.1, bf16[32,1536]{1,0:T(8,128)(2,1)S(1)} %collective-permute-done.refs_1_.refs_2_.refs_4_, ...), custom_call_target="tpu_custom_call" | custom-call | tf_op jit(solution)/shard_map/pallas_call | solution.py:69
  24.1 2.4 %shard_map.84 = (bf16[768,1536]{1,0:T(8,128)(2,1)S(1)}, bf16[768,1536]{1,0:T(8,128)(2,1)S(1)}) custom-call(s32[1]{0:T(128)} %bitcast.refs_0_, bf16[6144,1536]{1,0:T(8,128)(2,1)} %refs_6_.1, bf16[64,1536]{1,0:T(8,128)(2,1)S(1)} %shard_map.83.refs_2_), custom_call_target="tpu_custom_call" | custom-call | tf_op jit(solution)/shard_map/pallas_call | solution.py:69
  26.5 3.3 %collective-permute-start.7 = (bf16[64,1536]{1,0:T(8,128)(2,1)S(1)}, bf16[64,1536]{1,0:T(8,128)(2,1)S(1)}, u32[]{:S(2)}, u32[]{:S(2)}) collective-permute-start(bf16[64,1536]{1,0:T(8,128)(2,1)S(1)} %shard_map.83.refs_2_), channel_id=1, source_target_pairs={{0,1},{1,0},{2,3},{3,2},{4,5},{5,4},{6,7},{7,6},{8,9},{9,8},{10,11... | collective-permute-start | bytes 589832 | tf_op jit(solution)/shard_map/ppermute | solution.py:28
  32.0 2.6 %collective-permute-done.7.refs_3_.refs_5_ = bf16[64,1536]{1,0:T(8,128)(2,1)S(1)} collective-permute-done((bf16[64,1536]{1,0:T(8,128)(2,1)S(1)}, bf16[64,1536]{1,0:T(8,128)(2,1)S(1)}, u32[]{:S(2)}, u32[]{:S(2)}) %collective-permute-start.7) | collective-permute-done | bytes 196640 | tf_op jit(solution)/shard_map/ppermute | solution.py:28
  34.7 3.2 %shard_map.86 = (bf16[2,128,768]{2,1,0:T(8,128)(2,1)S(1)}, bf16[2,128,768]{2,1,0:T(8,128)(2,1)S(1)}, bf16[768,1536]{1,0:T(8,128)(2,1)S(1)}, bf16[768,1536]{1,0:T(8,128)(2,1)S(1)}) custom-call(s32[1]{0:T(128)} %bitcast.refs_0_, bf16[32,1536]{1,0:T(8,128)(2,1)S(1)} %copy-done, bf16[32,1536]{1,0:T(8,128)(2,1)S(1)} %collective-permute-done.2.refs_1_.refs_2_.refs_4_, ...), custom_call_target="tpu_custom_call" | custom-call | tf_op jit(solution)/shard_map/pallas_call | solution.py:69
  38.2 1.5 %collective-permute-done.9.refs_1_ = bf16[2,128,768]{2,1,0:T(8,128)(2,1)S(1)} collective-permute-done((bf16[2,128,768]{2,1,0:T(8,128)(2,1)S(1)}, bf16[2,128,768]{2,1,0:T(8,128)(2,1)S(1)}, u32[]{:S(2)}, u32[]{:S(2)}) %collective-permute-start.9) | collective-permute-done | bytes 393248 | tf_op jit(solution)/shard_map/ppermute | solution.py:28
  39.8 1.5 %collective-permute-start.11 = (bf16[2,128,768]{2,1,0:T(8,128)(2,1)S(1)}, bf16[2,128,768]{2,1,0:T(8,128)(2,1)S(1)}, u32[]{:S(2)}, u32[]{:S(2)}) collective-permute-start(bf16[2,128,768]{2,1,0:T(8,128)(2,1)S(1)} %shard_map.88.refs_7_), channel_id=1, source_target_pairs={{0,8},{4,20},{8,0},{12,28},{16,24},{20,4},{24,16},{28,12},{1,9},{5... | collective-permute-start | bytes 1179656 | tf_op jit(solution)/shard_map/ppermute | solution.py:38
  41.3 2.4 %shard_map.89 = (bf16[1,128,768]{2,1,0:T(8,128)(2,1)S(1)}, bf16[1,128,768]{2,1,0:T(8,128)(2,1)S(1)}, bf16[768,1536]{1,0:T(8,128)(2,1)S(1)}, bf16[768,1536]{1,0:T(8,128)(2,1)S(1)}) custom-call(s32[1]{0:T(128)} %bitcast.refs_0_, bf16[32,1536]{1,0:T(8,128)(2,1)S(1)} %copy-done, bf16[32,1536]{1,0:T(8,128)(2,1)S(1)} %collective-permute-done.2.refs_1_.refs_2_.refs_4_, ...), custom_call_target="tpu_custom_call" | custom-call | tf_op jit(solution)/shard_map/pallas_call | solution.py:69
  44.4 1.8 %shard_map.90 = (bf16[1,128,768]{2,1,0:T(8,128)(2,1)S(1)}, bf16[1,128,768]{2,1,0:T(8,128)(2,1)S(1)}) custom-call(s32[1]{0:T(128)} %bitcast.refs_0_, bf16[32,1536]{1,0:T(8,128)(2,1)S(1)} %copy-done, bf16[32,1536]{1,0:T(8,128)(2,1)S(1)} %collective-permute-done.2.refs_1_.refs_2_.refs_4_, bf16[64,1536]{1,0:T(8,128)(2,1)S(1)} %collective-permute-done.7.refs_3_.refs_5_, ...), custom_call_target="tpu_custom_call" | custom-call | tf_op jit(solution)/shard_map/pallas_call | solution.py:69
  50.4 3.1 %collective-permute-done.14.refs_4_ = bf16[1,128,768]{2,1,0:T(8,128)(2,1)S(1)} collective-permute-done((bf16[1,128,768]{2,1,0:T(8,128)(2,1)S(1)}, bf16[1,128,768]{2,1,0:T(8,128)(2,1)S(1)}, u32[]{:S(2)}, u32[]{:S(2)}) %collective-permute-start.14) | collective-permute-done | bytes 196640 | tf_op jit(solution)/shard_map/ppermute | solution.py:38
  53.8 1.5 %collective-permute-start.16 = (bf16[128,768]{1,0:T(8,128)(2,1)S(1)}, bf16[128,768]{1,0:T(8,128)(2,1)S(1)}, u32[]{:S(2)}, u32[]{:S(2)}) collective-permute-start(bf16[128,768]{1,0:T(8,128)(2,1)S(1)} %shard_map.93.refs_2_.refs_0_), channel_id=1, source_target_pairs={{0,8},{4,20},{8,0},{12,28},{16,24},{20,4},{24,16},{28,12},{1,9},{5... | collective-permute-start | bytes 589832 | tf_op jit(solution)/shard_map/ppermute | solution.py:38
  55.3 4.5 %collective-permute-done.12.refs_1_ = bf16[256,768]{1,0:T(8,128)(2,1)S(1)} collective-permute-done((bf16[256,768]{1,0:T(8,128)(2,1)S(1)}, bf16[256,768]{1,0:T(8,128)(2,1)S(1)}, u32[]{:S(2)}, u32[]{:S(2)}) %collective-permute-start.12) | collective-permute-done | bytes 393248 | tf_op jit(solution)/shard_map/ppermute | solution.py:38
  60.5 1.7 %collective-permute-done.15.refs_2_ = bf16[512,768]{1,0:T(8,128)(2,1)S(1)} collective-permute-done((bf16[512,768]{1,0:T(8,128)(2,1)S(1)}, bf16[512,768]{1,0:T(8,128)(2,1)S(1)}, u32[]{:S(2)}, u32[]{:S(2)}) %collective-permute-start.15) | collective-permute-done | bytes 786464 | tf_op jit(solution)/shard_map/ppermute | solution.py:28
  62.2 9.8 %shard_map.96 = (bf16[64,1536]{1,0:T(8,128)(2,1)S(1)}, bf16[64,1536]{1,0:T(8,128)(2,1)S(1)}, bf16[6144,1536]{1,0:T(8,128)(2,1)}) custom-call(s32[1]{0:T(128)} %bitcast.refs_0_, bf16[512,768]{1,0:T(8,128)(2,1)S(1)} %shard_map.94.refs_2_.refs_1_, bf16[512,768]{1,0:T(8,128)(2,1)S(1)} %collective-permute-done.15.refs_2_, bf16[32,1536]{1,0:T(8,128)(2,1)S(1)} %copy-done, ...), custom_call_target="tpu_custom_call" | custom-call | flops 2415919104 | bytes 18874368 | tf_op jit(solution)/shard_map/pallas_call | solution.py:69
  72.3 1.8 %collective-permute-start.17 = (bf16[64,1536]{1,0:T(8,128)(2,1)S(1)}, bf16[64,1536]{1,0:T(8,128)(2,1)S(1)}, u32[]{:S(2)}, u32[]{:S(2)}) collective-permute-start(bf16[64,1536]{1,0:T(8,128)(2,1)S(1)} %get-tuple-element.72), channel_id=1, source_target_pairs={{0,1},{1,0},{2,3},{3,2},{4,5},{5,4},{6,7},{7,6},{8,9},{9,8},{10,11... | collective-permute-start | bytes 589832 | tf_op jit(solution)/shard_map/ppermute | solution.py:28
  74.1 3.1 %shard_map.98.refs_5_.refs_6_ = f32[128,1536]{1,0:T(8,128)S(1)} custom-call(bf16[512,768]{1,0:T(8,128)(2,1)S(1)} %shard_map.97.refs_0_.refs_5_.refs_1_, bf16[1536,768]{1,0:T(8,128)(2,1)S(1)} %get-tuple-element.46.refs_2_.refs_7_.refs_1_, bf16[1536,768]{1,0:T(8,128)(2,1)S(1)} %get-tuple-element.49.refs_6_.refs_2_, ...), custom_call_target="tpu_custom_call" | custom-call | flops 1207959552 | bytes 9437184 | tf_op jit(solution)/shard_map/pallas_call | solution.py:69
  77.2 3.1 %shard_map.99 = (bf16[32,1536]{1,0:T(8,128)(2,1)S(1)}, bf16[32,1536]{1,0:T(8,128)(2,1)S(1)}, bf16[32,1536]{1,0:T(8,128)(2,1)S(1)}, bf16[32,1536]{1,0:T(8,128)(2,1)S(1)}) custom-call(bf16[512,768]{1,0:T(8,128)(2,1)S(1)} %collective-permute-done.19.refs_0_.refs_2_, bf16[1536,768]{1,0:T(8,128)(2,1)S(1)} %get-tuple-element.44.refs_5_.refs_1_, ...), custom_call_target="tpu_custom_call" | custom-call | flops 1207959552 | bytes 9437184 | tf_op jit(solution)/shard_map/pallas_call | solution.py:69
  80.3 1.5 %collective-permute-start.21 = (bf16[32,1536]{1,0:T(8,128)(2,1)S(1)}, bf16[32,1536]{1,0:T(8,128)(2,1)S(1)}, u32[]{:S(2)}, u32[]{:S(2)}) collective-permute-start(bf16[32,1536]{1,0:T(8,128)(2,1)S(1)} %get-tuple-element.74.refs_2_), channel_id=1, source_target_pairs={{0,3},{1,2},{2,1},{3,0},{4,7},{5,6},{6,5},{7,4},{8,11},{9,10},{10,... | collective-permute-start | bytes 294920 | tf_op jit(solution)/shard_map/ppermute | solution.py:28
  82.2 2.6 %collective-permute-start.22 = (bf16[32,1536]{1,0:T(8,128)(2,1)S(1)}, bf16[32,1536]{1,0:T(8,128)(2,1)S(1)}, u32[]{:S(2)}, u32[]{:S(2)}) collective-permute-start(bf16[32,1536]{1,0:T(8,128)(2,1)S(1)} %get-tuple-element.78), channel_id=1, source_target_pairs={{0,2},{1,3},{2,0},{3,1},{4,6},{5,7},{6,4},{7,5},{8,10},{9,11},{10,... | collective-permute-start | bytes 294920 | tf_op jit(solution)/shard_map/ppermute | solution.py:28
  85.7 8.8 %shard_map.101.refs_6_ = bf16[1536,6144]{1,0:T(8,128)(2,1)} custom-call(s32[1]{0:T(128)} %bitcast.refs_0_, bf16[512,768]{1,0:T(8,128)(2,1)S(1)} %shard_map.97.refs_0_.refs_5_.refs_1_, bf16[512,768]{1,0:T(8,128)(2,1)S(1)} %collective-permute-done.19.refs_0_.refs_2_, bf16[32,1536]{1,0:T(8,128)(2,1)S(1)} %copy-done.1, ...), custom_call_target="tpu_custom_call" | custom-call | flops 2415919104 | bytes 18874368 | tf_op jit(solution)/shard_map/pallas_call | solution.py:69
  (56 shorter events, 18.0 us)
Async XLA Ops:
  0.6 9.2 %collective-permute-start = (bf16[32,1536]{1,0:T(8,128)(2,1)}, bf16[32,1536]{1,0:T(8,128)(2,1)S(1)}, u32[]{:S(2)}, u32[]{:S(2)}) collective-permute-start(bf16[32,1536]{1,0:T(8,128)(2,1)} %refs_3_.3), channel_id=1, source_target_pairs={{0,2},{1,3},{2,0},{3,1},{4,6},{5,7},{6,4},{7,5},{8,10},{9,11},{10,... | collective-permute-start | bytes 294920 | tf_op jit(solution)/shard_map/ppermute | solution.py:28
  9.9 8.3 %collective-permute-start.1 = (bf16[64,1536]{1,0:T(8,128)(2,1)S(1)}, bf16[64,1536]{1,0:T(8,128)(2,1)S(1)}, u32[]{:S(2)}, u32[]{:S(2)}) collective-permute-start(bf16[64,1536]{1,0:T(8,128)(2,1)S(1)} %shard_map.76.refs_1_), channel_id=1, source_target_pairs={{0,1},{1,0},{2,3},{3,2},{4,5},{5,4},{6,7},{7,6},{8,9},{9,8},{10,11... | collective-permute-start | bytes 589832 | tf_op jit(solution)/shard_map/ppermute | solution.py:28
  11.1 6.2 %collective-permute-start.2 = (bf16[32,1536]{1,0:T(8,128)(2,1)S(1)}, bf16[32,1536]{1,0:T(8,128)(2,1)S(1)}, u32[]{:S(2)}, u32[]{:S(2)}) collective-permute-start(bf16[32,1536]{1,0:T(8,128)(2,1)S(1)} %shard_map.77.refs_2_), channel_id=1, source_target_pairs={{0,2},{1,3},{2,0},{3,1},{4,6},{5,7},{6,4},{7,5},{8,10},{9,11},{10,... | collective-permute-start | bytes 294920 | tf_op jit(solution)/shard_map/ppermute | solution.py:28
  20.5 2.1 %collective-permute-start.4 = (bf16[2,128,768]{2,1,0:T(8,128)(2,1)S(1)}, bf16[2,128,768]{2,1,0:T(8,128)(2,1)S(1)}, u32[]{:S(2)}, u32[]{:S(2)}) collective-permute-start(bf16[2,128,768]{2,1,0:T(8,128)(2,1)S(1)} %get-tuple-element.55), channel_id=1, source_target_pairs={{0,4},{4,0},{8,12},{12,8},{16,20},{20,16},{24,28},{28,24},{1,5},{5... | collective-permute-start | bytes 1179656 | tf_op jit(solution)/shard_map/ppermute | solution.py:28
  22.1 7.8 %collective-permute-start.3 = (bf16[2,128,768]{2,1,0:T(8,128)(2,1)S(1)}, bf16[2,128,768]{2,1,0:T(8,128)(2,1)S(1)}, u32[]{:S(2)}, u32[]{:S(2)}) collective-permute-start(bf16[2,128,768]{2,1,0:T(8,128)(2,1)S(1)} %get-tuple-element.53.refs_2_), channel_id=1, source_target_pairs={{0,4},{4,0},{8,12},{12,8},{16,20},{20,16},{24,28},{28,24},{1,5},{5... | collective-permute-start | bytes 1179656 | tf_op jit(solution)/shard_map/ppermute | solution.py:28
  22.7 7.8 %collective-permute-start.5 = (bf16[2,128,768]{2,1,0:T(8,128)(2,1)S(1)}, bf16[2,128,768]{2,1,0:T(8,128)(2,1)S(1)}, u32[]{:S(2)}, u32[]{:S(2)}) collective-permute-start(bf16[2,128,768]{2,1,0:T(8,128)(2,1)S(1)} %shard_map.82.refs_1_), channel_id=1, source_target_pairs={{0,8},{4,20},{8,0},{12,28},{16,24},{20,4},{24,16},{28,12},{1,9},{5... | collective-permute-start | bytes 1179656 | tf_op jit(solution)/shard_map/ppermute | solution.py:38
  26.5 8.2 %collective-permute-start.7 = (bf16[64,1536]{1,0:T(8,128)(2,1)S(1)}, bf16[64,1536]{1,0:T(8,128)(2,1)S(1)}, u32[]{:S(2)}, u32[]{:S(2)}) collective-permute-start(bf16[64,1536]{1,0:T(8,128)(2,1)S(1)} %shard_map.83.refs_2_), channel_id=1, source_target_pairs={{0,1},{1,0},{2,3},{3,2},{4,5},{5,4},{6,7},{7,6},{8,9},{9,8},{10,11... | collective-permute-start | bytes 589832 | tf_op jit(solution)/shard_map/ppermute | solution.py:28
  30.6 7.4 %collective-permute-start.6 = (bf16[1,128,768]{2,1,0:T(8,128)(2,1)S(1)}, bf16[1,128,768]{2,1,0:T(8,128)(2,1)S(1)}, u32[]{:S(2)}, u32[]{:S(2)}) collective-permute-start(bf16[1,128,768]{2,1,0:T(8,128)(2,1)S(1)} %shard_map.85.refs_9_), channel_id=1, source_target_pairs={{0,16},{4,12},{8,24},{12,4},{16,0},{20,28},{24,8},{28,20},{1,17},{... | collective-permute-start | bytes 589832 | tf_op jit(solution)/shard_map/ppermute | solution.py:38
  37.9 1.8 %collective-permute-start.9 = (bf16[2,128,768]{2,1,0:T(8,128)(2,1)S(1)}, bf16[2,128,768]{2,1,0:T(8,128)(2,1)S(1)}, u32[]{:S(2)}, u32[]{:S(2)}) collective-permute-start(bf16[2,128,768]{2,1,0:T(8,128)(2,1)S(1)} %get-tuple-element.63), channel_id=1, source_target_pairs={{0,4},{4,0},{8,12},{12,8},{16,20},{20,16},{24,28},{28,24},{1,5},{5... | collective-permute-start | bytes 1179656 | tf_op jit(solution)/shard_map/ppermute | solution.py:28
  39.8 7.8 %collective-permute-start.11 = (bf16[2,128,768]{2,1,0:T(8,128)(2,1)S(1)}, bf16[2,128,768]{2,1,0:T(8,128)(2,1)S(1)}, u32[]{:S(2)}, u32[]{:S(2)}) collective-permute-start(bf16[2,128,768]{2,1,0:T(8,128)(2,1)S(1)} %shard_map.88.refs_7_), channel_id=1, source_target_pairs={{0,8},{4,20},{8,0},{12,28},{16,24},{20,4},{24,16},{28,12},{1,9},{5... | collective-permute-start | bytes 1179656 | tf_op jit(solution)/shard_map/ppermute | solution.py:38
  43.7 2.8 %collective-permute-start.10 = (bf16[1,128,768]{2,1,0:T(8,128)(2,1)S(1)}, bf16[1,128,768]{2,1,0:T(8,128)(2,1)S(1)}, u32[]{:S(2)}, u32[]{:S(2)}) collective-permute-start(bf16[1,128,768]{2,1,0:T(8,128)(2,1)S(1)} %get-tuple-element.65), channel_id=1, source_target_pairs={{0,4},{4,0},{8,12},{12,8},{16,20},{20,16},{24,28},{28,24},{1,5},{5... | collective-permute-start | bytes 589832 | tf_op jit(solution)/shard_map/ppermute | solution.py:28
  43.8 6.0 %collective-permute-start.8 = (bf16[128,768]{1,0:T(8,128)(2,1)S(1)}, bf16[128,768]{1,0:T(8,128)(2,1)S(1)}, u32[]{:S(2)}, u32[]{:S(2)}) collective-permute-start(bf16[128,768]{1,0:T(8,128)(2,1)S(1)} %get-tuple-element.60.refs_2_.refs_0_), channel_id=1, source_target_pairs={{0,8},{4,20},{8,0},{12,28},{16,24},{20,4},{24,16},{28,12},{1,9},{5... | collective-permute-start | bytes 589832 | tf_op jit(solution)/shard_map/ppermute | solution.py:38
  46.3 4.1 %collective-permute-start.13 = (bf16[1,128,768]{2,1,0:T(8,128)(2,1)S(1)}, bf16[1,128,768]{2,1,0:T(8,128)(2,1)S(1)}, u32[]{:S(2)}, u32[]{:S(2)}) collective-permute-start(bf16[1,128,768]{2,1,0:T(8,128)(2,1)S(1)} %get-tuple-element.68.refs_3_), channel_id=1, source_target_pairs={{0,4},{4,0},{8,12},{12,8},{16,20},{20,16},{24,28},{28,24},{1,5},{5... | collective-permute-start | bytes 589832 | tf_op jit(solution)/shard_map/ppermute | solution.py:28
  47.7 5.7 %collective-permute-start.14 = (bf16[1,128,768]{2,1,0:T(8,128)(2,1)S(1)}, bf16[1,128,768]{2,1,0:T(8,128)(2,1)S(1)}, u32[]{:S(2)}, u32[]{:S(2)}) collective-permute-start(bf16[1,128,768]{2,1,0:T(8,128)(2,1)S(1)} %shard_map.91.refs_2_), channel_id=1, source_target_pairs={{0,16},{4,12},{8,24},{12,4},{16,0},{20,28},{24,8},{28,20},{1,17},{... | collective-permute-start | bytes 589832 | tf_op jit(solution)/shard_map/ppermute | solution.py:38
  49.8 10.0 %collective-permute-start.12 = (bf16[256,768]{1,0:T(8,128)(2,1)S(1)}, bf16[256,768]{1,0:T(8,128)(2,1)S(1)}, u32[]{:S(2)}, u32[]{:S(2)}) collective-permute-start(bf16[256,768]{1,0:T(8,128)(2,1)S(1)} %shard_map.92.refs_5_.refs_0_), channel_id=1, source_target_pairs={{0,16},{4,12},{8,24},{12,4},{16,0},{20,28},{24,8},{28,20},{1,17},{... | collective-permute-start | bytes 1179656 | tf_op jit(solution)/shard_map/ppermute | solution.py:38
  53.8 6.1 %collective-permute-start.16 = (bf16[128,768]{1,0:T(8,128)(2,1)S(1)}, bf16[128,768]{1,0:T(8,128)(2,1)S(1)}, u32[]{:S(2)}, u32[]{:S(2)}) collective-permute-start(bf16[128,768]{1,0:T(8,128)(2,1)S(1)} %shard_map.93.refs_2_.refs_0_), channel_id=1, source_target_pairs={{0,8},{4,20},{8,0},{12,28},{16,24},{20,4},{24,16},{28,12},{1,9},{5... | collective-permute-start | bytes 589832 | tf_op jit(solution)/shard_map/ppermute | solution.py:38
  59.8 2.4 %collective-permute-start.15 = (bf16[512,768]{1,0:T(8,128)(2,1)S(1)}, bf16[512,768]{1,0:T(8,128)(2,1)S(1)}, u32[]{:S(2)}, u32[]{:S(2)}) collective-permute-start(bf16[512,768]{1,0:T(8,128)(2,1)S(1)} %shard_map.94.refs_2_.refs_1_), channel_id=1, source_target_pairs={{0,4},{4,0},{8,12},{12,8},{16,20},{20,16},{24,28},{28,24},{1,5},{5... | collective-permute-start | bytes 2359304 | tf_op jit(solution)/shard_map/ppermute | solution.py:28
  60.0 12.1 %collective-permute-start.18 = (bf16[256,768]{1,0:T(8,128)(2,1)S(1)}, bf16[256,768]{1,0:T(8,128)(2,1)S(1)}, u32[]{:S(2)}, u32[]{:S(2)}) collective-permute-start(bf16[256,768]{1,0:T(8,128)(2,1)S(1)} %shard_map.95.refs_14_.refs_0_), channel_id=1, source_target_pairs={{0,16},{4,12},{8,24},{12,4},{16,0},{20,28},{24,8},{28,20},{1,17},{... | collective-permute-start | bytes 1179656 | tf_op jit(solution)/shard_map/ppermute | solution.py:38
  72.1 5.1 %collective-permute-start.19 = (bf16[512,768]{1,0:T(8,128)(2,1)S(1)}, bf16[512,768]{1,0:T(8,128)(2,1)S(1)}, u32[]{:S(2)}, u32[]{:S(2)}) collective-permute-start(bf16[512,768]{1,0:T(8,128)(2,1)S(1)} %shard_map.97.refs_0_.refs_5_.refs_1_), channel_id=1, source_target_pairs={{0,4},{4,0},{8,12},{12,8},{16,20},{20,16},{24,28},{28,24},{1,5},{5... | collective-permute-start | bytes 2359304 | tf_op jit(solution)/shard_map/ppermute | solution.py:28
  72.3 9.5 %collective-permute-start.17 = (bf16[64,1536]{1,0:T(8,128)(2,1)S(1)}, bf16[64,1536]{1,0:T(8,128)(2,1)S(1)}, u32[]{:S(2)}, u32[]{:S(2)}) collective-permute-start(bf16[64,1536]{1,0:T(8,128)(2,1)S(1)} %get-tuple-element.72), channel_id=1, source_target_pairs={{0,1},{1,0},{2,3},{3,2},{4,5},{5,4},{6,7},{7,6},{8,9},{9,8},{10,11... | collective-permute-start | bytes 589832 | tf_op jit(solution)/shard_map/ppermute | solution.py:28
  80.3 14.2 %collective-permute-start.21 = (bf16[32,1536]{1,0:T(8,128)(2,1)S(1)}, bf16[32,1536]{1,0:T(8,128)(2,1)S(1)}, u32[]{:S(2)}, u32[]{:S(2)}) collective-permute-start(bf16[32,1536]{1,0:T(8,128)(2,1)S(1)} %get-tuple-element.74.refs_2_), channel_id=1, source_target_pairs={{0,3},{1,2},{2,1},{3,0},{4,7},{5,6},{6,5},{7,4},{8,11},{9,10},{10,... | collective-permute-start | bytes 294920 | tf_op jit(solution)/shard_map/ppermute | solution.py:28
  81.9 12.6 %collective-permute-start.20 = (bf16[32,1536]{1,0:T(8,128)(2,1)S(1)}, bf16[32,1536]{1,0:T(8,128)(2,1)S(1)}, u32[]{:S(2)}, u32[]{:S(2)}) collective-permute-start(bf16[32,1536]{1,0:T(8,128)(2,1)S(1)} %get-tuple-element.76.refs_6_), channel_id=1, source_target_pairs={{0,2},{1,3},{2,0},{3,1},{4,6},{5,7},{6,4},{7,5},{8,10},{9,11},{10,... | collective-permute-start | bytes 294920 | tf_op jit(solution)/shard_map/ppermute | solution.py:28
  82.2 13.4 %collective-permute-start.22 = (bf16[32,1536]{1,0:T(8,128)(2,1)S(1)}, bf16[32,1536]{1,0:T(8,128)(2,1)S(1)}, u32[]{:S(2)}, u32[]{:S(2)}) collective-permute-start(bf16[32,1536]{1,0:T(8,128)(2,1)S(1)} %get-tuple-element.78), channel_id=1, source_target_pairs={{0,2},{1,3},{2,0},{3,1},{4,6},{5,7},{6,4},{7,5},{8,10},{9,11},{10,... | collective-permute-start | bytes 294920 | tf_op jit(solution)/shard_map/ppermute | solution.py:28
  84.9 10.8 %collective-permute-start.23 = (bf16[32,1536]{1,0:T(8,128)(2,1)S(1)}, bf16[32,1536]{1,0:T(8,128)(2,1)S(1)}, u32[]{:S(2)}, u32[]{:S(2)}) collective-permute-start(bf16[32,1536]{1,0:T(8,128)(2,1)S(1)} %get-tuple-element.79), channel_id=1, source_target_pairs={{0,1},{1,0},{2,3},{3,2},{4,5},{5,4},{6,7},{7,6},{8,9},{9,8},{10,11... | collective-permute-start | bytes 294920 | tf_op jit(solution)/shard_map/ppermute | solution.py:28
  (2 other events, 6.8 us)

commit v7 on v6

--- a/solution.py
+++ b/solution.py
@@ -13,6 +13,7 @@
 WRITES = 6
 READ_CUTS, WRITE_CUTS = 4, 3
 PART_COST = 6 * 10**9
+BACK_COST = 6 * 10**9
 
 
 def gelu_fn(value):
@@ -181,7 +182,7 @@
     )
 
 
-def project(weight, shards, positions, blocks, after=()):
+def project(weight, shards, positions, blocks, after=(), flops=0):
     pieces, order = shards
     coming = Coming(blocks)
     tokens, n = sum(piece.shape[0] for piece in pieces), len(positions)
@@ -216,7 +217,7 @@
         + in_vmem([weight.held[key] for key in keys])
         + coming.inputs,
         [("vmem", ((n, tokens, block), BF16))] * 2 + coming.outs,
-        0,
+        flops,
         0,
         after,
         [pltpu.VMEM((tokens, weight.width), BF16)] + coming.scratch,
@@ -421,7 +422,7 @@
         refs[-1][...] = gelu_back(hidden_ref[...], block_of(terms)(refs))
 
     arrays = [hidden] + [array for array, block in terms]
-    return call(kernel, in_vmem(arrays), [("vmem", (hidden.shape, BF16))], PART_COST, 0)[0]
+    return call(kernel, in_vmem(arrays), [("vmem", (hidden.shape, BF16))], BACK_COST, 0)[0]
 
 
 def exchange_col(parts, cols):
@@ -469,17 +470,17 @@
     sent = one_block([(here, 0), (got_here, 0), (came, 1)])
     terms = [(here, 1), (got_here, 1), (came, 0), (across(sent, 1, rows), 0)]
 
-    keep, sent = project(w_out, cot_shards, first, wanted[12:14])
+    keep, sent = project(w_out, cot_shards, first, wanted[12:14], (), PART_COST)
     got = other_core(sent)
     hidden, act = activate(terms)
     came = across(added([keep, got])[0], 0, rows)
     keep, sent = project(w_out, cot_shards, second, wanted[14:])
     got = other_core(sent)
+    stack = doubled(act, 0, PART_COST)
     own_keep, sent = project(w_out, cot_shards, own, [])
     own_got = other_core(sent)
     sent = one_block([(keep, 0), (got, 0), (came, 1)])
     last = across(sent, 1, rows)
-    stack = doubled(act, 0)
     grad_hidden = activate_back(hidden, [(own_keep, 0), (own_got, 0), (came, 0), (last, 0)])
     stack = doubled(stack, 1)
     act = stack, other_core(stack)

time: 96.5 us -> 96.7 us (level)
  starting transfers between devices: 28.2 us -> 31.1 us
  waiting for transfers between devices: 19.2 us -> 16.4 us
    ppermute x16, waiting for transfers between devices: 8.26 us -> 3.55 us  [swap(): return lax.ppermute(value, axis, [(i, i ^ flip) for i in range(count)])]
    ppermute x8, waiting for transfers between devices: 11 us -> 12.9 us  [across(): return lax.ppermute(value, 'row', [(i, i ^ flips[i]) for i in range(rows)])]
    ppermute x8, starting transfers between devices: 8.13 us -> 9.89 us  [across(): return lax.ppermute(value, 'row', [(i, i ^ flips[i]) for i in range(rows)])]
    ppermute x16, starting transfers between devices: 20 us -> 21.3 us  [swap(): return lax.ppermute(value, axis, [(i, i ^ flip) for i in range(count)])]
where the time goes in v7:
time: 96.7 us; the launch traced here: 96.6 us
  Pallas kernels  48.1 us (50%)
  starting transfers between devices  31.1 us (32%)
  waiting for transfers between devices  16.4 us (17%)
    pallas_call x28, Pallas kernels, call(): pl.pallas_call(body, in_specs=[specs[space] for space, value in arrays] +...  48.1 us
    ppermute x16, starting transfers between devices, swap(): return lax.ppermute(value, axis, [(i, i ^ flip) for i in range(count)])  21.3 us
    ppermute x8, waiting for transfers between devices, across(): return lax.ppermute(value, 'row', [(i, i ^ flips[i]) for i in range(rows)])  12.9 us
    ppermute x8, starting transfers between devices, across(): return lax.ppermute(value, 'row', [(i, i ^ flips[i]) for i in range(rows)])  9.89 us
    ppermute x16, waiting for transfers between devices, swap(): return lax.ppermute(value, axis, [(i, i ^ flip) for i in range(count)])  3.55 us
  transfers between devices with their start and end apart: 24, of which 11 were waited for; matrix products, arithmetic and copies ran while one was open for 0% of the time, Pallas kernels for 46%

profile of v7, /device:TPU:0, one launch (start us, length us, event | category | flops | bytes accessed | tf_op | source)
XLA Modules:
  0.0 96.6 jit_solution(5552482589856038942)
XLA Ops:
  0.6 4.1 %collective-permute-start = (bf16[32,1536]{1,0:T(8,128)(2,1)}, bf16[32,1536]{1,0:T(8,128)(2,1)S(1)}, u32[]{:S(2)}, u32[]{:S(2)}) collective-permute-start(bf16[32,1536]{1,0:T(8,128)(2,1)} %refs_3_.3), channel_id=1, source_target_pairs={{0,2},{1,3},{2,0},{3,1},{4,6},{5,7},{6,4},{7,5},{8,10},{9,11},{10,... | collective-permute-start | bytes 294920 | tf_op jit(solution)/shard_map/ppermute | solution.py:29
  4.7 4.6 %shard_map.75 = (bf16[1536,768]{1,0:T(8,128)(2,1)S(1)}, bf16[1536,768]{1,0:T(8,128)(2,1)S(1)}, bf16[1536,768]{1,0:T(8,128)(2,1)S(1)}, bf16[1536,768]{1,0:T(8,128)(2,1)S(1)}, bf16[1536,768]{1,0:T(8,128)(2,1)S(1)}) custom-call(s32[1]{0:T(128)} %bitcast.refs_0_, bf16[1536,6144]{1,0:T(8,128)(2,1)} %refs_1_.9), custom_call_target="tpu_custom_call" | custom-call | tf_op jit(solution)/shard_map/pallas_call | solution.py:70
  11.1 3.0 %collective-permute-start.2 = (bf16[32,1536]{1,0:T(8,128)(2,1)S(1)}, bf16[32,1536]{1,0:T(8,128)(2,1)S(1)}, u32[]{:S(2)}, u32[]{:S(2)}) collective-permute-start(bf16[32,1536]{1,0:T(8,128)(2,1)S(1)} %shard_map.77.refs_2_), channel_id=1, source_target_pairs={{0,2},{1,3},{2,0},{3,1},{4,6},{5,7},{6,4},{7,5},{8,10},{9,11},{10,... | collective-permute-start | bytes 294920 | tf_op jit(solution)/shard_map/ppermute | solution.py:29
  14.1 3.1 %shard_map.78 = (bf16[1536,768]{1,0:T(8,128)(2,1)S(1)}, bf16[1536,768]{1,0:T(8,128)(2,1)S(1)}, bf16[1536,768]{1,0:T(8,128)(2,1)S(1)}) custom-call(s32[1]{0:T(128)} %bitcast.refs_0_, bf16[1536,6144]{1,0:T(8,128)(2,1)} %refs_1_.9, bf16[32,1536]{1,0:T(8,128)(2,1)S(1)} %shard_map.77.refs_2_), custom_call_target="tpu_custom_call" | custom-call | tf_op jit(solution)/shard_map/pallas_call | solution.py:70
  18.1 2.4 %shard_map.80 = (bf16[2,128,768]{2,1,0:T(8,128)(2,1)S(1)}, bf16[2,128,768]{2,1,0:T(8,128)(2,1)S(1)}, bf16[768,1536]{1,0:T(8,128)(2,1)S(1)}, bf16[768,1536]{1,0:T(8,128)(2,1)S(1)}) custom-call(s32[1]{0:T(128)} %bitcast.refs_0_, bf16[32,1536]{1,0:T(8,128)(2,1)S(1)} %copy-done.1, bf16[32,1536]{1,0:T(8,128)(2,1)S(1)} %collective-permute-done.refs_1_.refs_2_.refs_4_, ...), custom_call_target="tpu_custom_call" | custom-call | tf_op jit(solution)/shard_map/pallas_call | solution.py:70
  20.6 1.4 %shard_map.81 = (bf16[2,128,768]{2,1,0:T(8,128)(2,1)S(1)}, bf16[2,128,768]{2,1,0:T(8,128)(2,1)S(1)}) custom-call(s32[1]{0:T(128)} %bitcast.refs_0_, bf16[32,1536]{1,0:T(8,128)(2,1)S(1)} %copy-done.1, bf16[32,1536]{1,0:T(8,128)(2,1)S(1)} %collective-permute-done.refs_1_.refs_2_.refs_4_, bf16[64,1536]{1,0:T(8,128)(2,1)S(1)} %collective-permute-done.1.refs_3_.refs_5_, ...), custom_call_target="tpu_custom_call" | custom-call | tf_op jit(solution)/shard_map/pallas_call | solution.py:70
  22.7 1.4 %collective-permute-start.5 = (bf16[2,128,768]{2,1,0:T(8,128)(2,1)S(1)}, bf16[2,128,768]{2,1,0:T(8,128)(2,1)S(1)}, u32[]{:S(2)}, u32[]{:S(2)}) collective-permute-start(bf16[2,128,768]{2,1,0:T(8,128)(2,1)S(1)} %shard_map.82.refs_1_), channel_id=1, source_target_pairs={{0,8},{4,20},{8,0},{12,28},{16,24},{20,4},{24,16},{28,12},{1,9},{5... | collective-permute-start | bytes 1179656 | tf_op jit(solution)/shard_map/ppermute | solution.py:39
  24.1 3.3 %collective-permute-start.7 = (bf16[64,1536]{1,0:T(8,128)(2,1)S(1)}, bf16[64,1536]{1,0:T(8,128)(2,1)S(1)}, u32[]{:S(2)}, u32[]{:S(2)}) collective-permute-start(bf16[64,1536]{1,0:T(8,128)(2,1)S(1)} %shard_map.83.refs_2_), channel_id=1, source_target_pairs={{0,1},{1,0},{2,3},{3,2},{4,5},{5,4},{6,7},{7,6},{8,9},{9,8},{10,11... | collective-permute-start | bytes 589832 | tf_op jit(solution)/shard_map/ppermute | solution.py:29
  27.4 2.4 %shard_map.84 = (bf16[768,1536]{1,0:T(8,128)(2,1)S(1)}, bf16[768,1536]{1,0:T(8,128)(2,1)S(1)}) custom-call(s32[1]{0:T(128)} %bitcast.refs_0_, bf16[6144,1536]{1,0:T(8,128)(2,1)} %refs_6_.1, bf16[64,1536]{1,0:T(8,128)(2,1)S(1)} %shard_map.83.refs_2_), custom_call_target="tpu_custom_call" | custom-call | tf_op jit(solution)/shard_map/pallas_call | solution.py:70
  30.6 1.4 %collective-permute-start.6 = (bf16[1,128,768]{2,1,0:T(8,128)(2,1)S(1)}, bf16[1,128,768]{2,1,0:T(8,128)(2,1)S(1)}, u32[]{:S(2)}, u32[]{:S(2)}) collective-permute-start(bf16[1,128,768]{2,1,0:T(8,128)(2,1)S(1)} %shard_map.85.refs_9_), channel_id=1, source_target_pairs={{0,16},{4,12},{8,24},{12,4},{16,0},{20,28},{24,8},{28,20},{1,17},{... | collective-permute-start | bytes 589832 | tf_op jit(solution)/shard_map/ppermute | solution.py:39
  32.3 3.2 %shard_map.86 = (bf16[2,128,768]{2,1,0:T(8,128)(2,1)S(1)}, bf16[2,128,768]{2,1,0:T(8,128)(2,1)S(1)}, bf16[768,1536]{1,0:T(8,128)(2,1)S(1)}, bf16[768,1536]{1,0:T(8,128)(2,1)S(1)}) custom-call(s32[1]{0:T(128)} %bitcast.refs_0_, bf16[32,1536]{1,0:T(8,128)(2,1)S(1)} %copy-done, bf16[32,1536]{1,0:T(8,128)(2,1)S(1)} %collective-permute-done.2.refs_1_.refs_2_.refs_4_, ...), custom_call_target="tpu_custom_call" | custom-call | flops 6000000000 | tf_op jit(solution)/shard_map/pallas_call | solution.py:70
  38.9 2.4 %shard_map.89 = (bf16[1,128,768]{2,1,0:T(8,128)(2,1)S(1)}, bf16[1,128,768]{2,1,0:T(8,128)(2,1)S(1)}, bf16[768,1536]{1,0:T(8,128)(2,1)S(1)}, bf16[768,1536]{1,0:T(8,128)(2,1)S(1)}) custom-call(s32[1]{0:T(128)} %bitcast.refs_0_, bf16[32,1536]{1,0:T(8,128)(2,1)S(1)} %copy-done, bf16[32,1536]{1,0:T(8,128)(2,1)S(1)} %collective-permute-done.2.refs_1_.refs_2_.refs_4_, ...), custom_call_target="tpu_custom_call" | custom-call | tf_op jit(solution)/shard_map/pallas_call | solution.py:70
  42.3 1.8 %shard_map.91 = (bf16[1,128,768]{2,1,0:T(8,128)(2,1)S(1)}, bf16[1,128,768]{2,1,0:T(8,128)(2,1)S(1)}) custom-call(s32[1]{0:T(128)} %bitcast.refs_0_, bf16[32,1536]{1,0:T(8,128)(2,1)S(1)} %copy-done, bf16[32,1536]{1,0:T(8,128)(2,1)S(1)} %collective-permute-done.2.refs_1_.refs_2_.refs_4_, bf16[64,1536]{1,0:T(8,128)(2,1)S(1)} %collective-permute-done.7.refs_3_.refs_5_, ...), custom_call_target="tpu_custom_call" | custom-call | tf_op jit(solution)/shard_map/pallas_call | solution.py:70
  44.3 2.3 %collective-permute-done.12.refs_2_.refs_3_ = bf16[2,128,768]{2,1,0:T(8,128)(2,1)S(1)} collective-permute-done((bf16[2,128,768]{2,1,0:T(8,128)(2,1)S(1)}, bf16[2,128,768]{2,1,0:T(8,128)(2,1)S(1)}, u32[]{:S(2)}, u32[]{:S(2)}) %collective-permute-start.12) | collective-permute-done | bytes 393248 | tf_op jit(solution)/shard_map/ppermute | solution.py:39
  46.6 1.4 %collective-permute-start.14 = (bf16[1,128,768]{2,1,0:T(8,128)(2,1)S(1)}, bf16[1,128,768]{2,1,0:T(8,128)(2,1)S(1)}, u32[]{:S(2)}, u32[]{:S(2)}) collective-permute-start(bf16[1,128,768]{2,1,0:T(8,128)(2,1)S(1)} %shard_map.92.refs_5_), channel_id=1, source_target_pairs={{0,16},{4,12},{8,24},{12,4},{16,0},{20,28},{24,8},{28,20},{1,17},{... | collective-permute-start | bytes 589832 | tf_op jit(solution)/shard_map/ppermute | solution.py:39
  48.7 3.6 %collective-permute-done.14.refs_4_ = bf16[1,128,768]{2,1,0:T(8,128)(2,1)S(1)} collective-permute-done((bf16[1,128,768]{2,1,0:T(8,128)(2,1)S(1)}, bf16[1,128,768]{2,1,0:T(8,128)(2,1)S(1)}, u32[]{:S(2)}, u32[]{:S(2)}) %collective-permute-start.14) | collective-permute-done | bytes 196640 | tf_op jit(solution)/shard_map/ppermute | solution.py:39
  54.1 4.6 %collective-permute-done.10.refs_1_ = bf16[256,768]{1,0:T(8,128)(2,1)S(1)} collective-permute-done((bf16[256,768]{1,0:T(8,128)(2,1)S(1)}, bf16[256,768]{1,0:T(8,128)(2,1)S(1)}, u32[]{:S(2)}, u32[]{:S(2)}) %collective-permute-start.10) | collective-permute-done | bytes 393248 | tf_op jit(solution)/shard_map/ppermute | solution.py:39
  58.8 1.4 %collective-permute-start.18 = (bf16[256,768]{1,0:T(8,128)(2,1)S(1)}, bf16[256,768]{1,0:T(8,128)(2,1)S(1)}, u32[]{:S(2)}, u32[]{:S(2)}) collective-permute-start(bf16[256,768]{1,0:T(8,128)(2,1)S(1)} %shard_map.95.refs_14_.refs_0_), channel_id=1, source_target_pairs={{0,16},{4,12},{8,24},{12,4},{16,0},{20,28},{24,8},{28,20},{1,17},{... | collective-permute-start | bytes 1179656 | tf_op jit(solution)/shard_map/ppermute | solution.py:39
  61.1 9.8 %shard_map.96 = (bf16[64,1536]{1,0:T(8,128)(2,1)S(1)}, bf16[64,1536]{1,0:T(8,128)(2,1)S(1)}, bf16[6144,1536]{1,0:T(8,128)(2,1)}) custom-call(s32[1]{0:T(128)} %bitcast.refs_0_, bf16[512,768]{1,0:T(8,128)(2,1)S(1)} %shard_map.94.refs_2_.refs_1_, bf16[512,768]{1,0:T(8,128)(2,1)S(1)} %collective-permute-done.15.refs_2_, bf16[32,1536]{1,0:T(8,128)(2,1)S(1)} %copy-done, ...), custom_call_target="tpu_custom_call" | custom-call | flops 2415919104 | bytes 18874368 | tf_op jit(solution)/shard_map/pallas_call | solution.py:70
  71.2 3.1 %collective-permute-start.17 = (bf16[64,1536]{1,0:T(8,128)(2,1)S(1)}, bf16[64,1536]{1,0:T(8,128)(2,1)S(1)}, u32[]{:S(2)}, u32[]{:S(2)}) collective-permute-start(bf16[64,1536]{1,0:T(8,128)(2,1)S(1)} %get-tuple-element.72), channel_id=1, source_target_pairs={{0,1},{1,0},{2,3},{3,2},{4,5},{5,4},{6,7},{7,6},{8,9},{9,8},{10,11... | collective-permute-start | bytes 589832 | tf_op jit(solution)/shard_map/ppermute | solution.py:29
  74.3 3.1 %shard_map.98.refs_5_.refs_6_ = f32[128,1536]{1,0:T(8,128)S(1)} custom-call(bf16[512,768]{1,0:T(8,128)(2,1)S(1)} %shard_map.97.refs_0_.refs_5_.refs_1_, bf16[1536,768]{1,0:T(8,128)(2,1)S(1)} %get-tuple-element.46.refs_2_.refs_7_.refs_1_, bf16[1536,768]{1,0:T(8,128)(2,1)S(1)} %get-tuple-element.49.refs_6_.refs_2_, ...), custom_call_target="tpu_custom_call" | custom-call | flops 1207959552 | bytes 9437184 | tf_op jit(solution)/shard_map/pallas_call | solution.py:70
  77.4 3.1 %shard_map.99 = (bf16[32,1536]{1,0:T(8,128)(2,1)S(1)}, bf16[32,1536]{1,0:T(8,128)(2,1)S(1)}, bf16[32,1536]{1,0:T(8,128)(2,1)S(1)}, bf16[32,1536]{1,0:T(8,128)(2,1)S(1)}) custom-call(bf16[512,768]{1,0:T(8,128)(2,1)S(1)} %collective-permute-done.19.refs_0_.refs_2_, bf16[1536,768]{1,0:T(8,128)(2,1)S(1)} %get-tuple-element.44.refs_5_.refs_1_, ...), custom_call_target="tpu_custom_call" | custom-call | flops 1207959552 | bytes 9437184 | tf_op jit(solution)/shard_map/pallas_call | solution.py:70
  82.4 2.4 %collective-permute-start.22 = (bf16[32,1536]{1,0:T(8,128)(2,1)S(1)}, bf16[32,1536]{1,0:T(8,128)(2,1)S(1)}, u32[]{:S(2)}, u32[]{:S(2)}) collective-permute-start(bf16[32,1536]{1,0:T(8,128)(2,1)S(1)} %get-tuple-element.78), channel_id=1, source_target_pairs={{0,2},{1,3},{2,0},{3,1},{4,6},{5,7},{6,4},{7,5},{8,10},{9,11},{10,... | collective-permute-start | bytes 294920 | tf_op jit(solution)/shard_map/ppermute | solution.py:29
  85.9 8.8 %shard_map.101.refs_6_ = bf16[1536,6144]{1,0:T(8,128)(2,1)} custom-call(s32[1]{0:T(128)} %bitcast.refs_0_, bf16[512,768]{1,0:T(8,128)(2,1)S(1)} %shard_map.97.refs_0_.refs_5_.refs_1_, bf16[512,768]{1,0:T(8,128)(2,1)S(1)} %collective-permute-done.19.refs_0_.refs_2_, bf16[32,1536]{1,0:T(8,128)(2,1)S(1)} %copy-done.1, ...), custom_call_target="tpu_custom_call" | custom-call | flops 2415919104 | bytes 18874368 | tf_op jit(solution)/shard_map/pallas_call | solution.py:70
  (56 shorter events, 17.4 us)
Async XLA Ops:
  0.6 9.2 %collective-permute-start = (bf16[32,1536]{1,0:T(8,128)(2,1)}, bf16[32,1536]{1,0:T(8,128)(2,1)S(1)}, u32[]{:S(2)}, u32[]{:S(2)}) collective-permute-start(bf16[32,1536]{1,0:T(8,128)(2,1)} %refs_3_.3), channel_id=1, source_target_pairs={{0,2},{1,3},{2,0},{3,1},{4,6},{5,7},{6,4},{7,5},{8,10},{9,11},{10,... | collective-permute-start | bytes 294920 | tf_op jit(solution)/shard_map/ppermute | solution.py:29
  9.9 8.3 %collective-permute-start.1 = (bf16[64,1536]{1,0:T(8,128)(2,1)S(1)}, bf16[64,1536]{1,0:T(8,128)(2,1)S(1)}, u32[]{:S(2)}, u32[]{:S(2)}) collective-permute-start(bf16[64,1536]{1,0:T(8,128)(2,1)S(1)} %shard_map.76.refs_1_), channel_id=1, source_target_pairs={{0,1},{1,0},{2,3},{3,2},{4,5},{5,4},{6,7},{7,6},{8,9},{9,8},{10,11... | collective-permute-start | bytes 589832 | tf_op jit(solution)/shard_map/ppermute | solution.py:29
  11.1 6.2 %collective-permute-start.2 = (bf16[32,1536]{1,0:T(8,128)(2,1)S(1)}, bf16[32,1536]{1,0:T(8,128)(2,1)S(1)}, u32[]{:S(2)}, u32[]{:S(2)}) collective-permute-start(bf16[32,1536]{1,0:T(8,128)(2,1)S(1)} %shard_map.77.refs_2_), channel_id=1, source_target_pairs={{0,2},{1,3},{2,0},{3,1},{4,6},{5,7},{6,4},{7,5},{8,10},{9,11},{10,... | collective-permute-start | bytes 294920 | tf_op jit(solution)/shard_map/ppermute | solution.py:29
  20.5 2.0 %collective-permute-start.4 = (bf16[2,128,768]{2,1,0:T(8,128)(2,1)S(1)}, bf16[2,128,768]{2,1,0:T(8,128)(2,1)S(1)}, u32[]{:S(2)}, u32[]{:S(2)}) collective-permute-start(bf16[2,128,768]{2,1,0:T(8,128)(2,1)S(1)} %get-tuple-element.55), channel_id=1, source_target_pairs={{0,4},{4,0},{8,12},{12,8},{16,20},{20,16},{24,28},{28,24},{1,5},{5... | collective-permute-start | bytes 1179656 | tf_op jit(solution)/shard_map/ppermute | solution.py:29
  22.0 7.8 %collective-permute-start.3 = (bf16[2,128,768]{2,1,0:T(8,128)(2,1)S(1)}, bf16[2,128,768]{2,1,0:T(8,128)(2,1)S(1)}, u32[]{:S(2)}, u32[]{:S(2)}) collective-permute-start(bf16[2,128,768]{2,1,0:T(8,128)(2,1)S(1)} %get-tuple-element.53.refs_2_), channel_id=1, source_target_pairs={{0,4},{4,0},{8,12},{12,8},{16,20},{20,16},{24,28},{28,24},{1,5},{5... | collective-permute-start | bytes 1179656 | tf_op jit(solution)/shard_map/ppermute | solution.py:29
  22.7 7.8 %collective-permute-start.5 = (bf16[2,128,768]{2,1,0:T(8,128)(2,1)S(1)}, bf16[2,128,768]{2,1,0:T(8,128)(2,1)S(1)}, u32[]{:S(2)}, u32[]{:S(2)}) collective-permute-start(bf16[2,128,768]{2,1,0:T(8,128)(2,1)S(1)} %shard_map.82.refs_1_), channel_id=1, source_target_pairs={{0,8},{4,20},{8,0},{12,28},{16,24},{20,4},{24,16},{28,12},{1,9},{5... | collective-permute-start | bytes 1179656 | tf_op jit(solution)/shard_map/ppermute | solution.py:39
  24.1 8.2 %collective-permute-start.7 = (bf16[64,1536]{1,0:T(8,128)(2,1)S(1)}, bf16[64,1536]{1,0:T(8,128)(2,1)S(1)}, u32[]{:S(2)}, u32[]{:S(2)}) collective-permute-start(bf16[64,1536]{1,0:T(8,128)(2,1)S(1)} %shard_map.83.refs_2_), channel_id=1, source_target_pairs={{0,1},{1,0},{2,3},{3,2},{4,5},{5,4},{6,7},{7,6},{8,9},{9,8},{10,11... | collective-permute-start | bytes 589832 | tf_op jit(solution)/shard_map/ppermute | solution.py:29
  30.6 5.7 %collective-permute-start.6 = (bf16[1,128,768]{2,1,0:T(8,128)(2,1)S(1)}, bf16[1,128,768]{2,1,0:T(8,128)(2,1)S(1)}, u32[]{:S(2)}, u32[]{:S(2)}) collective-permute-start(bf16[1,128,768]{2,1,0:T(8,128)(2,1)S(1)} %shard_map.85.refs_9_), channel_id=1, source_target_pairs={{0,16},{4,12},{8,24},{12,4},{16,0},{20,28},{24,8},{28,20},{1,17},{... | collective-permute-start | bytes 589832 | tf_op jit(solution)/shard_map/ppermute | solution.py:39
  35.5 2.4 %collective-permute-start.9 = (bf16[2,128,768]{2,1,0:T(8,128)(2,1)S(1)}, bf16[2,128,768]{2,1,0:T(8,128)(2,1)S(1)}, u32[]{:S(2)}, u32[]{:S(2)}) collective-permute-start(bf16[2,128,768]{2,1,0:T(8,128)(2,1)S(1)} %get-tuple-element.63), channel_id=1, source_target_pairs={{0,4},{4,0},{8,12},{12,8},{16,20},{20,16},{24,28},{28,24},{1,5},{5... | collective-permute-start | bytes 1179656 | tf_op jit(solution)/shard_map/ppermute | solution.py:29
  36.6 5.7 %collective-permute-start.8 = (bf16[128,768]{1,0:T(8,128)(2,1)S(1)}, bf16[128,768]{1,0:T(8,128)(2,1)S(1)}, u32[]{:S(2)}, u32[]{:S(2)}) collective-permute-start(bf16[128,768]{1,0:T(8,128)(2,1)S(1)} %get-tuple-element.60.refs_2_.refs_0_), channel_id=1, source_target_pairs={{0,8},{4,20},{8,0},{12,28},{16,24},{20,4},{24,16},{28,12},{1,9},{5... | collective-permute-start | bytes 589832 | tf_op jit(solution)/shard_map/ppermute | solution.py:39
  38.1 8.5 %collective-permute-start.12 = (bf16[2,128,768]{2,1,0:T(8,128)(2,1)S(1)}, bf16[2,128,768]{2,1,0:T(8,128)(2,1)S(1)}, u32[]{:S(2)}, u32[]{:S(2)}) collective-permute-start(bf16[2,128,768]{2,1,0:T(8,128)(2,1)S(1)} %shard_map.88.refs_7_), channel_id=1, source_target_pairs={{0,8},{4,20},{8,0},{12,28},{16,24},{20,4},{24,16},{28,12},{1,9},{5... | collective-permute-start | bytes 1179656 | tf_op jit(solution)/shard_map/ppermute | solution.py:39
  41.3 3.0 %collective-permute-start.13 = (bf16[1,128,768]{2,1,0:T(8,128)(2,1)S(1)}, bf16[1,128,768]{2,1,0:T(8,128)(2,1)S(1)}, u32[]{:S(2)}, u32[]{:S(2)}) collective-permute-start(bf16[1,128,768]{2,1,0:T(8,128)(2,1)S(1)} %get-tuple-element.70), channel_id=1, source_target_pairs={{0,4},{4,0},{8,12},{12,8},{16,20},{20,16},{24,28},{28,24},{1,5},{5... | collective-permute-start | bytes 589832 | tf_op jit(solution)/shard_map/ppermute | solution.py:29
  44.2 4.5 %collective-permute-start.11 = (bf16[1,128,768]{2,1,0:T(8,128)(2,1)S(1)}, bf16[1,128,768]{2,1,0:T(8,128)(2,1)S(1)}, u32[]{:S(2)}, u32[]{:S(2)}) collective-permute-start(bf16[1,128,768]{2,1,0:T(8,128)(2,1)S(1)} %get-tuple-element.68.refs_3_), channel_id=1, source_target_pairs={{0,4},{4,0},{8,12},{12,8},{16,20},{20,16},{24,28},{28,24},{1,5},{5... | collective-permute-start | bytes 589832 | tf_op jit(solution)/shard_map/ppermute | solution.py:29
  46.6 5.7 %collective-permute-start.14 = (bf16[1,128,768]{2,1,0:T(8,128)(2,1)S(1)}, bf16[1,128,768]{2,1,0:T(8,128)(2,1)S(1)}, u32[]{:S(2)}, u32[]{:S(2)}) collective-permute-start(bf16[1,128,768]{2,1,0:T(8,128)(2,1)S(1)} %shard_map.92.refs_5_), channel_id=1, source_target_pairs={{0,16},{4,12},{8,24},{12,4},{16,0},{20,28},{24,8},{28,20},{1,17},{... | collective-permute-start | bytes 589832 | tf_op jit(solution)/shard_map/ppermute | solution.py:39
  48.0 10.6 %collective-permute-start.10 = (bf16[256,768]{1,0:T(8,128)(2,1)S(1)}, bf16[256,768]{1,0:T(8,128)(2,1)S(1)}, u32[]{:S(2)}, u32[]{:S(2)}) collective-permute-start(bf16[256,768]{1,0:T(8,128)(2,1)S(1)} %shard_map.90.refs_6_.refs_0_), channel_id=1, source_target_pairs={{0,16},{4,12},{8,24},{12,4},{16,0},{20,28},{24,8},{28,20},{1,17},{... | collective-permute-start | bytes 1179656 | tf_op jit(solution)/shard_map/ppermute | solution.py:39
  52.7 6.1 %collective-permute-start.16 = (bf16[128,768]{1,0:T(8,128)(2,1)S(1)}, bf16[128,768]{1,0:T(8,128)(2,1)S(1)}, u32[]{:S(2)}, u32[]{:S(2)}) collective-permute-start(bf16[128,768]{1,0:T(8,128)(2,1)S(1)} %shard_map.93.refs_2_.refs_0_), channel_id=1, source_target_pairs={{0,8},{4,20},{8,0},{12,28},{16,24},{20,4},{24,16},{28,12},{1,9},{5... | collective-permute-start | bytes 589832 | tf_op jit(solution)/shard_map/ppermute | solution.py:39
  58.7 2.4 %collective-permute-start.15 = (bf16[512,768]{1,0:T(8,128)(2,1)S(1)}, bf16[512,768]{1,0:T(8,128)(2,1)S(1)}, u32[]{:S(2)}, u32[]{:S(2)}) collective-permute-start(bf16[512,768]{1,0:T(8,128)(2,1)S(1)} %shard_map.94.refs_2_.refs_1_), channel_id=1, source_target_pairs={{0,4},{4,0},{8,12},{12,8},{16,20},{20,16},{24,28},{28,24},{1,5},{5... | collective-permute-start | bytes 2359304 | tf_op jit(solution)/shard_map/ppermute | solution.py:29
  58.8 12.1 %collective-permute-start.18 = (bf16[256,768]{1,0:T(8,128)(2,1)S(1)}, bf16[256,768]{1,0:T(8,128)(2,1)S(1)}, u32[]{:S(2)}, u32[]{:S(2)}) collective-permute-start(bf16[256,768]{1,0:T(8,128)(2,1)S(1)} %shard_map.95.refs_14_.refs_0_), channel_id=1, source_target_pairs={{0,16},{4,12},{8,24},{12,4},{16,0},{20,28},{24,8},{28,20},{1,17},{... | collective-permute-start | bytes 1179656 | tf_op jit(solution)/shard_map/ppermute | solution.py:39
  71.0 6.4 %collective-permute-start.19 = (bf16[512,768]{1,0:T(8,128)(2,1)S(1)}, bf16[512,768]{1,0:T(8,128)(2,1)S(1)}, u32[]{:S(2)}, u32[]{:S(2)}) collective-permute-start(bf16[512,768]{1,0:T(8,128)(2,1)S(1)} %shard_map.97.refs_0_.refs_5_.refs_1_), channel_id=1, source_target_pairs={{0,4},{4,0},{8,12},{12,8},{16,20},{20,16},{24,28},{28,24},{1,5},{5... | collective-permute-start | bytes 2359304 | tf_op jit(solution)/shard_map/ppermute | solution.py:29
  71.2 10.6 %collective-permute-start.17 = (bf16[64,1536]{1,0:T(8,128)(2,1)S(1)}, bf16[64,1536]{1,0:T(8,128)(2,1)S(1)}, u32[]{:S(2)}, u32[]{:S(2)}) collective-permute-start(bf16[64,1536]{1,0:T(8,128)(2,1)S(1)} %get-tuple-element.72), channel_id=1, source_target_pairs={{0,1},{1,0},{2,3},{3,2},{4,5},{5,4},{6,7},{7,6},{8,9},{9,8},{10,11... | collective-permute-start | bytes 589832 | tf_op jit(solution)/shard_map/ppermute | solution.py:29
  80.5 14.2 %collective-permute-start.21 = (bf16[32,1536]{1,0:T(8,128)(2,1)S(1)}, bf16[32,1536]{1,0:T(8,128)(2,1)S(1)}, u32[]{:S(2)}, u32[]{:S(2)}) collective-permute-start(bf16[32,1536]{1,0:T(8,128)(2,1)S(1)} %get-tuple-element.74.refs_2_), channel_id=1, source_target_pairs={{0,3},{1,2},{2,1},{3,0},{4,7},{5,6},{6,5},{7,4},{8,11},{9,10},{10,... | collective-permute-start | bytes 294920 | tf_op jit(solution)/shard_map/ppermute | solution.py:29
  81.8 12.9 %collective-permute-start.20 = (bf16[32,1536]{1,0:T(8,128)(2,1)S(1)}, bf16[32,1536]{1,0:T(8,128)(2,1)S(1)}, u32[]{:S(2)}, u32[]{:S(2)}) collective-permute-start(bf16[32,1536]{1,0:T(8,128)(2,1)S(1)} %get-tuple-element.76.refs_6_), channel_id=1, source_target_pairs={{0,2},{1,3},{2,0},{3,1},{4,6},{5,7},{6,4},{7,5},{8,10},{9,11},{10,... | collective-permute-start | bytes 294920 | tf_op jit(solution)/shard_map/ppermute | solution.py:29
  82.4 13.4 %collective-permute-start.22 = (bf16[32,1536]{1,0:T(8,128)(2,1)S(1)}, bf16[32,1536]{1,0:T(8,128)(2,1)S(1)}, u32[]{:S(2)}, u32[]{:S(2)}) collective-permute-start(bf16[32,1536]{1,0:T(8,128)(2,1)S(1)} %get-tuple-element.78), channel_id=1, source_target_pairs={{0,2},{1,3},{2,0},{3,1},{4,6},{5,7},{6,4},{7,5},{8,10},{9,11},{10,... | collective-permute-start | bytes 294920 | tf_op jit(solution)/shard_map/ppermute | solution.py:29
  84.8 11.1 %collective-permute-start.23 = (bf16[32,1536]{1,0:T(8,128)(2,1)S(1)}, bf16[32,1536]{1,0:T(8,128)(2,1)S(1)}, u32[]{:S(2)}, u32[]{:S(2)}) collective-permute-start(bf16[32,1536]{1,0:T(8,128)(2,1)S(1)} %get-tuple-element.79), channel_id=1, source_target_pairs={{0,1},{1,0},{2,3},{3,2},{4,5},{5,4},{6,7},{7,6},{8,9},{9,8},{10,11... | collective-permute-start | bytes 294920 | tf_op jit(solution)/shard_map/ppermute | solution.py:29
  (2 other events, 6.8 us)
